TPU v7x, 32 devices: a whole 2x2x4 slice. The times are simulated.
32 devices in a mesh: dp: 4 (over x, core), seq: 4 (over z), mp: 2 (over y).
Axes of the slice: x: 2, y: 2, z: 4, core: 2. Of those that a mesh axis runs over, the one named last changes fastest.
Arguments:
- tokens_in: bfloat16 [2, 4, 704, 2048], P(None, 'dp', 'seq'), may hold values from -6 to 6
- cotangent: bfloat16 [2, 4, 704, 2048], P(None, 'dp', 'seq'), may hold values from -6 to 6
- seq_source: int32 [2, 4], P(None, 'dp'), may hold values from 0 to 7
- source_weight: float32 [8], replicated, may hold values from 0.5 to 2
- input_weight: bfloat16 [2048, 2560], P(('dp', 'seq'), 'mp'), may hold values from -0.125 to 0.125
- gelu_weight: bfloat16 [2048, 2560], P(('dp', 'seq'), 'mp'), may hold values from -0.125 to 0.125
- decay_gates: bfloat16 [16, 25600], P('mp', ('dp', 'seq')), may hold values from -0.5 to 0.5
- input_gates: bfloat16 [16, 25600], P('mp', ('dp', 'seq')), may hold values from -0.5 to 0.5
- channel_params: bfloat16 [8, 2, 1280], P(None, 'mp', ('dp', 'seq')), may hold values from -3 to 14, as said below
- norm_gains: bfloat16 [2, 2048], P(None, ('dp', 'seq')), may hold values from 0.099609375 to 1.8984375
- output_weight: bfloat16 [2560, 2048], P('mp', ('dp', 'seq')), may hold values from -0.5 to 0.5
- mlp_gate: bfloat16 [2048, 6144], P(('dp', 'seq'), 'mp'), may hold values from -0.125 to 0.125
- mlp_up: bfloat16 [2048, 6144], P(('dp', 'seq'), 'mp'), may hold values from -0.125 to 0.125
- mlp_down: bfloat16 [6144, 2048], P('mp', ('dp', 'seq')), may hold values from -0.15625 to 0.15625
Outputs:
- block_out: bfloat16 [2, 4, 704, 2048], P(None, 'dp', 'seq')
- grad_tokens: float32 [2, 4, 704, 2048], P(None, 'dp', 'seq')
- grad_input_weight: float32 [2048, 2560], P(('dp', 'seq'), 'mp')
- grad_gelu_weight: float32 [2048, 2560], P(('dp', 'seq'), 'mp')
- grad_decay_gates: float32 [16, 25600], P('mp', ('dp', 'seq'))
- grad_input_gates: float32 [16, 25600], P('mp', ('dp', 'seq'))
- grad_channel_params: float32 [8, 2, 1280], P(None, 'mp', ('dp', 'seq'))
- grad_norm_gains: float32 [2, 2048], P(None, ('dp', 'seq'))
- grad_output_weight: float32 [2560, 2048], P('mp', ('dp', 'seq'))
- grad_mlp_gate: float32 [2048, 6144], P(('dp', 'seq'), 'mp')
- grad_mlp_up: float32 [2048, 6144], P(('dp', 'seq'), 'mp')
- grad_mlp_down: float32 [6144, 2048], P('mp', ('dp', 'seq'))
Inputs may be any that keep to these rules, and one draw needn't show every extreme that they name: `channel_params`: row 0 (the decay parameters) lies between 4 and 14 and differs per channel; rows 1 to 7 are of order one.
All inputs are finite; a program needn't handle non-finite values.
Results may differ from a plain program's by a relative error of at most 0.011.
Values may be sent and summed in bfloat16 or wider, within the bound.
A program may use at most 1.9375 GiB of HBM per device.

v0:
```python
import jax
import jax.numpy as jnp
from jax import lax
from jax.sharding import PartitionSpec as P

WIDTH = 2560
HEADS = 16


EPSILON = 1e-06
DECAY_SCALE = 8.0


def from_behind(shard, axis, by):
    count = lax.axis_size(axis)
    pairs = [(i, i + by) for i in range(count) if 0 <= i + by < count]
    return lax.ppermute(shard, axis, pairs)


def carried_in(shard, axis, combine, identity, reverse):
    count, here = (lax.axis_size(axis), lax.axis_index(axis))
    everything = lax.all_gather(shard, axis)
    start = jnp.broadcast_to(jnp.asarray(identity, shard.dtype), shard.shape)

    def lap(k, before):
        at = count - 1 - k if reverse else k
        reached = at > here if reverse else at < here
        new = combine(before, everything[at])
        return jnp.where(reached, new, before)

    return lax.fori_loop(0, count, lap, start)


def normalize(values, gain_vec):
    return (
        values * lax.rsqrt(jnp.mean(values * values, axis=-1, keepdims=True) + EPSILON) * gain_vec
    )


def smooth_gate(values):
    return jax.nn.gelu(values, approximate=True)


def coefficients(inputs, logit_a, logit_i, lambda_param):
    log_decay = -DECAY_SCALE * jax.nn.sigmoid(logit_a) * jax.nn.softplus(-lambda_param)
    decay_rate = jnp.exp(log_decay)
    drive_term = jnp.sqrt(-jnp.expm1(2.0 * log_decay)) * jax.nn.sigmoid(logit_i) * inputs
    return (decay_rate, drive_term)


def combine(earlier, later_pair):
    return (earlier[0] * later_pair[0], later_pair[1] + later_pair[0] * earlier[1])


def combine_stacked(earlier, later_pair):
    return jnp.stack(
        [earlier[0] * later_pair[0], later_pair[1] + later_pair[0] * earlier[1]], axis=0
    )


def gated_product(gate_in, up_in):
    return smooth_gate(gate_in) * up_in


def owner_terms(records, smalls, group, count):
    joined_sum = None
    for record, small in zip(records, smalls):
        (
            normed,
            x_grad,
            y_grad,
            mixed,
            proj_grad,
            normed_two,
            gate_grad,
            up_grad,
            hidden,
            down_grad,
        ) = record
        shard_d = normed.shape[1] // group

        def rows_of(left, right):
            term = jnp.einsum("td,tw->dw", left, right, preferred_element_type=jnp.float32)
            return term.reshape(count, -1)

        def cols_of(left, right):
            term = jnp.einsum("tw,td->wd", left, right, preferred_element_type=jnp.float32)
            return jnp.transpose(term.reshape(term.shape[0], count, shard_d), (1, 0, 2)).reshape(
                count, -1
            )

        def small_of(full, dim_one):
            shape_one = full.shape
            split_shape = (
                shape_one[:dim_one]
                + (group, shape_one[dim_one] // group)
                + shape_one[dim_one + 1 :]
            )
            owners = jnp.moveaxis(full.reshape(split_shape), dim_one, 0).reshape(group, -1)
            return owners

        terms = [
            rows_of(normed, x_grad),
            rows_of(normed, y_grad),
            small_of(small[0], 1),
            small_of(small[1], 1),
            small_of(small[2], 2),
            small_of(small[3], 1),
            cols_of(mixed, proj_grad),
            rows_of(normed_two, gate_grad),
            rows_of(normed_two, up_grad),
            cols_of(hidden, down_grad),
        ]
        joined = jnp.concatenate(terms, axis=1)
        joined_sum = joined
    return joined_sum


def unpack_share(flat_share, templates):
    results = []
    position = 0
    for template in templates:
        count = 1
        for extent in template.shape:
            count = count * extent
        results.append(flat_share[0, position : position + count].reshape(template.shape))
        position = position + count
    return tuple(results)


def gather_first(input_weight, gelu_weight, decay_gates, input_gates, channel_params, norm_gains):
    return (
        lax.all_gather(input_weight, ("dp", "seq"), axis=0, tiled=True),
        lax.all_gather(gelu_weight, ("dp", "seq"), axis=0, tiled=True),
        lax.all_gather(decay_gates, ("dp", "seq"), axis=1, tiled=True),
        lax.all_gather(input_gates, ("dp", "seq"), axis=1, tiled=True),
        lax.all_gather(channel_params, ("dp", "seq"), axis=2, tiled=True),
        lax.all_gather(norm_gains, ("dp", "seq"), axis=1, tiled=True),
    )


def gather_second(output_weight, mlp_gate, mlp_up, mlp_down):
    return (
        lax.all_gather(output_weight, ("dp", "seq"), axis=1, tiled=True),
        lax.all_gather(mlp_gate, ("dp", "seq"), axis=0, tiled=True),
        lax.all_gather(mlp_up, ("dp", "seq"), axis=0, tiled=True),
        lax.all_gather(mlp_down, ("dp", "seq"), axis=1, tiled=True),
    )


def gather_first_again(
    input_weight, gelu_weight, decay_gates, input_gates, channel_params, norm_gains
):
    return (
        lax.all_gather(input_weight, ("dp", "seq"), axis=0, tiled=True),
        lax.all_gather(gelu_weight, ("dp", "seq"), axis=0, tiled=True),
        lax.all_gather(decay_gates, ("dp", "seq"), axis=1, tiled=True),
        lax.all_gather(input_gates, ("dp", "seq"), axis=1, tiled=True),
        lax.all_gather(channel_params, ("dp", "seq"), axis=2, tiled=True),
        lax.all_gather(norm_gains, ("dp", "seq"), axis=1, tiled=True),
    )


def gather_second_again(output_weight, mlp_gate, mlp_up, mlp_down):
    return (
        lax.all_gather(output_weight, ("dp", "seq"), axis=1, tiled=True),
        lax.all_gather(mlp_gate, ("dp", "seq"), axis=0, tiled=True),
        lax.all_gather(mlp_up, ("dp", "seq"), axis=0, tiled=True),
        lax.all_gather(mlp_down, ("dp", "seq"), axis=1, tiled=True),
    )


def unpack_first(fetched):
    wide_x, wide_y, full_decay, full_input, full_channels, full_gains = fetched
    heads_local = full_decay.shape[0]
    block_size = WIDTH // HEADS
    return (
        wide_x,
        wide_y,
        full_decay.reshape(heads_local, block_size, block_size),
        full_input.reshape(heads_local, block_size, block_size),
        full_channels.reshape(8, -1).astype(jnp.float32),
        full_gains.astype(jnp.float32),
    )


def forward_pass(tokens, first_set, second_set):
    wide_x, wide_y, decay_blocks, input_blocks, recurrence, gains = first_set
    proj_out, proj_gate, proj_up, proj_down = second_set
    rows_here = tokens.shape[0]
    heads_local, block_size = (decay_blocks.shape[0], decay_blocks.shape[1])
    residual = tokens.astype(jnp.float32)
    normed = normalize(residual, gains[0]).astype(jnp.bfloat16)
    branch_x = jnp.dot(normed, wide_x, preferred_element_type=jnp.float32).astype(jnp.bfloat16)
    branch_y = jnp.dot(normed, wide_y, preferred_element_type=jnp.float32)
    rim_rows = from_behind(branch_x[rows_here - 3 :], "seq", 1)
    padded = jnp.concatenate([rim_rows, branch_x], axis=0).astype(jnp.float32)
    conv_sum = recurrence[3]
    for offset in range(4):
        conv_sum = conv_sum + recurrence[4 + offset] * padded[3 - offset : 3 - offset + rows_here]
    inputs = conv_sum.astype(jnp.bfloat16)
    split_in = inputs.reshape(rows_here, heads_local, block_size)
    logit_a = (
        jnp.einsum(
            "thi,hij->thj", split_in, decay_blocks, preferred_element_type=jnp.float32
        ).reshape(rows_here, -1)
        + recurrence[1]
    )
    logit_i = (
        jnp.einsum(
            "thi,hij->thj", split_in, input_blocks, preferred_element_type=jnp.float32
        ).reshape(rows_here, -1)
        + recurrence[2]
    )
    decay_rate, drive_term = coefficients(
        inputs.astype(jnp.float32), logit_a, logit_i, recurrence[0]
    )
    running, local_state = lax.associative_scan(combine, (decay_rate, drive_term), axis=0)
    identity_pair = jnp.stack([jnp.ones_like(decay_rate[0]), jnp.zeros_like(decay_rate[0])], axis=0)
    end_pair = jnp.stack([running[rows_here - 1], local_state[rows_here - 1]], axis=0)
    incoming = carried_in(end_pair, "seq", combine_stacked, identity_pair, False)[1]
    states = local_state + running * incoming
    gelu_y = smooth_gate(branch_y)
    mixed = (gelu_y * states).astype(jnp.bfloat16)
    projected = lax.psum(jnp.dot(mixed, proj_out, preferred_element_type=jnp.float32), "mp")
    middle = residual + projected
    normed_two = normalize(middle, gains[1]).astype(jnp.bfloat16)
    gate_pre = jnp.dot(normed_two, proj_gate, preferred_element_type=jnp.float32)
    up_pre = jnp.dot(normed_two, proj_up, preferred_element_type=jnp.float32)
    hidden = gated_product(gate_pre, up_pre).astype(jnp.bfloat16)
    result = middle + lax.psum(jnp.dot(hidden, proj_down, preferred_element_type=jnp.float32), "mp")
    saved_state = (
        residual,
        normed,
        branch_y,
        padded,
        inputs,
        logit_a,
        logit_i,
        decay_rate,
        running,
        incoming,
        states,
        gelu_y,
        mixed,
        middle,
        normed_two,
        gate_pre,
        up_pre,
        hidden,
    )
    return (result, saved_state)


def backward_pass(upstream, saved_state, first_set, second_set):
    wide_x, wide_y, decay_blocks, input_blocks, recurrence, gains = first_set
    proj_out, proj_gate, proj_up, proj_down = second_set
    (
        residual,
        normed,
        branch_y,
        padded,
        inputs,
        logit_a,
        logit_i,
        decay_rate,
        running,
        incoming,
        states,
        gelu_y,
        mixed,
        middle,
        normed_two,
        gate_pre,
        up_pre,
        hidden,
    ) = saved_state
    rows_here = residual.shape[0]
    heads_local, block_size = (decay_blocks.shape[0], decay_blocks.shape[1])
    down_grad = upstream.astype(jnp.bfloat16)
    hidden_grad = jnp.einsum("td,fd->tf", down_grad, proj_down, preferred_element_type=jnp.float32)
    gate_grad, up_grad = jax.vjp(gated_product, gate_pre, up_pre)[1](hidden_grad)
    gate_grad = gate_grad.astype(jnp.bfloat16)
    up_grad = up_grad.astype(jnp.bfloat16)
    normed_two_part = jnp.einsum(
        "tf,df->td", gate_grad, proj_gate, preferred_element_type=jnp.float32
    ) + jnp.einsum("tf,df->td", up_grad, proj_up, preferred_element_type=jnp.float32)
    normed_two_grad = lax.psum(normed_two_part, "mp")
    middle_part, gain_two = jax.vjp(normalize, middle, gains[1])[1](normed_two_grad)
    middle_grad = upstream + middle_part
    proj_grad = middle_grad.astype(jnp.bfloat16)
    mixed_grad = jnp.einsum("td,wd->tw", proj_grad, proj_out, preferred_element_type=jnp.float32)
    state_grad = mixed_grad * gelu_y
    branch_y_grad = jax.vjp(smooth_gate, branch_y)[1](mixed_grad * states)[0].astype(jnp.bfloat16)
    next_decay = jnp.concatenate([decay_rate[1:], jnp.ones_like(decay_rate[:1])], axis=0)
    after_product, local_adjoint = lax.associative_scan(
        combine, (next_decay, state_grad), axis=0, reverse=True
    )
    identity_pair = jnp.stack([jnp.ones_like(decay_rate[0]), jnp.zeros_like(decay_rate[0])], axis=0)
    start_pair = jnp.stack([running[rows_here - 1], decay_rate[0] * local_adjoint[0]], axis=0)
    later_adjoint = carried_in(start_pair, "seq", combine_stacked, identity_pair, True)[1]
    adjoint = local_adjoint + after_product * later_adjoint
    previous = jnp.concatenate([incoming[None], states[: rows_here - 1]], axis=0)
    coef_pull = jax.vjp(coefficients, inputs.astype(jnp.float32), logit_a, logit_i, recurrence[0])[
        1
    ]
    input_direct, grad_la, grad_li, grad_lambda = coef_pull((adjoint * previous, adjoint))
    grad_la = grad_la.astype(jnp.bfloat16).reshape(rows_here, heads_local, block_size)
    grad_li = grad_li.astype(jnp.bfloat16).reshape(rows_here, heads_local, block_size)
    split_in = inputs.reshape(rows_here, heads_local, block_size)
    grad_decay_blocks = jnp.einsum(
        "thi,thj->hij", split_in, grad_la, preferred_element_type=jnp.float32
    )
    grad_input_blocks = jnp.einsum(
        "thi,thj->hij", split_in, grad_li, preferred_element_type=jnp.float32
    )
    input_grad = (
        input_direct
        + jnp.einsum(
            "thj,hij->thi", grad_la, decay_blocks, preferred_element_type=jnp.float32
        ).reshape(rows_here, -1)
        + jnp.einsum(
            "thj,hij->thi", grad_li, input_blocks, preferred_element_type=jnp.float32
        ).reshape(rows_here, -1)
    )
    channels_local = input_grad.shape[1]
    zero_rows = jnp.zeros((3, channels_local), jnp.float32)
    spread = jnp.concatenate([zero_rows, input_grad, zero_rows], axis=0)
    padded_grad = jnp.zeros((rows_here + 3, channels_local), jnp.float32)
    tap_grads = []
    for offset in range(4):
        padded_grad = padded_grad + recurrence[4 + offset] * spread[offset : offset + rows_here + 3]
        tap_grads.append(jnp.sum(input_grad * padded[3 - offset : 3 - offset + rows_here], axis=0))
    returned = from_behind(padded_grad[:3], "seq", -1)
    branch_x_grad = padded_grad[3:] + jnp.concatenate(
        [jnp.zeros((rows_here - 3, channels_local), jnp.float32), returned], axis=0
    )
    branch_x_grad = branch_x_grad.astype(jnp.bfloat16)
    normed_part = jnp.einsum(
        "tw,dw->td", branch_x_grad, wide_x, preferred_element_type=jnp.float32
    ) + jnp.einsum("tw,dw->td", branch_y_grad, wide_y, preferred_element_type=jnp.float32)
    normed_grad = lax.psum(normed_part.astype(jnp.bfloat16), "mp").astype(jnp.float32)
    residual_part, gain_one = jax.vjp(normalize, residual, gains[0])[1](normed_grad)
    token_grad = middle_grad + residual_part
    channel_grad = jnp.stack(
        [
            grad_lambda,
            jnp.sum(grad_la.astype(jnp.float32), axis=0).reshape(-1),
            jnp.sum(grad_li.astype(jnp.float32), axis=0).reshape(-1),
            jnp.sum(input_grad, axis=0),
        ]
        + tap_grads,
        axis=0,
    )
    small_grads = (
        grad_decay_blocks.reshape(heads_local, -1),
        grad_input_blocks.reshape(heads_local, -1),
        channel_grad.reshape(8, 1, -1),
        jnp.stack([gain_one, gain_two], axis=0),
    )
    record = (
        normed,
        branch_x_grad,
        branch_y_grad,
        mixed,
        proj_grad,
        normed_two,
        gate_grad,
        up_grad,
        hidden,
        down_grad,
    )
    return (token_grad, small_grads, record)


def on_device(
    tokens_in,
    cotangent,
    seq_source,
    source_weight,
    input_weight,
    gelu_weight,
    decay_gates,
    input_gates,
    channel_params,
    norm_gains,
    output_weight,
    mlp_gate,
    mlp_up,
    mlp_down,
):
    batches = tokens_in.shape[0]
    group = lax.axis_size(("dp", "seq"))
    source_ids = jnp.arange(source_weight.shape[0], dtype=jnp.int32)
    templates = (
        input_weight,
        gelu_weight,
        decay_gates,
        input_gates,
        channel_params,
        norm_gains,
        output_weight,
        mlp_gate,
        mlp_up,
        mlp_down,
    )
    outputs = []
    token_grads = []
    totals = None
    for micro_batch in range(batches):
        first_set = unpack_first(
            gather_first(
                input_weight, gelu_weight, decay_gates, input_gates, channel_params, norm_gains
            )
        )
        second_set = gather_second(output_weight, mlp_gate, mlp_up, mlp_down)
        result, saved_state = forward_pass(tokens_in[micro_batch, 0], first_set, second_set)
        outputs.append(result.astype(jnp.bfloat16))
        source_match = seq_source[micro_batch, 0] == source_ids
        loss_weight = jnp.sum(jnp.where(source_match, source_weight, 0.0))
        upstream = cotangent[micro_batch, 0].astype(jnp.float32) * loss_weight
        first_set = unpack_first(
            gather_first_again(
                input_weight, gelu_weight, decay_gates, input_gates, channel_params, norm_gains
            )
        )
        second_set = gather_second_again(output_weight, mlp_gate, mlp_up, mlp_down)
        token_grad, small_grads, record = backward_pass(
            upstream, saved_state, first_set, second_set
        )
        token_grads.append(token_grad)
        flat_share = lax.psum_scatter(
            owner_terms([record], [small_grads], group, lax.axis_size(("dp", "seq")) * 1),
            ("dp", "seq"),
            scatter_dimension=0,
            tiled=True,
        )
        shares = unpack_share(flat_share, templates)
        totals = (
            shares
            if totals is None
            else tuple((left + right for left, right in zip(totals, shares)))
        )
    block_out = jnp.stack(outputs, axis=0)[:, None]
    grad_tokens = jnp.stack(token_grads, axis=0)[:, None]
    return (block_out, grad_tokens) + tuple(totals)


def solution(mesh):
    placed = (
        P(None, "dp", "seq", None),
        P(None, "dp", "seq", None),
        P(None, "dp"),
        P(),
        P(("dp", "seq"), "mp"),
        P(("dp", "seq"), "mp"),
        P("mp", ("dp", "seq")),
        P("mp", ("dp", "seq")),
        P(None, "mp", ("dp", "seq")),
        P(None, ("dp", "seq")),
        P("mp", ("dp", "seq")),
        P(("dp", "seq"), "mp"),
        P(("dp", "seq"), "mp"),
        P("mp", ("dp", "seq")),
    )
    return jax.shard_map(
        on_device,
        mesh=mesh,
        in_specs=placed,
        out_specs=(
            P(None, "dp", "seq", None),
            P(None, "dp", "seq", None),
            P(("dp", "seq"), "mp"),
            P(("dp", "seq"), "mp"),
            P("mp", ("dp", "seq")),
            P("mp", ("dp", "seq")),
            P(None, "mp", ("dp", "seq")),
            P(None, ("dp", "seq")),
            P("mp", ("dp", "seq")),
            P(("dp", "seq"), "mp"),
            P(("dp", "seq"), "mp"),
            P("mp", ("dp", "seq")),
        ),
        check_vma=False,
    )
```

profile of v0, /device:TPU:1, one launch (start us, length us, event | category | flops | bytes accessed | tf_op | source)
XLA Modules:
  0.0 5410.9 jit_solution(70877296992955554)
XLA Ops:
  10.2 30.4 all_gather.36
  42.6 42.6 all_gather.38
  85.9 31.8 slice_reduce_fusion
  117.9 36.3 all-gather.5
  155.6 38.0 all-gather.4
  449.9 12.4 all-gather.7
  536.1 10.6 all-gather.6
  551.5 6.3 multiply_convert_fusion.6
  611.7 44.2 all-reduce.139.cloned.1.call-done
  660.1 99.4 %all-gather.23.cloned.1.call-done = bf16[2048,3072]{1,0:T(8,128)(2,1)} async-done(((bf16[128,3072]{1,0:T(8,128)(2,1)}), bf16[2048,3072]{1,0:T(8,128)(2,1)}) %all-gather.23.cloned.1.call-update) | async-done | bytes 12582928 | tf_op jit(solution)/shard_map/all_gather | solution.py:145
  759.5 8.3 fusion.197
  767.8 93.1 %all-gather.25.cloned.1.call-done = bf16[2048,3072]{1,0:T(8,128)(2,1)} async-done(((bf16[128,3072]{1,0:T(8,128)(2,1)}), bf16[2048,3072]{1,0:T(8,128)(2,1)}) %all-gather.25.cloned.1.call-update) | async-done | bytes 12582928 | tf_op jit(solution)/shard_map/all_gather | solution.py:146
  860.9 8.3 fusion.198
  869.3 96.1 %all-gather.27.cloned.1.call-done = bf16[3072,2048]{1,0:T(8,128)(2,1)} async-done(((bf16[3072,128]{1,0:T(8,128)(2,1)}), bf16[3072,2048]{1,0:T(8,128)(2,1)}) %all-gather.27.cloned.1.call-update) | async-done | bytes 12582928 | tf_op jit(solution)/shard_map/all_gather | solution.py:147
  965.4 13.2 multiply_convert_fusion
  979.5 10.2 fusion.210
  989.8 23.0 reshape.450
  1012.8 10.2 fusion.211
  1023.0 22.6 reshape.451
  1045.6 8.5 fusion.191
  1054.1 8.4 fusion.192
  1068.0 8.2 fusion.199
  1076.2 12.3 multiply_convert_fusion.1
  1088.6 8.6 fusion.193
  1097.2 10.1 convolution_add_fusion.2
  1107.3 10.5 fusion.200
  1117.8 7.0 convolution_add_fusion.3
  1126.0 10.6 fusion.206
  1136.6 23.1 reshape.439
  1159.7 10.3 fusion.207
  1170.0 22.7 reshape.440
  1192.7 11.1 fusion.40
  1203.9 11.0 fusion.42
  1214.9 50.7 all-reduce.137.cloned.1.call-done
  1269.1 6.5 fusion.30
  1390.1 6.4 rev.16
  1397.8 6.4 rev.17
  1404.2 10.7 all-gather.8
  1415.2 6.4 rev.18
  1423.8 10.4 rev.19
  1434.2 10.3 all-gather.9
  1529.0 11.6 reshape.443
  1556.1 10.5 copy.211
  1566.6 11.4 reshape.432
  1593.7 8.9 copy.230
  1608.2 11.6 reshape.442
  1619.8 7.2 constant_dynamic-update-slice_fusion.15
  1632.4 11.5 reshape.431
  1643.9 7.4 constant_dynamic-update-slice_fusion.7
  1661.9 7.6 constant_dynamic-update-slice_fusion.14
  1672.5 8.5 constant_dynamic-update-slice_fusion.6
  1684.1 34.5 all-reduce.141.cloned.1.call-done
  1722.3 7.2 bitcast_dynamic-update-slice_fusion.3
  1729.6 19.6 constant_dynamic-update-slice_fusion.9
  1749.1 19.5 constant_dynamic-update-slice_fusion.8
  1769.9 34.4 bitcast_dynamic-update-slice_fusion
  1805.7 15.8 bitcast_dynamic-update-slice_fusion.2
  1821.4 19.8 constant_dynamic-update-slice_fusion.1
  1841.2 19.8 constant_dynamic-update-slice_fusion
  1862.5 34.6 bitcast_dynamic-update-slice_fusion.1
  1904.0 1669.3 %all-reduce.135.cloned.1.call-done = f32[16,1697664]{1,0:T(8,128)} async-done(((f32[16,1697664]{1,0:T(8,128)}), f32[16,1697664]{1,0:T(8,128)}) %all-reduce.135.cloned.1.call-update) | async-done | bytes 108650512
  3573.3 1771.6 %all-reduce.133.cloned.1.call-done = f32[16,1697664]{1,0:T(8,128)} async-done(((f32[16,1697664]{1,0:T(8,128)}), f32[16,1697664]{1,0:T(8,128)}) %all-reduce.133.cloned.1.call-update) | async-done | bytes 108650512
  5344.9 16.4 fusion.84
  5369.1 30.2 fusion.24
  (1201 shorter events, 700.6 us)
Async XLA Ops:
  7.2 35.3 copy-start.240
  7.2 187.7 %all-gather.19.cloned.1.call-start = ((), (), s32[]{:S(2)}) async-start(), calls=%async_computation.1 | async-start | bytes 5570560 | tf_op jit(solution)/shard_map/all_gather | solution.py:133
  7.9 543.6 %all-gather.17.cloned.1.call-start = ((), (), s32[]{:S(2)}) async-start(), calls=%async_computation | async-start | bytes 5570560 | tf_op jit(solution)/shard_map/all_gather | solution.py:134
  8.7 552.1 %all-gather.21.cloned.1.call-start = ((), (), s32[]{:S(2)}) async-start(), calls=%async_computation.2 | async-start | bytes 5570560 | tf_op jit(solution)/shard_map/all_gather | solution.py:144
  9.4 646.5 %all-reduce.139.cloned.1.call-start = ((), (), s32[]{:S(2)}) async-start(), calls=%async_computation.9 | async-start | bytes 5767168 | tf_op jit(solution)/shard_map/psum | solution.py:225
  10.2 75.7 %copy-start.97 = (f32[2,1280]{1,0:T(2,128)}, f32[2,1280]{1,0:T(2,128)S(1)}, u32[]{:S(2)}) copy-start(f32[2,1280]{1,0:T(2,128)S(1)} %copy.285) | copy-start | bytes 30724
  40.6 517.3 %copy-start.86 = (f32[1,2048]{1,0:T(1,128)}, f32[1,2048]{1,0:T(1,128)S(1)}, u32[]{:S(2)}) copy-start(f32[1,2048]{1,0:T(1,128)S(1)} %get-tuple-element.751) | copy-start | bytes 24580
  40.6 617.6 %copy-start.144 = (f32[1,2048]{1,0:T(1,128)}, f32[1,2048]{1,0:T(1,128)S(1)}, u32[]{:S(2)}) copy-start(f32[1,2048]{1,0:T(1,128)S(1)} %get-tuple-element.750) | copy-start | bytes 24580
  42.4 42.8 copy-start.233
  42.4 75.4 %copy-start.235 = (f32[176]{0:T(256)}, f32[176]{0:T(256)S(1)}, u32[]{:S(2)}) copy-start(f32[176]{0:T(256)S(1)} %get-tuple-element.471) | copy-start | bytes 2116
  42.5 152.4 %copy-start.156 = (f32[176]{0:T(256)}, f32[176]{0:T(256)S(1)}, u32[]{:S(2)}) copy-start(f32[176]{0:T(256)S(1)} %fusion.132) | copy-start | bytes 2116
  85.9 32.0 copy-start.191
  117.8 89.8 %copy-start.148 = (f32[1280]{0:T(1024)}, f32[1280]{0:T(1024)S(1)}, u32[]{:S(2)}) copy-start(f32[1280]{0:T(1024)S(1)} %get-tuple-element.477) | copy-start | bytes 15364
  117.8 89.8 %copy-start.150 = (f32[1280]{0:T(1024)}, f32[1280]{0:T(1024)S(1)}, u32[]{:S(2)}) copy-start(f32[1280]{0:T(1024)S(1)} %get-tuple-element.478) | copy-start | bytes 15364
  117.8 89.8 %copy-start.152 = (f32[1280]{0:T(1024)}, f32[1280]{0:T(1024)S(1)}, u32[]{:S(2)}) copy-start(f32[1280]{0:T(1024)S(1)} %get-tuple-element.479) | copy-start | bytes 15364
  117.8 89.8 %copy-start.154 = (f32[1280]{0:T(1024)}, f32[1280]{0:T(1024)S(1)}, u32[]{:S(2)}) copy-start(f32[1280]{0:T(1024)S(1)} %get-tuple-element.480) | copy-start | bytes 15364
  117.8 109.5 %copy-start.135 = (f32[1280]{0:T(1024)}, f32[1280]{0:T(1024)S(1)}, u32[]{:S(2)}) copy-start(f32[1280]{0:T(1024)S(1)} %get-tuple-element.474) | copy-start | bytes 15364
  117.8 109.5 %copy-start.137 = (f32[1280]{0:T(1024)}, f32[1280]{0:T(1024)S(1)}, u32[]{:S(2)}) copy-start(f32[1280]{0:T(1024)S(1)} %get-tuple-element.476) | copy-start | bytes 15364
  117.8 455.3 %copy-start.146 = (f32[1280]{0:T(1024)}, f32[1280]{0:T(1024)S(1)}, u32[]{:S(2)}) copy-start(f32[1280]{0:T(1024)S(1)} %get-tuple-element.475) | copy-start | bytes 15364
  117.9 84.7 %copy-start.160 = (f32[176]{0:T(256)}, f32[176]{0:T(256)S(1)}, u32[]{:S(2)}) copy-start(f32[176]{0:T(256)S(1)} %fusion.134) | copy-start | bytes 2116
  155.5 60.9 %copy-start.21 = (bf16[8,160,160]{2,1,0:T(8,128)(2,1)}, bf16[8,160,160]{2,1,0:T(8,128)(2,1)S(1)}, u32[]{:S(2)}) copy-start(bf16[8,160,160]{2,1,0:T(8,128)(2,1)S(1)} %reshape.418) | copy-start | bytes 1228804
  194.9 20.1 copy-start.23
  198.8 7.8 collective-permute-start
  203.8 3.7 collective-permute-start.1
  254.9 37.9 copy-start.51
  443.3 20.4 copy-start.140
  443.3 20.4 copy-start.141
  529.5 21.1 copy-start.101
  531.3 20.2 copy-start.161
  568.0 191.5 %all-gather.23.cloned.1.call-start = ((), (), s32[]{:S(2)}) async-start(), calls=%async_computation.3 | async-start | bytes 13369344 | tf_op jit(solution)/shard_map/all_gather | solution.py:145
  568.6 292.3 %all-gather.25.cloned.1.call-start = ((), (), s32[]{:S(2)}) async-start(), calls=%async_computation.4 | async-start | bytes 13369344 | tf_op jit(solution)/shard_map/all_gather | solution.py:146
  569.2 396.2 %all-gather.27.cloned.1.call-start = ((), (), s32[]{:S(2)}) async-start(), calls=%async_computation.5 | async-start | bytes 13369344 | tf_op jit(solution)/shard_map/all_gather | solution.py:147
  569.9 695.7 %all-reduce.137.cloned.1.call-start = ((), (), s32[]{:S(2)}) async-start(), calls=%async_computation.8 | async-start | bytes 11534336 | tf_op jit(solution)/shard_map/psum | solution.py:231
  978.6 34.2 copy-start.55
  1097.1 20.6 slice-start
  1097.1 20.6 slice-start.1
  1124.8 593.9 %all-reduce.141.cloned.1.call-start = ((), (), s32[]{:S(2)}) async-start(), calls=%async_computation.10 | async-start | bytes 2883584 | tf_op jit(solution)/shard_map/psum | solution.py:342
  1170.0 22.7 copy-start.81
  1170.0 22.7 copy-start.120
  1203.9 61.8 %copy-start.11 = (f32[176,2048]{1,0:T(8,128)S(1)}, f32[176,2048]{1,0:T(8,128)}, u32[]{:S(2)}) copy-start(f32[176,2048]{1,0:T(8,128)} %copy-done.10) | copy-start | bytes 4325380
  1203.9 61.8 %copy-start.13 = (f32[176,2048]{1,0:T(8,128)S(1)}, f32[176,2048]{1,0:T(8,128)}, u32[]{:S(2)}) copy-start(f32[176,2048]{1,0:T(8,128)} %copy-done.12) | copy-start | bytes 4325380
  1203.9 61.8 %copy-start.145 = (f32[1,2048]{1,0:T(1,128)S(1)}, f32[1,2048]{1,0:T(1,128)}, u32[]{:S(2)}) copy-start(f32[1,2048]{1,0:T(1,128)} %copy-done.144) | copy-start | bytes 24580
  1203.9 61.8 %copy-start.226 = (f32[176]{0:T(256)S(1)}, f32[176]{0:T(256)}, u32[]{:S(2)}) copy-start(f32[176]{0:T(256)} %copy-done.225) | copy-start | bytes 2116
  1203.9 61.8 %copy-start.228 = (f32[176]{0:T(256)S(1)}, f32[176]{0:T(256)}, u32[]{:S(2)}) copy-start(f32[176]{0:T(256)} %copy-done.227) | copy-start | bytes 2116
  1421.6 23.1 copy-start.37
  1422.7 22.0 copy-start.16
  1423.7 20.7 copy-start.118
  1423.7 21.0 copy-start.9
  1423.7 21.1 copy-start.15
  1423.7 21.1 copy-start.136
  1423.7 21.1 copy-start.138
  1423.8 21.1 copy-start.139
  1508.5 94.0 %collective-permute-start.3 = (f32[3,1280]{1,0:T(4,128)}, f32[3,1280]{1,0:T(4,128)S(1)}, u32[]{:S(2)}, u32[]{:S(2)}) collective-permute-start(f32[3,1280]{1,0:T(4,128)} %slice.1673), channel_id=1, source_target_pairs={{2,0},{4,2},{6,4},{3,1},{5,3},{7,5},{10,8},{12,10},{14,12},{11,9},... | collective-permute-start | bytes 46088 | tf_op jit(solution)/shard_map/ppermute | solution.py:17
  1510.4 116.6 %collective-permute-start.2 = (f32[3,1280]{1,0:T(4,128)}, f32[3,1280]{1,0:T(4,128)S(1)}, u32[]{:S(2)}, u32[]{:S(2)}) collective-permute-start(f32[3,1280]{1,0:T(4,128)} %slice.1634), channel_id=1, source_target_pairs={{2,0},{4,2},{6,4},{3,1},{5,3},{7,5},{10,8},{12,10},{14,12},{11,9},... | collective-permute-start | bytes 46088 | tf_op jit(solution)/shard_map/ppermute | solution.py:17
  1661.8 1911.4 %all-reduce.135.cloned.1.call-start = ((), (), s32[]{:S(2)}) async-start(), calls=%async_computation.7 | async-start | bytes 217300992
  1729.6 39.1 slice-start.9
  1729.6 39.1 slice-start.10
  1729.6 39.1 slice-start.11
  1749.1 20.8 slice-start.14
  1804.4 3540.5 %all-reduce.133.cloned.1.call-start = ((), (), s32[]{:S(2)}) async-start(), calls=%async_computation.6 | async-start | bytes 217300992
  1821.4 39.6 slice-start.3
  1821.4 39.6 slice-start.4
  1821.4 39.6 slice-start.5
  1841.2 21.3 slice-start.8
  (216 other events, 1308.7 us)
Sparse Core Ops, SparseCore 0:
  10.3 62.6 all-gather.18
  75.3 57.5 all-gather.16
  135.0 64.1 all-gather.20
  568.1 87.7 all-reduce.138
  658.3 101.1 all-gather.22
  762.0 98.9 all-gather.24
  863.2 102.1 all-gather.26
  1124.9 140.6 all-reduce.136
  1661.9 56.6 all-reduce.140
  1804.5 1768.7 all-reduce.134
  3577.6 1767.2 all-reduce.132
where the time goes:
time: 5430 us; the launch traced here: 5410 us
  waiting for transfers between devices  3860 us (71%)
  local copies, waits for them, and re-layouts  803 us (15%)
  matrix products  273 us (5%)
  other arithmetic  251 us (5%)
  blocking collectives  191 us (4%)
    unnamed x13, waiting for transfers between devices  3440 us
    unnamed x555, local copies, waits for them, and re-layouts  168 us
    reshape x8, local copies, waits for them, and re-layouts, rows_of(): return term.reshape(count, -1)  137 us
    slice x96, local copies, waits for them, and re-layouts, forward_pass(): lax.associative_scan(combine, (decay_rate, drive_term), axis=0)  129 us
  transfers between devices with their start and end apart: 15, of which 9 were waited for; matrix products, arithmetic and copies ran while one was open for 14% of the time, Pallas kernels for 0%

commit v1 on v0

v1 whole, which is shorter than its diff:
```python
import jax
import jax.numpy as jnp
import numpy as np
from jax import lax
from jax.experimental import pallas as pl
from jax.experimental.pallas import tpu as pltpu
from jax.sharding import Mesh, PartitionSpec as P

WIDTH = 2560
HEADS = 16
BLOCK = WIDTH // HEADS
EPSILON = 1e-06
DECAY_SCALE = 8.0
AXES = ("dx", "dc", "zh", "zl", "mp")
BF = jnp.bfloat16
F32 = jnp.float32


def swap_pairs(sizes, partner):
    pairs = []
    for flat in range(int(np.prod(sizes))):
        coords = np.unravel_index(flat, sizes)
        pairs.append((flat, int(np.ravel_multi_index(partner(*map(int, coords)), sizes))))
    return pairs


def gather_blocks(x, axis, dim):
    if lax.axis_size(axis) != 2:
        return lax.all_gather(x, axis, axis=dim, tiled=False)
    here = lax.axis_index(axis)
    other = lax.ppermute(x, axis, [(0, 1), (1, 0)])
    low = jnp.where(here == 0, x, other)
    high = jnp.where(here == 0, other, x)
    return jnp.stack([low, high], axis=dim)


def scatter_blocks(x, axis, dim):
    if lax.axis_size(axis) != 2:
        n = x.shape[dim]
        out = lax.psum_scatter(x.astype(BF), axis, scatter_dimension=dim, tiled=True)
        return lax.squeeze(out, [dim]).astype(F32)
    here = lax.axis_index(axis)
    mine = lax.dynamic_index_in_dim(x, here, dim, keepdims=False)
    theirs = lax.dynamic_index_in_dim(x, 1 - here, dim, keepdims=False)
    got = lax.ppermute(theirs.astype(BF), axis, [(0, 1), (1, 0)])
    return mine.astype(F32) + got.astype(F32)


def fetch_weight(shard, parts):
    rows, cols = shard[0].shape[0], None
    pieces = [s.reshape(rows, parts, -1) for s in shard]
    joined = jnp.concatenate(pieces, axis=2) if len(pieces) > 1 else pieces[0]
    cols = joined.shape[2]
    x = jnp.transpose(joined, (1, 0, 2))
    x = lax.all_to_all(x, ("dc", "zl"), 0, 0, tiled=True)
    x = x.reshape(2, 2, rows, cols)
    x = gather_blocks(x, "zh", 1)
    x = gather_blocks(x, "dx", 0)
    return x.reshape(-1, cols)


def return_grad(grad, rows):
    cols = grad.shape[1]
    dxn, zhn = lax.axis_size("dx"), lax.axis_size("zh")
    g = grad.reshape(dxn, 2, zhn, 2, rows, cols)
    g = scatter_blocks(g, "dx", 0)
    g = scatter_blocks(g, "zh", 1)
    g = g.astype(BF).reshape(4, rows, cols)
    return lax.all_to_all(g, ("dc", "zl"), 0, 0, tiled=True)


class Tokens:
    def __init__(self, sizes):
        self.core = swap_pairs(sizes, lambda a, b, c, d, e: (a, 1 - b, c, d, e))
        self.first = swap_pairs(
            sizes, lambda a, b, c, d, e: (a, b, c, d, 1 - e) if b == 0 else (a, b, c, 1 - d, e)
        )
        self.second = swap_pairs(
            sizes, lambda a, b, c, d, e: (a, b, c, 1 - d, e) if b == 0 else (a, b, c, d, 1 - e)
        )
        self.dc, self.zl, self.mp = (lax.axis_index(n) for n in ("dc", "zl", "mp"))

    def order(self, dc):
        mp, zl = self.mp, self.zl
        own = mp * 2 + zl
        by_mp = (1 - mp) * 2 + zl
        by_zl = mp * 2 + 1 - zl
        both = (1 - mp) * 2 + 1 - zl
        one = jnp.where(dc == 0, by_mp, by_zl)
        two = jnp.where(dc == 0, by_zl, by_mp)
        return own, one, two, both

    def gather(self, x):
        rows, width = x.shape
        one = lax.ppermute(x, AXES, self.first)
        two = lax.ppermute(jnp.stack([x, one]), AXES, self.second)
        far = [lax.ppermute(v, AXES, self.core) for v in (x, one, two)]
        out = jnp.zeros((8, rows, width), x.dtype)
        for dc, blocks in (
            (self.dc, (x, one, two[0], two[1])),
            (1 - self.dc, (far[0], far[1], far[2][0], far[2][1])),
        ):
            for at, block in zip(self.order(dc), blocks):
                out = lax.dynamic_update_index_in_dim(out, block, dc * 4 + at, 0)
        return out.reshape(8 * rows, width)

    def scatter(self, x):
        rows, width = x.shape[0] // 8, x.shape[1]
        x = x.reshape(2, 4, rows, width)
        theirs = lax.dynamic_index_in_dim(x, 1 - self.dc, 0, keepdims=False).astype(BF)
        mine = lax.dynamic_index_in_dim(x, self.dc, 0, keepdims=False)
        total = mine.astype(F32) + lax.ppermute(theirs, AXES, self.core).astype(F32)
        own, one, two, both = self.order(self.dc)
        pick = lambda at: lax.dynamic_index_in_dim(total, at, 0, keepdims=False)
        got = lax.ppermute(jnp.stack([pick(two), pick(both)]).astype(BF), AXES, self.second)
        keep_own = pick(own) + got[0].astype(F32)
        keep_one = pick(one) + got[1].astype(F32)
        got = lax.ppermute(keep_one.astype(BF), AXES, self.first)
        return keep_own + got.astype(F32)


def scan_body(reverse, a_ref, b_ref, p_ref, h_ref):
    length, width = a_ref.shape[1], a_ref.shape[2]
    row = lax.broadcasted_iota(jnp.int32, (8, width), 0)

    def tile(i, carry):
        ca, ch = carry
        at = (length // 8 - 1 - i if reverse else i) * 8
        at = pl.multiple_of(at, 8)
        a = a_ref[0, pl.ds(at, 8), :]
        b = b_ref[0, pl.ds(at, 8), :]
        for step in (1, 2, 4):
            if reverse:
                inside = row < 8 - step
                shift = 8 - step
            else:
                inside = row >= step
                shift = step
            sa = jnp.where(inside, pltpu.roll(a, shift, 0), 1.0)
            sb = jnp.where(inside, pltpu.roll(b, shift, 0), 0.0)
            b = b + a * sb
            a = a * sa
        h = b + a * ch
        p = a * ca
        h_ref[0, pl.ds(at, 8), :] = h
        p_ref[0, pl.ds(at, 8), :] = p
        last = 0 if reverse else 7
        return p[last : last + 1, :], h[last : last + 1, :]

    lax.fori_loop(
        0,
        length // 8,
        tile,
        (jnp.ones((1, width), F32), jnp.zeros((1, width), F32)),
    )


def local_scan(a, b, reverse):
    segs, length, width = a.shape
    spec = pl.BlockSpec((1, length, width), lambda s: (s, 0, 0))
    return pl.pallas_call(
        lambda *refs: scan_body(reverse, *refs),
        grid=(segs,),
        in_specs=[spec, spec],
        out_specs=[spec, spec],
        out_shape=[jax.ShapeDtypeStruct(a.shape, F32)] * 2,
        cost_estimate=pl.CostEstimate(
            flops=20 * a.size, bytes_accessed=16 * a.size, transcendentals=0
        ),
    )(a, b)


def carried(product, state, reverse):
    count = lax.axis_size("zh")
    if count == 2:
        return lax.ppermute(state, "zh", [(1, 0)] if reverse else [(0, 1)])
    here = lax.axis_index("zh")
    pairs = lax.all_gather(jnp.stack([product, state]), "zh")
    total = jnp.zeros_like(state)
    for k in range(count):
        at = count - 1 - k if reverse else k
        reached = at > here if reverse else at < here
        total = jnp.where(reached, pairs[at, 1] + pairs[at, 0] * total, total)
    return total


def from_behind(x, by):
    count = lax.axis_size("zh")
    return lax.ppermute(
        x, "zh", [(i, i + by) for i in range(count) if 0 <= i + by < count]
    )


def inverse_rms(values):
    return lax.rsqrt(jnp.mean(values * values, axis=-1, keepdims=True) + EPSILON)


def norm_grad(values, gain, upstream):
    inv = inverse_rms(values)
    scaled = values * inv
    up = upstream * gain
    inner = jnp.mean(up * scaled, axis=-1, keepdims=True)
    return inv * (up - scaled * inner), jnp.sum(upstream * scaled, axis=0)


def gelu(v):
    return jax.nn.gelu(v, approximate=True)


def gelu_both(v):
    c = 0.7978845608028654
    t = jnp.tanh(c * (v + 0.044715 * v * v * v))
    value = 0.5 * v * (1.0 + t)
    slope = 0.5 * (1.0 + t) + 0.5 * v * (1.0 - t * t) * c * (1.0 + 3 * 0.044715 * v * v)
    return value, slope


def dot(a, b, dims, out=F32):
    r = lax.dot_general(a, b, (dims, ((), ())), preferred_element_type=F32)
    return r.astype(out)


NN = ((1,), (0,))
NT = ((1,), (1,))
TN = ((0,), (0,))


def on_device(
    tokens_in,
    cotangent,
    seq_source,
    source_weight,
    input_weight,
    gelu_weight,
    decay_gates,
    input_gates,
    channel_params,
    norm_gains,
    output_weight,
    mlp_gate,
    mlp_up,
    mlp_down,
):
    sizes = tuple(lax.axis_size(n) for n in AXES)
    dxn, _, zhn, _, _ = sizes
    group = dxn * 2 * zhn * 2
    dc, zl, mp = (lax.axis_index(n) for n in ("dc", "zl", "mp"))
    slot = dc * 2 + zl
    exchange = Tokens(sizes)
    length = tokens_in.shape[2]
    width = tokens_in.shape[3]
    local = input_weight.shape[1] // 4
    heads = decay_gates.shape[0] // 4
    drows = input_weight.shape[0]
    piece = decay_gates.shape[1]

    own = lax.dynamic_index_in_dim(tokens_in[:, 0], mp, 0, keepdims=False)
    own_cot = lax.dynamic_index_in_dim(cotangent[:, 0], mp, 0, keepdims=False).astype(F32)
    source = lax.dynamic_index_in_dim(seq_source[:, 0], mp, 0, keepdims=False)
    scale = jnp.sum(
        jnp.where(jnp.arange(source_weight.shape[0], dtype=jnp.int32) == source, source_weight, 0.0)
    )
    dout = own_cot * scale
    tokens = exchange.gather(own)
    dm = exchange.gather(dout.astype(BF))

    small = jnp.concatenate([channel_params.reshape(-1), norm_gains.reshape(-1)])
    small = lax.all_gather(small, ("dx", "dc", "zh", "zl"))
    nch = channel_params.size
    channels = small[:, :nch].reshape(group, 8, -1).transpose(1, 0, 2).reshape(8, -1)
    channels = lax.dynamic_slice_in_dim(channels, slot * local, local, 1).astype(F32)
    gains = small[:, nch:].reshape(group, 2, -1).transpose(1, 0, 2).reshape(2, -1).astype(F32)

    w_ig = fetch_weight([input_weight, gelu_weight], 4)
    gates = jnp.stack([decay_gates, input_gates]).reshape(2, 4, heads, piece)
    gates = gates.transpose(1, 0, 2, 3)
    gates = lax.all_to_all(gates, ("dc", "zl"), 0, 0, tiled=True).reshape(2, 2, 2 * heads * piece)
    gates = gather_blocks(gather_blocks(gates, "zh", 1), "dx", 0)
    gates = gates.reshape(group, 2 * heads, piece).transpose(1, 0, 2)
    gates = gates.reshape(2, heads, BLOCK, BLOCK)
    w_o = fetch_weight([output_weight.T], 4)
    ff = mlp_gate.shape[1] // 4
    half = ff // 2

    gate4, up4, down4 = (v.reshape(drows, 4, ff) for v in (mlp_gate, mlp_up, mlp_down.T))
    w_gu = []
    for k in range(2):
        cut = slice(k * half, (k + 1) * half)
        w_gu.append(
            fetch_weight(
                [gate4[:, :, cut].reshape(drows, -1), up4[:, :, cut].reshape(drows, -1)], 4
            )
        )
    w_d = fetch_weight([down4.reshape(drows, -1)], 4)

    wide = tokens.astype(F32)
    n1 = (wide * inverse_rms(wide) * gains[0]).astype(BF)
    both = dot(n1, w_ig, NN)
    xb = both[:, :local].astype(BF).reshape(4, 2 * length, local)
    gy = both[:, local:].reshape(4, 2 * length, local)
    rim = from_behind(xb[:, -3:], 1)
    padded = jnp.concatenate([rim, xb], axis=1).astype(F32)
    conv = channels[3]
    for k in range(4):
        conv = conv + channels[4 + k] * padded[:, 3 - k : 3 - k + 2 * length]
    u = conv.astype(BF)
    zero = jnp.zeros((BLOCK, BLOCK), BF)
    blocks = jnp.concatenate(
        [
            jnp.concatenate(
                [gates[g, h] if k == h else zero for g in range(2) for k in range(heads)], axis=1
            )
            for h in range(heads)
        ],
        axis=0,
    )
    u2 = u.reshape(-1, local)
    logits = dot(u2, blocks, NN).reshape(4, 2 * length, 2 * local)
    sig_a = jax.nn.sigmoid(logits[..., :local] + channels[1])
    sig_i = jax.nn.sigmoid(logits[..., local:] + channels[2])
    soft = jax.nn.softplus(-channels[0])
    log_decay = -DECAY_SCALE * sig_a * soft
    decay = jnp.exp(log_decay)
    root = jnp.sqrt(-jnp.expm1(2.0 * log_decay))
    uf = u.astype(F32)
    drive = root * sig_i * uf
    running, state = local_scan(decay, drive, False)
    incoming = carried(running[:, -1], state[:, -1], False)
    states = state + running * incoming[:, None]
    gelu_y, slope_y = gelu_both(gy)
    mixed = (gelu_y * states).astype(BF).reshape(-1, local)
    middle = own.astype(F32) + exchange.scatter(dot(mixed, w_o, NT))
    n2_own = (middle * inverse_rms(middle) * gains[1]).astype(BF)
    n2 = exchange.gather(n2_own)

    hidden, gates_pre = [], []
    for k in range(2):
        pre = dot(n2, w_gu[k], NN)
        gm, up = pre[:, :half], pre[:, half:]
        gates_pre.append((gm, up))
        hidden.append((gelu(gm) * up).astype(BF))
    hidden = jnp.concatenate(hidden, axis=1)
    g_down = dot(dm, hidden, TN, BF)
    share_down = return_grad(g_down, drows)
    dhm = dot(dm, w_d, NN)
    pair_grads, g_gu, dn2 = [], [], None
    for k in range(2):
        gm, up = gates_pre[k]
        value, slope = gelu_both(gm)
        d = dhm[:, k * half : (k + 1) * half]
        pair = jnp.concatenate([(d * up * slope).astype(BF), (d * value).astype(BF)], axis=1)
        pair_grads.append(pair)
        term = dot(pair, w_gu[k], NT)
        dn2 = term if dn2 is None else dn2 + term
    share_gu = [return_grad(dot(n2, pair_grads[k], TN, BF), drows) for k in range(2)]
    dn2_own = exchange.scatter(dn2)
    part, gain_two = norm_grad(middle, gains[1], dn2_own)
    dr1 = dout + part
    do = exchange.gather(dr1.astype(BF))

    result = middle + exchange.scatter(dot(hidden, w_d, NT))
    result = result.astype(BF)

    share_o = return_grad(dot(do, mixed, TN, BF), drows)
    dz = dot(do, w_o, NN).reshape(4, 2 * length, local)
    dh = dz * gelu_y
    dgy = (dz * states * slope_y).astype(BF)
    ones = jnp.ones_like(decay[:, :1])
    after, adjoint = local_scan(jnp.concatenate([decay[:, 1:], ones], axis=1), dh, True)
    later = carried(running[:, -1], decay[:, 0] * adjoint[:, 0], True)
    adjoint = adjoint + after * later[:, None]
    previous = jnp.concatenate([incoming[:, None], states[:, :-1]], axis=1)
    d_root = adjoint * sig_i * uf
    d_sig_i = adjoint * root * uf
    du0 = adjoint * root * sig_i
    d_log = adjoint * previous * decay - d_root * decay * decay / root
    dra = (d_log * (-DECAY_SCALE * soft) * sig_a * (1.0 - sig_a)).astype(BF)
    dri = (d_sig_i * sig_i * (1.0 - sig_i)).astype(BF)
    dlam = jnp.sum(d_log * sig_a, axis=(0, 1)) * DECAY_SCALE * jax.nn.sigmoid(-channels[0])
    dlogits = jnp.concatenate([dra, dri], axis=2).reshape(-1, 2 * local)
    g_blocks = dot(u2, dlogits, TN)
    du = du0 + dot(dlogits, blocks, NT).reshape(4, 2 * length, local)
    zeros = jnp.zeros((4, 3, local), F32)
    spread = jnp.concatenate([zeros, du, zeros], axis=1)
    dpad = jnp.zeros((4, 2 * length + 3, local), F32)
    taps = []
    for k in range(4):
        dpad = dpad + channels[4 + k] * spread[:, k : k + 2 * length + 3]
        taps.append(jnp.sum(du * padded[:, 3 - k : 3 - k + 2 * length], axis=(0, 1)))
    back = from_behind(dpad[:, :3], -1)
    dxb = dpad[:, 3:] + jnp.concatenate(
        [jnp.zeros((4, 2 * length - 3, local), F32), back], axis=1
    )
    dboth = jnp.concatenate([dxb.astype(BF), dgy], axis=2).reshape(-1, 2 * local)
    share_ig = return_grad(dot(n1, dboth, TN, BF), drows)
    dn1_own = exchange.scatter(dot(dboth, w_ig, NT))
    part, gain_one = norm_grad(own.astype(F32), gains[0], dn1_own)
    dx_own = dr1 + part

    g_gates = jnp.stack(
        [
            jnp.stack(
                [
                    g_blocks[
                        h * BLOCK : (h + 1) * BLOCK,
                        g * local + h * BLOCK : g * local + (h + 1) * BLOCK,
                    ]
                    for h in range(heads)
                ]
            )
            for g in range(2)
        ]
    )
    g_gates = g_gates.reshape(2 * heads, group, piece).transpose(1, 0, 2)
    g_gates = g_gates.reshape(dxn, 2, zhn, 2, 2 * heads * piece)
    g_gates = scatter_blocks(scatter_blocks(g_gates, "dx", 0), "zh", 1)
    g_gates = g_gates.reshape(4, 2, heads, piece).astype(BF)
    g_gates = lax.all_to_all(g_gates, ("dc", "zl"), 0, 0, tiled=True).astype(F32)
    g_gates = g_gates.transpose(1, 0, 2, 3).reshape(2, 4 * heads, piece)

    channel_grad = jnp.stack(
        [
            dlam,
            jnp.sum(dra.astype(F32), axis=(0, 1)),
            jnp.sum(dri.astype(F32), axis=(0, 1)),
            jnp.sum(du, axis=(0, 1)),
        ]
        + taps
    )
    spot = (mp * 4 + slot).astype(jnp.int32)
    table = jnp.where(
        jnp.arange(8, dtype=jnp.int32)[:, None, None] == spot, channel_grad[None], 0.0
    )
    sums = jnp.concatenate([table.reshape(-1), gain_one, gain_two])
    sums = lax.psum(sums, AXES)
    share = lax.axis_index(("dx", "dc", "zh", "zl"))
    table = sums[: table.size].reshape(2, 4, 8, local).transpose(0, 2, 1, 3)
    table = lax.dynamic_index_in_dim(table.reshape(2, 8, 4 * local), mp, 0, keepdims=False)
    per = 4 * local // group
    g_channels = lax.dynamic_slice_in_dim(table, share * per, per, 1).reshape(8, 1, per)
    g_gains = sums[-2 * width :].reshape(2, width)
    g_gains = lax.dynamic_slice_in_dim(g_gains, share * drows, drows, 1)

    def both_batches(rows):
        other = lax.ppermute(rows, "mp", [(0, 1), (1, 0)])
        return jnp.stack([jnp.where(mp == 0, rows, other), jnp.where(mp == 0, other, rows)])

    block_out = both_batches(result)[:, None]
    grad_tokens = both_batches(dx_own)[:, None]

    def columns(share, at, count):
        return (
            share[:, :, at : at + count].astype(F32).transpose(1, 0, 2).reshape(drows, 4 * count)
        )

    g_gate = jnp.stack([s[:, :, :half] for s in share_gu], axis=2)
    g_up = jnp.stack([s[:, :, half:] for s in share_gu], axis=2)
    g_gate, g_up = (
        v.astype(F32).transpose(1, 0, 2, 3).reshape(drows, 4 * ff) for v in (g_gate, g_up)
    )
    return (
        block_out,
        grad_tokens,
        columns(share_ig, 0, local),
        columns(share_ig, local, local),
        g_gates[0],
        g_gates[1],
        g_channels,
        g_gains,
        columns(share_o, 0, local).T,
        g_gate,
        g_up,
        columns(share_down, 0, ff).T,
    )


def solution(mesh):
    dpn, seqn, mpn = (mesh.shape[n] for n in ("dp", "seq", "mp"))
    fine = Mesh(mesh.devices.reshape(dpn // 2, 2, seqn // 2, 2, mpn), AXES)
    dp, seq = ("dx", "dc"), ("zh", "zl")
    shards = dp + seq
    weights = (
        P(shards, "mp"),
        P(shards, "mp"),
        P("mp", shards),
        P("mp", shards),
        P(None, "mp", shards),
        P(None, shards),
        P("mp", shards),
        P(shards, "mp"),
        P(shards, "mp"),
        P("mp", shards),
    )
    rows = P(None, dp, seq, None)
    return jax.shard_map(
        on_device,
        mesh=fine,
        in_specs=(rows, rows, P(None, dp), P()) + weights,
        out_specs=(rows, rows) + weights,
        check_vma=False,
    )
```

time: 5430 us -> 1130 us (0.21)
  waiting for transfers between devices: 3860 us -> 480 us
  local copies, waits for them, and re-layouts: 803 us -> 154 us
  starting transfers between devices: 9.73 us -> 177 us
  matrix products: 273 us -> 108 us
  blocking collectives: 191 us -> 30 us
  other arithmetic: 251 us -> 146 us
    unnamed x13 -> x1, waiting for transfers between devices: 3440 us -> 0.02 us
    ppermute x4 -> x62, waiting for transfers between devices: 0.68 us -> 330 us  [the longest x12 176 us: gather_blocks(): other = lax.ppermute(x, axis, [(0, 1), (1, 0)])]
    all_gather x6 -> x0, waiting for transfers between devices: 289 us -> none  [the longest x1 99.4 us: gather_second(): lax.all_gather(mlp_gate, ('dp', 'seq'), axis=0, tiled=True)]
    slice x214 -> x15, local copies, waits for them, and re-layouts: 239 us -> 11.8 us  [the longest x2 5.81 us: on_device(): gy = both[:, local:].reshape(4, 2 * length, local)]
    reshape x31 -> x21, local copies, waits for them, and re-layouts: 186 us -> 21 us  [the longest x2 4.01 us: on_device(): g_gates = g_gates.reshape(2 * heads, group, piece).transpose(1, 0, 2)]
    dot_general x48 -> x18, matrix products: 273 us -> 108 us  [dot(): r = lax.dot_general(a, b, (dims, ((), ())), preferred_element_type=F32)]
    all_gather x8 -> x1, blocking collectives: 191 us -> 30 us  [on_device(): small = lax.all_gather(small, ('dx', 'dc', 'zh', 'zl'))]
    unnamed x555 -> x225, local copies, waits for them, and re-layouts: 168 us -> 29.1 us
  transfers between devices with their start and end apart: 15 -> 75, of which waited for: 9 -> 26; matrix products, arithmetic and copies ran while one was open for 14% -> 29% of each run, Pallas kernels for 0% -> 1%
where the time goes in v1:
time: 1130 us; the launch traced here: 1120 us
  waiting for transfers between devices  480 us (42%)
  starting transfers between devices  177 us (16%)
  local copies, waits for them, and re-layouts  154 us (14%)
  other arithmetic  146 us (13%)
  matrix products  108 us (10%)
  blocking collectives  30 us (3%)
  between operations  16.6 us (1%)
  Pallas kernels  12.6 us (1%)
    ppermute x12, waiting for transfers between devices, gather_blocks(): other = lax.ppermute(x, axis, [(0, 1), (1, 0)])  176 us
    ppermute x12, waiting for transfers between devices, scatter_blocks(): got = lax.ppermute(theirs.astype(BF), axis, [(0, 1), (1, 0)])  119 us
    psum x1, waiting for transfers between devices, on_device(): sums = lax.psum(sums, AXES)  117 us
    dot_general x18, matrix products, dot(): r = lax.dot_general(a, b, (dims, ((), ())), preferred_element_type=F32)  108 us
    ppermute x12, starting transfers between devices, gather(): far = [lax.ppermute(v, AXES, self.core) for v in (x, one, two)]  52.7 us
    dynamic_update_slice x28, local copies, waits for them, and re-layouts, gather(): out = lax.dynamic_update_index_in_dim(out, block, dc * 4 + at, 0)  33.8 us
    all_to_all x5, starting transfers between devices, fetch_weight(): x = lax.all_to_all(x, ('dc', 'zl'), 0, 0, tiled=True)  30.7 us
    all_gather x1, blocking collectives, on_device(): small = lax.all_gather(small, ('dx', 'dc', 'zh', 'zl'))  30 us
  transfers between devices with their start and end apart: 75, of which 26 were waited for; matrix products, arithmetic and copies ran while one was open for 29% of the time, Pallas kernels for 1%

profile of v1, /device:TPU:1, one launch (start us, length us, event | category | flops | bytes accessed | tf_op | source)
XLA Modules:
  0.0 1124.5 jit_solution(14678745070411948513)
XLA Ops:
  19.1 30.0 %all-gather.1 = bf16[16,1,896]{2,1,0:T(2,128)(2,1)S(1)} all-gather(bf16[1,1,896]{2,1,0:T(2,128)(2,1)S(1)} %reshape.494), channel_id=2, replica_groups=mesh['dx'=2,'dc'=2,'zh'=2,'zl'=2,'mp'=2] {'dx','dc','zh','zl'}, dimensions={0}, use_global_device_ids=true | all-gather | bytes 30464 | tf_op jit(solution)/shard_map/all_gather | solution.py:268
  61.3 7.6 all-to-all-start.2
  78.4 4.9 all-to-all-start
  93.0 7.7 all-to-all-start.3
  106.5 17.8 %collective-permute-done.5 = bf16[2,2,128,640]{3,2,1,0:T(8,128)(2,1)S(1)} collective-permute-done((bf16[2,2,128,640]{3,2,1,0:T(8,128)(2,1)S(1)}, bf16[2,2,128,640]{3,2,1,0:T(8,128)(2,1)S(1)}, u32[]{:S(2)}, u32[]{:S(2)}) %collective-permute-start.5) | collective-permute-done | bytes 655392 | tf_op jit(solution)/shard_map/ppermute | solution.py:31
  124.9 12.4 %collective-permute-start.4 = (bf16[2,176,2048]{2,1,0:T(8,128)(2,1)}, bf16[2,176,2048]{2,1,0:T(8,128)(2,1)S(1)}, u32[]{:S(2)}, u32[]{:S(2)}) collective-permute-start(bf16[2,176,2048]{2,1,0:T(8,128)(2,1)} %collective-permute-done.1), channel_id=1, source_target_pairs={{0,8},{1,9},{2,10},{3,11},{4,12},{5,13},{6,14},{7,15},{8,0},{9,1},... | collective-permute-start | bytes 4325384 | tf_op jit(solution)/shard_map/ppermute | solution.py:97
  145.6 5.2 collective-permute-done.6
  157.2 4.0 fusion.2
  161.3 4.6 fusion.127
  169.0 5.0 collective-permute-start.7
  180.8 4.7 convert_multiply_fusion.4
  185.5 6.2 shard_map.229
  204.6 5.2 multiply_convert_fusion.3
  214.0 4.2 copy-done.6
  220.2 13.5 %collective-permute-start.13 = (bf16[4,176,2048]{2,1,0:T(8,128)(2,1)}, bf16[4,176,2048]{2,1,0:T(8,128)(2,1)}, u32[]{:S(2)}, u32[]{:S(2)}) collective-permute-start(bf16[4,176,2048]{2,1,0:T(8,128)(2,1)} %fusion.3), channel_id=1, source_target_pairs={{0,8},{1,9},{2,10},{3,11},{4,12},{5,13},{6,14},{7,15},{8,0},{9,1},... | collective-permute-start | bytes 8650760 | tf_op jit(solution)/shard_map/ppermute | solution.py:112
  234.8 5.5 all-to-all-start.5
  246.8 5.2 all-to-all-done.5
  252.0 5.0 all-to-all-start.4
  268.3 4.8 bitcast_add_fusion.3
  273.5 62.0 %collective-permute-done.21 = bf16[2,2,128,768]{3,2,1,0:T(8,128)(2,1)} collective-permute-done((bf16[2,2,128,768]{3,2,1,0:T(8,128)(2,1)}, bf16[2,2,128,768]{3,2,1,0:T(8,128)(2,1)}, u32[]{:S(2)}, u32[]{:S(2)}) %collective-permute-start.21) | collective-permute-done | bytes 786464 | tf_op jit(solution)/shard_map/ppermute | solution.py:31
  339.4 13.0 %collective-permute-done.25 = bf16[2,2,128,768]{3,2,1,0:T(8,128)(2,1)} collective-permute-done((bf16[2,2,128,768]{3,2,1,0:T(8,128)(2,1)S(1)}, bf16[2,2,128,768]{3,2,1,0:T(8,128)(2,1)}, u32[]{:S(2)}, u32[]{:S(2)}) %collective-permute-start.25) | collective-permute-done | bytes 786464 | tf_op jit(solution)/shard_map/ppermute | solution.py:31
  355.4 13.8 %collective-permute-done.23 = bf16[2,2,128,768]{3,2,1,0:T(8,128)(2,1)S(1)} collective-permute-done((bf16[2,2,128,768]{3,2,1,0:T(8,128)(2,1)}, bf16[2,2,128,768]{3,2,1,0:T(8,128)(2,1)S(1)}, u32[]{:S(2)}, u32[]{:S(2)}) %collective-permute-start.23) | collective-permute-done | bytes 786464 | tf_op jit(solution)/shard_map/ppermute | solution.py:31
  379.0 13.8 %collective-permute-done.15 = bf16[176,2048]{1,0:T(8,128)(2,1)S(1)} collective-permute-done((bf16[176,2048]{1,0:T(8,128)(2,1)S(1)}, bf16[176,2048]{1,0:T(8,128)(2,1)S(1)}, u32[]{:S(2)}, u32[]{:S(2)}) %collective-permute-start.15) | collective-permute-done | bytes 720928 | tf_op jit(solution)/shard_map/ppermute | solution.py:118
  392.8 13.2 %collective-permute-start.35 = (bf16[2,176,2048]{2,1,0:T(8,128)(2,1)}, bf16[2,176,2048]{2,1,0:T(8,128)(2,1)S(1)}, u32[]{:S(2)}, u32[]{:S(2)}) collective-permute-start(bf16[2,176,2048]{2,1,0:T(8,128)(2,1)} %collective-permute-done.32), channel_id=1, source_target_pairs={{0,8},{1,9},{2,10},{3,11},{4,12},{5,13},{6,14},{7,15},{8,0},{9,1},... | collective-permute-start | bytes 4325384 | tf_op jit(solution)/shard_map/ppermute | solution.py:97
  408.5 28.1 %collective-permute-done.24 = bf16[2,2,2,128,768]{4,3,2,0,1:T(8,128)(2,1)S(1)} collective-permute-done((bf16[2,2,2,128,768]{4,3,2,0,1:T(8,128)(2,1)S(1)}, bf16[2,2,2,128,768]{4,3,2,0,1:T(8,128)(2,1)S(1)}, u32[]{:S(2)}, u32[]{:S(2)}) %collective-permute-start.24) | collective-permute-done | bytes 1572896 | tf_op jit(solution)/shard_map/ppermute | solution.py:31
  439.1 31.2 %collective-permute-done.26 = bf16[2,2,2,128,768]{4,3,2,1,0:T(8,128)(2,1)S(1)} collective-permute-done((bf16[2,2,2,128,768]{4,3,2,1,0:T(8,128)(2,1)S(1)}, bf16[2,2,2,128,768]{4,3,2,1,0:T(8,128)(2,1)S(1)}, u32[]{:S(2)}, u32[]{:S(2)}) %collective-permute-start.26) | collective-permute-done | bytes 1572896 | tf_op jit(solution)/shard_map/ppermute | solution.py:31
  480.0 5.6 fusion.128
  485.6 5.3 fusion.129
  491.9 7.5 fusion.131
  499.4 4.8 fusion.46
  504.2 7.0 convolution_convert_fusion.2
  511.2 7.5 fusion.79
  518.7 6.5 convolution_convert_fusion.1
  525.2 9.8 convolution_add_fusion
  537.7 11.2 convolution_convert_fusion
  558.0 4.2 copy.176
  562.3 7.3 fusion.130
  572.6 47.2 %collective-permute-done.56 = bf16[2,2,2,128,768]{4,3,2,1,0:T(8,128)(2,1)} collective-permute-done((bf16[2,2,2,128,768]{4,3,2,1,0:T(8,128)(2,1)}, bf16[2,2,2,128,768]{4,3,2,1,0:T(8,128)(2,1)}, u32[]{:S(2)}, u32[]{:S(2)}) %collective-permute-start.56) | collective-permute-done | bytes 1572896 | tf_op jit(solution)/shard_map/ppermute | solution.py:45
  623.4 4.8 bitcast_add_fusion.1
  632.6 20.9 %collective-permute-done.58 = bf16[2,2,2,128,768]{4,3,2,1,0:T(8,128)(2,1)} collective-permute-done((bf16[2,2,2,128,768]{4,3,2,1,0:T(8,128)(2,1)}, bf16[2,2,2,128,768]{4,3,2,1,0:T(8,128)(2,1)}, u32[]{:S(2)}, u32[]{:S(2)}) %collective-permute-start.58) | collective-permute-done | bytes 1572896 | tf_op jit(solution)/shard_map/ppermute | solution.py:45
  667.9 6.0 all-to-all-start.9
  673.9 37.8 %collective-permute-done.59 = bf16[2,2,128,768]{3,2,1,0:T(8,128)(2,1)} collective-permute-done((bf16[2,2,128,768]{3,2,1,0:T(8,128)(2,1)}, bf16[2,2,128,768]{3,2,1,0:T(8,128)(2,1)}, u32[]{:S(2)}, u32[]{:S(2)}) %collective-permute-start.59) | collective-permute-done | bytes 786464 | tf_op jit(solution)/shard_map/ppermute | solution.py:45
  716.5 4.8 bitcast_add_fusion.2
  725.1 11.4 %collective-permute-done.38 = bf16[176,2048]{1,0:T(8,128)(2,1)S(1)} collective-permute-done((bf16[176,2048]{1,0:T(8,128)(2,1)S(1)}, bf16[176,2048]{1,0:T(8,128)(2,1)S(1)}, u32[]{:S(2)}, u32[]{:S(2)}) %collective-permute-start.38) | collective-permute-done | bytes 720928 | tf_op jit(solution)/shard_map/ppermute | solution.py:118
  739.4 4.2 all-to-all-start.10
  753.1 4.9 all-to-all-start.11
  764.0 4.6 collective-permute-done.39
  776.8 5.6 all-to-all-done.11
  793.3 15.0 %collective-permute-start.43 = (bf16[2,176,2048]{2,1,0:T(8,128)(2,1)}, bf16[2,176,2048]{2,1,0:T(8,128)(2,1)S(1)}, u32[]{:S(2)}, u32[]{:S(2)}) collective-permute-start(bf16[2,176,2048]{2,1,0:T(8,128)(2,1)} %collective-permute-done.40), channel_id=1, source_target_pairs={{0,8},{1,9},{2,10},{3,11},{4,12},{5,13},{6,14},{7,15},{8,0},{9,1},... | collective-permute-start | bytes 4325384 | tf_op jit(solution)/shard_map/ppermute | solution.py:97
  816.2 6.0 convolution_convert_fusion.4
  825.8 9.8 fusion.83
  835.6 6.4 shard_map.230
  848.3 6.5 convert_reduce_fusion
  854.8 4.7 convert_reduce_fusion.1
  859.6 4.6 multiply_reduce_fusion
  889.8 4.7 fusion.132
  896.5 5.4 convolution_convert_fusion.3
  904.6 3.9 collective-permute-start.53
  920.0 7.5 collective-permute-done.55
  928.6 5.2 collective-permute-done.50
  943.2 5.9 all-to-all-start.8
  950.5 20.5 %all-to-all-done.8 = bf16[4,128,320]{1,2,0:T(8,128)(2,1)S(1)} async-done(((bf16[4,128,320]{1,2,0:T(8,128)(2,1)}), bf16[4,128,320]{1,2,0:T(8,128)(2,1)S(1)}, u32[]{:S(2)}, u32[]{:S(2)}) %all-to-all-start.8) | async-done | bytes 327712 | tf_op jit(solution)/shard_map/all_to_all | solution.py:69
  981.3 4.8 fusion.73
  990.5 117.4 %all-reduce.6.cloned.1.call-done = f32[24576]{0:T(1024)} async-done(((f32[24576]{0:T(1024)}), f32[24576]{0:T(1024)}) %all-reduce.6.cloned.1.call-update) | async-done | bytes 98320 | tf_op jit(solution)/shard_map/psum | solution.py:435
  (569 shorter events, 322.1 us)
Async XLA Ops:
  9.1 75.3 %collective-permute-start = (bf16[176,2048]{1,0:T(8,128)(2,1)S(1)}, bf16[176,2048]{1,0:T(8,128)(2,1)S(1)}, u32[]{:S(2)}, u32[]{:S(2)}) collective-permute-start(bf16[176,2048]{1,0:T(8,128)(2,1)S(1)} %get-tuple-element.93), channel_id=1, source_target_pairs={{0,1},{1,0},{2,3},{3,2},{4,5},{5,4},{6,7},{7,6},{8,10},{9,11},{10,... | collective-permute-start | bytes 2162696 | tf_op jit(solution)/shard_map/ppermute | solution.py:95
  11.2 130.2 %collective-permute-start.2 = (bf16[176,2048]{1,0:T(8,128)(2,1)S(1)}, bf16[176,2048]{1,0:T(8,128)(2,1)}, u32[]{:S(2)}, u32[]{:S(2)}) collective-permute-start(bf16[176,2048]{1,0:T(8,128)(2,1)S(1)} %get-tuple-element.93), channel_id=1, source_target_pairs={{0,8},{1,9},{2,10},{3,11},{4,12},{5,13},{6,14},{7,15},{8,0},{9,1},... | collective-permute-start | bytes 2162696 | tf_op jit(solution)/shard_map/ppermute | solution.py:97
  14.3 46.9 %all-to-all-start.1 = ((bf16[4,2,2,1600]{3,2,1,0:T(2,128)(2,1)}), bf16[4,2,2,1600]{3,2,1,0:T(2,128)(2,1)S(1)}, u32[]{:S(2)}, u32[]{:S(2)}) async-start(bf16[4,2,2,1600]{3,2,1,0:T(2,128)(2,1)} %maximum_bitcast_fusion.10), calls=%async_computation.1 | async-start | bytes 106496 | tf_op jit(solution)/shard_map/all_to_all | solution.py:277
  61.3 17.1 %all-to-all-start.2 = ((bf16[4,128,320]{1,2,0:T(8,128)(2,1)}), bf16[4,128,320]{1,2,0:T(8,128)(2,1)}, u32[]{:S(2)}, u32[]{:S(2)}) async-start(bf16[4,128,320]{1,2,0:T(8,128)(2,1)} %bitcast.475), calls=%async_computation.2 | async-start | bytes 655360 | tf_op jit(solution)/shard_map/all_to_all | solution.py:55
  78.4 14.7 %all-to-all-start = ((bf16[4,128,640]{1,2,0:T(8,128)(2,1)}), bf16[4,128,640]{1,2,0:T(8,128)(2,1)S(1)}, u32[]{:S(2)}, u32[]{:S(2)}) async-start(bf16[4,128,640]{1,2,0:T(8,128)(2,1)} %maximum_bitcast_fusion.4), calls=%async_computation | async-start | bytes 1310720 | tf_op jit(solution)/shard_map/all_to_all | solution.py:55
  85.6 39.3 %collective-permute-start.1 = (bf16[2,176,2048]{2,1,0:T(8,128)(2,1)}, bf16[2,176,2048]{2,1,0:T(8,128)(2,1)}, u32[]{:S(2)}, u32[]{:S(2)}) collective-permute-start(bf16[2,176,2048]{2,1,0:T(8,128)(2,1)} %pad_maximum_fusion.13), channel_id=1, source_target_pairs={{0,2},{1,3},{2,0},{3,1},{4,6},{5,7},{6,4},{7,5},{8,9},{9,8},{10,11... | collective-permute-start | bytes 4325384 | tf_op jit(solution)/shard_map/ppermute | solution.py:96
  88.5 14.4 %collective-permute-start.11 = (bf16[2,2,128,320]{2,1,0,3:T(2,128)(2,1)S(1)}, bf16[2,2,128,320]{2,1,0,3:T(2,128)(2,1)}, u32[]{:S(2)}, u32[]{:S(2)}) collective-permute-start(bf16[2,2,128,320]{2,1,0,3:T(2,128)(2,1)S(1)} %bitcast.468), channel_id=1, source_target_pairs={{0,4},{4,0},{1,5},{5,1},{2,6},{6,2},{3,7},{7,3},{8,12},{12,8},{9,1... | collective-permute-start | bytes 983048 | tf_op jit(solution)/shard_map/ppermute | solution.py:31
  91.6 51.9 %collective-permute-start.3 = (bf16[176,2048]{1,0:T(8,128)(2,1)S(1)}, bf16[176,2048]{1,0:T(8,128)(2,1)}, u32[]{:S(2)}, u32[]{:S(2)}) collective-permute-start(bf16[176,2048]{1,0:T(8,128)(2,1)S(1)} %collective-permute-done), channel_id=1, source_target_pairs={{0,8},{1,9},{2,10},{3,11},{4,12},{5,13},{6,14},{7,15},{8,0},{9,1},... | collective-permute-start | bytes 2162696 | tf_op jit(solution)/shard_map/ppermute | solution.py:97
  93.0 141.8 %all-to-all-start.3 = ((bf16[4,128,768]{2,1,0:T(8,128)(2,1)}), bf16[4,128,768]{2,1,0:T(8,128)(2,1)}, u32[]{:S(2)}, u32[]{:S(2)}) async-start(bf16[4,128,768]{2,1,0:T(8,128)(2,1)} %maximum_bitcast_fusion.2), calls=%async_computation.3 | async-start | bytes 1572864 | tf_op jit(solution)/shard_map/all_to_all | solution.py:55
  101.1 23.2 %collective-permute-start.5 = (bf16[2,2,128,640]{3,2,1,0:T(8,128)(2,1)S(1)}, bf16[2,2,128,640]{3,2,1,0:T(8,128)(2,1)S(1)}, u32[]{:S(2)}, u32[]{:S(2)}) collective-permute-start(bf16[2,2,128,640]{3,2,1,0:T(8,128)(2,1)S(1)} %copy.152), channel_id=1, source_target_pairs={{0,4},{4,0},{1,5},{5,1},{2,6},{6,2},{3,7},{7,3},{8,12},{12,8},{9,1... | collective-permute-start | bytes 1966088 | tf_op jit(solution)/shard_map/ppermute | solution.py:31
  106.2 67.8 %collective-permute-start.12 = (bf16[2,2,2,128,320]{3,2,1,0,4:T(2,128)(2,1)}, bf16[2,2,2,128,320]{3,2,1,0,4:T(2,128)(2,1)}, u32[]{:S(2)}, u32[]{:S(2)}) collective-permute-start(bf16[2,2,2,128,320]{3,2,1,0,4:T(2,128)(2,1)} %pad_maximum_fusion.31), channel_id=1, source_target_pairs={{0,16},{16,0},{1,17},{17,1},{2,18},{18,2},{3,19},{19,3},{4,20},{20... | collective-permute-start | bytes 1966088 | tf_op jit(solution)/shard_map/ppermute | solution.py:31
  124.6 26.2 %collective-permute-start.6 = (bf16[2,2,2,128,640]{4,3,2,1,0:T(8,128)(2,1)S(1)}, bf16[2,2,2,128,640]{4,3,2,1,0:T(8,128)(2,1)S(1)}, u32[]{:S(2)}, u32[]{:S(2)}) collective-permute-start(bf16[2,2,2,128,640]{4,3,2,1,0:T(8,128)(2,1)S(1)} %pad_maximum_fusion.25), channel_id=1, source_target_pairs={{0,16},{16,0},{1,17},{17,1},{2,18},{18,2},{3,19},{19,3},{4,20},{20... | collective-permute-start | bytes 3932168 | tf_op jit(solution)/shard_map/ppermute | solution.py:31
  124.9 26.5 %collective-permute-start.4 = (bf16[2,176,2048]{2,1,0:T(8,128)(2,1)}, bf16[2,176,2048]{2,1,0:T(8,128)(2,1)S(1)}, u32[]{:S(2)}, u32[]{:S(2)}) collective-permute-start(bf16[2,176,2048]{2,1,0:T(8,128)(2,1)} %collective-permute-done.1), channel_id=1, source_target_pairs={{0,8},{1,9},{2,10},{3,11},{4,12},{5,13},{6,14},{7,15},{8,0},{9,1},... | collective-permute-start | bytes 4325384 | tf_op jit(solution)/shard_map/ppermute | solution.py:97
  220.2 48.1 %collective-permute-start.13 = (bf16[4,176,2048]{2,1,0:T(8,128)(2,1)}, bf16[4,176,2048]{2,1,0:T(8,128)(2,1)}, u32[]{:S(2)}, u32[]{:S(2)}) collective-permute-start(bf16[4,176,2048]{2,1,0:T(8,128)(2,1)} %fusion.3), channel_id=1, source_target_pairs={{0,8},{1,9},{2,10},{3,11},{4,12},{5,13},{6,14},{7,15},{8,0},{9,1},... | collective-permute-start | bytes 8650760 | tf_op jit(solution)/shard_map/ppermute | solution.py:112
  234.8 17.1 %all-to-all-start.5 = ((bf16[4,128,768]{2,1,0:T(8,128)(2,1)}), bf16[4,128,768]{2,1,0:T(8,128)(2,1)S(1)}, u32[]{:S(2)}, u32[]{:S(2)}) async-start(bf16[4,128,768]{2,1,0:T(8,128)(2,1)} %bitcast.443), calls=%async_computation.5 | async-start | bytes 1572864 | tf_op jit(solution)/shard_map/all_to_all | solution.py:55
  243.9 18.0 %collective-permute-start.31 = (bf16[176,2048]{1,0:T(8,128)(2,1)}, bf16[176,2048]{1,0:T(8,128)(2,1)}, u32[]{:S(2)}, u32[]{:S(2)}) collective-permute-start(bf16[176,2048]{1,0:T(8,128)(2,1)} %bitcast_convert_fusion), channel_id=1, source_target_pairs={{0,1},{1,0},{2,3},{3,2},{4,5},{5,4},{6,7},{7,6},{8,10},{9,11},{10,... | collective-permute-start | bytes 2162696 | tf_op jit(solution)/shard_map/ppermute | solution.py:95
  252.0 16.3 %all-to-all-start.4 = ((bf16[4,128,768]{2,1,0:T(8,128)(2,1)}), bf16[4,128,768]{2,1,0:T(8,128)(2,1)}, u32[]{:S(2)}, u32[]{:S(2)}) async-start(bf16[4,128,768]{2,1,0:T(8,128)(2,1)} %maximum_bitcast_fusion.3), calls=%async_computation.4 | async-start | bytes 1572864 | tf_op jit(solution)/shard_map/all_to_all | solution.py:55
  256.9 119.7 %collective-permute-start.33 = (bf16[176,2048]{1,0:T(8,128)(2,1)}, bf16[176,2048]{1,0:T(8,128)(2,1)}, u32[]{:S(2)}, u32[]{:S(2)}) collective-permute-start(bf16[176,2048]{1,0:T(8,128)(2,1)} %bitcast_convert_fusion), channel_id=1, source_target_pairs={{0,8},{1,9},{2,10},{3,11},{4,12},{5,13},{6,14},{7,15},{8,0},{9,1},... | collective-permute-start | bytes 2162696 | tf_op jit(solution)/shard_map/ppermute | solution.py:97
  263.1 107.8 %collective-permute-start.32 = (bf16[2,176,2048]{2,1,0:T(8,128)(2,1)S(1)}, bf16[2,176,2048]{2,1,0:T(8,128)(2,1)}, u32[]{:S(2)}, u32[]{:S(2)}) collective-permute-start(bf16[2,176,2048]{2,1,0:T(8,128)(2,1)S(1)} %pad_maximum_fusion.17), channel_id=1, source_target_pairs={{0,2},{1,3},{2,0},{3,1},{4,6},{5,7},{6,4},{7,5},{8,9},{9,8},{10,11... | collective-permute-start | bytes 4325384 | tf_op jit(solution)/shard_map/ppermute | solution.py:96
  265.9 69.7 %collective-permute-start.21 = (bf16[2,2,128,768]{3,2,1,0:T(8,128)(2,1)}, bf16[2,2,128,768]{3,2,1,0:T(8,128)(2,1)}, u32[]{:S(2)}, u32[]{:S(2)}) collective-permute-start(bf16[2,2,128,768]{3,2,1,0:T(8,128)(2,1)} %bitcast.59), channel_id=1, source_target_pairs={{0,4},{4,0},{1,5},{5,1},{2,6},{6,2},{3,7},{7,3},{8,12},{12,8},{9,1... | collective-permute-start | bytes 2359304 | tf_op jit(solution)/shard_map/ppermute | solution.py:31
  265.9 86.5 %collective-permute-start.25 = (bf16[2,2,128,768]{3,2,1,0:T(8,128)(2,1)S(1)}, bf16[2,2,128,768]{3,2,1,0:T(8,128)(2,1)}, u32[]{:S(2)}, u32[]{:S(2)}) collective-permute-start(bf16[2,2,128,768]{3,2,1,0:T(8,128)(2,1)S(1)} %bitcast.434), channel_id=1, source_target_pairs={{0,4},{4,0},{1,5},{5,1},{2,6},{6,2},{3,7},{7,3},{8,12},{12,8},{9,1... | collective-permute-start | bytes 2359304 | tf_op jit(solution)/shard_map/ppermute | solution.py:31
  268.2 100.9 %collective-permute-start.23 = (bf16[2,2,128,768]{3,2,1,0:T(8,128)(2,1)}, bf16[2,2,128,768]{3,2,1,0:T(8,128)(2,1)S(1)}, u32[]{:S(2)}, u32[]{:S(2)}) collective-permute-start(bf16[2,2,128,768]{3,2,1,0:T(8,128)(2,1)} %bitcast.68), channel_id=1, source_target_pairs={{0,4},{4,0},{1,5},{5,1},{2,6},{6,2},{3,7},{7,3},{8,12},{12,8},{9,1... | collective-permute-start | bytes 2359304 | tf_op jit(solution)/shard_map/ppermute | solution.py:31
  335.5 71.9 %collective-permute-start.34 = (bf16[176,2048]{1,0:T(8,128)(2,1)}, bf16[176,2048]{1,0:T(8,128)(2,1)S(1)}, u32[]{:S(2)}, u32[]{:S(2)}) collective-permute-start(bf16[176,2048]{1,0:T(8,128)(2,1)} %collective-permute-done.31), channel_id=1, source_target_pairs={{0,8},{1,9},{2,10},{3,11},{4,12},{5,13},{6,14},{7,15},{8,0},{9,1},... | collective-permute-start | bytes 2162696 | tf_op jit(solution)/shard_map/ppermute | solution.py:97
  352.4 21.9 %collective-permute-start.14 = (bf16[2,176,2048]{2,1,0:T(8,128)(2,1)S(1)}, bf16[2,176,2048]{2,1,0:T(8,128)(2,1)S(1)}, u32[]{:S(2)}, u32[]{:S(2)}) collective-permute-start(bf16[2,176,2048]{2,1,0:T(8,128)(2,1)S(1)} %pad_maximum_fusion.14), channel_id=1, source_target_pairs={{0,2},{1,3},{2,0},{3,1},{4,6},{5,7},{6,4},{7,5},{8,9},{9,8},{10,11... | collective-permute-start | bytes 4325384 | tf_op jit(solution)/shard_map/ppermute | solution.py:115
  369.2 69.4 %collective-permute-start.22 = (bf16[2,2,2,128,768]{4,3,2,1,0:T(8,128)(2,1)S(1)}, bf16[2,2,2,128,768]{4,3,2,1,0:T(8,128)(2,1)S(1)}, u32[]{:S(2)}, u32[]{:S(2)}) collective-permute-start(bf16[2,2,2,128,768]{4,3,2,1,0:T(8,128)(2,1)S(1)} %pad_maximum_fusion.10), channel_id=1, source_target_pairs={{0,16},{16,0},{1,17},{17,1},{2,18},{18,2},{3,19},{19,3},{4,20},{20... | collective-permute-start | bytes 4718600 | tf_op jit(solution)/shard_map/ppermute | solution.py:31
  371.0 65.6 %collective-permute-start.24 = (bf16[2,2,2,128,768]{4,3,2,0,1:T(8,128)(2,1)S(1)}, bf16[2,2,2,128,768]{4,3,2,0,1:T(8,128)(2,1)S(1)}, u32[]{:S(2)}, u32[]{:S(2)}) collective-permute-start(bf16[2,2,2,128,768]{4,3,2,0,1:T(8,128)(2,1)S(1)} %pad_maximum_fusion.11), channel_id=1, source_target_pairs={{0,16},{16,0},{1,17},{17,1},{2,18},{18,2},{3,19},{19,3},{4,20},{20... | collective-permute-start | bytes 4718600 | tf_op jit(solution)/shard_map/ppermute | solution.py:31
  374.5 18.3 %collective-permute-start.15 = (bf16[176,2048]{1,0:T(8,128)(2,1)S(1)}, bf16[176,2048]{1,0:T(8,128)(2,1)S(1)}, u32[]{:S(2)}, u32[]{:S(2)}) collective-permute-start(bf16[176,2048]{1,0:T(8,128)(2,1)S(1)} %fusion.88), channel_id=1, source_target_pairs={{0,1},{1,0},{2,3},{3,2},{4,5},{5,4},{6,7},{7,6},{8,10},{9,11},{10,... | collective-permute-start | bytes 2162696 | tf_op jit(solution)/shard_map/ppermute | solution.py:118
  376.6 93.7 %collective-permute-start.26 = (bf16[2,2,2,128,768]{4,3,2,1,0:T(8,128)(2,1)S(1)}, bf16[2,2,2,128,768]{4,3,2,1,0:T(8,128)(2,1)S(1)}, u32[]{:S(2)}, u32[]{:S(2)}) collective-permute-start(bf16[2,2,2,128,768]{4,3,2,1,0:T(8,128)(2,1)S(1)} %pad_maximum_fusion.12), channel_id=1, source_target_pairs={{0,16},{16,0},{1,17},{17,1},{2,18},{18,2},{3,19},{19,3},{4,20},{20... | collective-permute-start | bytes 4718600 | tf_op jit(solution)/shard_map/ppermute | solution.py:31
  392.8 84.1 %collective-permute-start.35 = (bf16[2,176,2048]{2,1,0:T(8,128)(2,1)}, bf16[2,176,2048]{2,1,0:T(8,128)(2,1)S(1)}, u32[]{:S(2)}, u32[]{:S(2)}) collective-permute-start(bf16[2,176,2048]{2,1,0:T(8,128)(2,1)} %collective-permute-done.32), channel_id=1, source_target_pairs={{0,8},{1,9},{2,10},{3,11},{4,12},{5,13},{6,14},{7,15},{8,0},{9,1},... | collective-permute-start | bytes 4325384 | tf_op jit(solution)/shard_map/ppermute | solution.py:97
  407.5 29.9 %collective-permute-start.16 = (bf16[176,2048]{1,0:T(8,128)(2,1)S(1)}, bf16[176,2048]{1,0:T(8,128)(2,1)S(1)}, u32[]{:S(2)}, u32[]{:S(2)}) collective-permute-start(bf16[176,2048]{1,0:T(8,128)(2,1)S(1)} %get-tuple-element.100), channel_id=1, source_target_pairs={{0,1},{1,0},{2,3},{3,2},{4,5},{5,4},{6,7},{7,6},{8,10},{9,11},{10,... | collective-permute-start | bytes 2162696 | tf_op jit(solution)/shard_map/ppermute | solution.py:95
  437.5 36.6 %collective-permute-start.17 = (bf16[2,176,2048]{2,1,0:T(8,128)(2,1)S(1)}, bf16[2,176,2048]{2,1,0:T(8,128)(2,1)S(1)}, u32[]{:S(2)}, u32[]{:S(2)}) collective-permute-start(bf16[2,176,2048]{2,1,0:T(8,128)(2,1)S(1)} %pad_maximum_fusion.15), channel_id=1, source_target_pairs={{0,2},{1,3},{2,0},{3,1},{4,6},{5,7},{6,4},{7,5},{8,9},{9,8},{10,11... | collective-permute-start | bytes 4325384 | tf_op jit(solution)/shard_map/ppermute | solution.py:96
  537.4 86.1 %collective-permute-start.36 = (bf16[4,176,2048]{2,1,0:T(8,128)(2,1)}, bf16[4,176,2048]{2,1,0:T(8,128)(2,1)}, u32[]{:S(2)}, u32[]{:S(2)}) collective-permute-start(bf16[4,176,2048]{2,1,0:T(8,128)(2,1)} %fusion.5), channel_id=1, source_target_pairs={{0,8},{1,9},{2,10},{3,11},{4,12},{5,13},{6,14},{7,15},{8,0},{9,1},... | collective-permute-start | bytes 8650760 | tf_op jit(solution)/shard_map/ppermute | solution.py:112
  550.2 108.2 %collective-permute-start.60 = (bf16[2,2,2,128,768]{4,3,2,1,0:T(8,128)(2,1)}, bf16[2,2,2,128,768]{4,3,2,1,0:T(8,128)(2,1)S(1)}, u32[]{:S(2)}, u32[]{:S(2)}) collective-permute-start(bf16[2,2,2,128,768]{4,3,2,1,0:T(8,128)(2,1)} %dynamic-slice_bitcast_fusion), channel_id=1, source_target_pairs={{0,16},{16,0},{1,17},{17,1},{2,18},{18,2},{3,19},{19,3},{4,20},{20... | collective-permute-start | bytes 4718600 | tf_op jit(solution)/shard_map/ppermute | solution.py:45
  553.8 66.0 %collective-permute-start.56 = (bf16[2,2,2,128,768]{4,3,2,1,0:T(8,128)(2,1)}, bf16[2,2,2,128,768]{4,3,2,1,0:T(8,128)(2,1)}, u32[]{:S(2)}, u32[]{:S(2)}) collective-permute-start(bf16[2,2,2,128,768]{4,3,2,1,0:T(8,128)(2,1)} %dynamic-slice_bitcast_fusion.2), channel_id=1, source_target_pairs={{0,16},{16,0},{1,17},{17,1},{2,18},{18,2},{3,19},{19,3},{4,20},{20... | collective-permute-start | bytes 4718600 | tf_op jit(solution)/shard_map/ppermute | solution.py:45
  555.3 98.2 %collective-permute-start.58 = (bf16[2,2,2,128,768]{4,3,2,1,0:T(8,128)(2,1)}, bf16[2,2,2,128,768]{4,3,2,1,0:T(8,128)(2,1)}, u32[]{:S(2)}, u32[]{:S(2)}) collective-permute-start(bf16[2,2,2,128,768]{4,3,2,1,0:T(8,128)(2,1)} %dynamic-slice_bitcast_fusion.1), channel_id=1, source_target_pairs={{0,16},{16,0},{1,17},{17,1},{2,18},{18,2},{3,19},{19,3},{4,20},{20... | collective-permute-start | bytes 4718600 | tf_op jit(solution)/shard_map/ppermute | solution.py:45
  571.7 144.8 %collective-permute-start.27 = (bf16[4,176,2048]{2,1,0:T(8,128)(2,1)}, bf16[4,176,2048]{2,1,0:T(8,128)(2,1)}, u32[]{:S(2)}, u32[]{:S(2)}) collective-permute-start(bf16[4,176,2048]{2,1,0:T(8,128)(2,1)} %fusion.4), channel_id=1, source_target_pairs={{0,8},{1,9},{2,10},{3,11},{4,12},{5,13},{6,14},{7,15},{8,0},{9,1},... | collective-permute-start | bytes 8650760 | tf_op jit(solution)/shard_map/ppermute | solution.py:112
  622.6 42.8 %collective-permute-start.57 = (bf16[2,2,128,768]{3,2,1,0:T(8,128)(2,1)}, bf16[2,2,128,768]{3,2,1,0:T(8,128)(2,1)}, u32[]{:S(2)}, u32[]{:S(2)}) collective-permute-start(bf16[2,2,128,768]{3,2,1,0:T(8,128)(2,1)} %fusion.85), channel_id=1, source_target_pairs={{0,4},{4,0},{1,5},{5,1},{2,6},{6,2},{3,7},{7,3},{8,12},{12,8},{9,1... | collective-permute-start | bytes 2359304 | tf_op jit(solution)/shard_map/ppermute | solution.py:45
  631.8 83.0 %collective-permute-start.37 = (bf16[2,176,2048]{2,1,0:T(8,128)(2,1)}, bf16[2,176,2048]{2,1,0:T(8,128)(2,1)}, u32[]{:S(2)}, u32[]{:S(2)}) collective-permute-start(bf16[2,176,2048]{2,1,0:T(8,128)(2,1)} %pad_maximum_fusion.18), channel_id=1, source_target_pairs={{0,2},{1,3},{2,0},{3,1},{4,6},{5,7},{6,4},{7,5},{8,9},{9,8},{10,11... | collective-permute-start | bytes 4325384 | tf_op jit(solution)/shard_map/ppermute | solution.py:115
  657.9 53.9 %collective-permute-start.59 = (bf16[2,2,128,768]{3,2,1,0:T(8,128)(2,1)}, bf16[2,2,128,768]{3,2,1,0:T(8,128)(2,1)}, u32[]{:S(2)}, u32[]{:S(2)}) collective-permute-start(bf16[2,2,128,768]{3,2,1,0:T(8,128)(2,1)} %fusion.86), channel_id=1, source_target_pairs={{0,4},{4,0},{1,5},{5,1},{2,6},{6,2},{3,7},{7,3},{8,12},{12,8},{9,1... | collective-permute-start | bytes 2359304 | tf_op jit(solution)/shard_map/ppermute | solution.py:45
  663.1 86.2 %collective-permute-start.61 = (bf16[2,2,128,768]{3,2,1,0:T(8,128)(2,1)}, bf16[2,2,128,768]{3,2,1,0:T(8,128)(2,1)}, u32[]{:S(2)}, u32[]{:S(2)}) collective-permute-start(bf16[2,2,128,768]{3,2,1,0:T(8,128)(2,1)} %fusion.87), channel_id=1, source_target_pairs={{0,4},{4,0},{1,5},{5,1},{2,6},{6,2},{3,7},{7,3},{8,12},{12,8},{9,1... | collective-permute-start | bytes 2359304 | tf_op jit(solution)/shard_map/ppermute | solution.py:45
  667.9 71.5 %all-to-all-start.9 = ((bf16[4,128,768]{1,2,0:T(8,128)(2,1)}), bf16[4,128,768]{1,2,0:T(8,128)(2,1)}, u32[]{:S(2)}, u32[]{:S(2)}) async-start(bf16[4,128,768]{1,2,0:T(8,128)(2,1)} %bitcast.164), calls=%async_computation.9 | async-start | bytes 1572864 | tf_op jit(solution)/shard_map/all_to_all | solution.py:69
  716.4 20.1 %collective-permute-start.38 = (bf16[176,2048]{1,0:T(8,128)(2,1)S(1)}, bf16[176,2048]{1,0:T(8,128)(2,1)S(1)}, u32[]{:S(2)}, u32[]{:S(2)}) collective-permute-start(bf16[176,2048]{1,0:T(8,128)(2,1)S(1)} %fusion.91), channel_id=1, source_target_pairs={{0,1},{1,0},{2,3},{3,2},{4,5},{5,4},{6,7},{7,6},{8,10},{9,11},{10,... | collective-permute-start | bytes 2162696 | tf_op jit(solution)/shard_map/ppermute | solution.py:118
  747.1 21.5 %collective-permute-start.39 = (bf16[176,2048]{1,0:T(8,128)(2,1)}, bf16[176,2048]{1,0:T(8,128)(2,1)}, u32[]{:S(2)}, u32[]{:S(2)}) collective-permute-start(bf16[176,2048]{1,0:T(8,128)(2,1)} %get-tuple-element.95), channel_id=1, source_target_pairs={{0,1},{1,0},{2,3},{3,2},{4,5},{5,4},{6,7},{7,6},{8,10},{9,11},{10,... | collective-permute-start | bytes 2162696 | tf_op jit(solution)/shard_map/ppermute | solution.py:95
  748.4 36.3 %collective-permute-start.28 = (bf16[2,176,2048]{2,1,0:T(8,128)(2,1)}, bf16[2,176,2048]{2,1,0:T(8,128)(2,1)}, u32[]{:S(2)}, u32[]{:S(2)}) collective-permute-start(bf16[2,176,2048]{2,1,0:T(8,128)(2,1)} %pad_maximum_fusion.16), channel_id=1, source_target_pairs={{0,2},{1,3},{2,0},{3,1},{4,6},{5,7},{6,4},{7,5},{8,9},{9,8},{10,11... | collective-permute-start | bytes 4325384 | tf_op jit(solution)/shard_map/ppermute | solution.py:115
  753.1 29.2 %all-to-all-start.11 = ((bf16[4,128,768]{1,2,0:T(8,128)(2,1)}), bf16[4,128,768]{1,2,0:T(8,128)(2,1)}, u32[]{:S(2)}, u32[]{:S(2)}) async-start(bf16[4,128,768]{1,2,0:T(8,128)(2,1)} %copy.192), calls=%async_computation.11 | async-start | bytes 1572864 | tf_op jit(solution)/shard_map/all_to_all | solution.py:69
  771.1 22.2 %collective-permute-start.40 = (bf16[2,176,2048]{2,1,0:T(8,128)(2,1)}, bf16[2,176,2048]{2,1,0:T(8,128)(2,1)}, u32[]{:S(2)}, u32[]{:S(2)}) collective-permute-start(bf16[2,176,2048]{2,1,0:T(8,128)(2,1)} %pad_maximum_fusion.19), channel_id=1, source_target_pairs={{0,2},{1,3},{2,0},{3,1},{4,6},{5,7},{6,4},{7,5},{8,9},{9,8},{10,11... | collective-permute-start | bytes 4325384 | tf_op jit(solution)/shard_map/ppermute | solution.py:96
  787.3 193.4 %collective-permute-start.29 = (bf16[176,2048]{1,0:T(8,128)(2,1)}, bf16[176,2048]{1,0:T(8,128)(2,1)}, u32[]{:S(2)}, u32[]{:S(2)}) collective-permute-start(bf16[176,2048]{1,0:T(8,128)(2,1)} %fusion.89), channel_id=1, source_target_pairs={{0,1},{1,0},{2,3},{3,2},{4,5},{5,4},{6,7},{7,6},{8,10},{9,11},{10,... | collective-permute-start | bytes 2162696 | tf_op jit(solution)/shard_map/ppermute | solution.py:118
  789.1 23.3 %collective-permute-start.41 = (bf16[176,2048]{1,0:T(8,128)(2,1)}, bf16[176,2048]{1,0:T(8,128)(2,1)S(1)}, u32[]{:S(2)}, u32[]{:S(2)}) collective-permute-start(bf16[176,2048]{1,0:T(8,128)(2,1)} %get-tuple-element.95), channel_id=1, source_target_pairs={{0,8},{1,9},{2,10},{3,11},{4,12},{5,13},{6,14},{7,15},{8,0},{9,1},... | collective-permute-start | bytes 2162696 | tf_op jit(solution)/shard_map/ppermute | solution.py:97
  791.2 22.1 %collective-permute-start.42 = (bf16[176,2048]{1,0:T(8,128)(2,1)}, bf16[176,2048]{1,0:T(8,128)(2,1)S(1)}, u32[]{:S(2)}, u32[]{:S(2)}) collective-permute-start(bf16[176,2048]{1,0:T(8,128)(2,1)} %collective-permute-done.39), channel_id=1, source_target_pairs={{0,8},{1,9},{2,10},{3,11},{4,12},{5,13},{6,14},{7,15},{8,0},{9,1},... | collective-permute-start | bytes 2162696 | tf_op jit(solution)/shard_map/ppermute | solution.py:97
  793.3 20.9 %collective-permute-start.43 = (bf16[2,176,2048]{2,1,0:T(8,128)(2,1)}, bf16[2,176,2048]{2,1,0:T(8,128)(2,1)S(1)}, u32[]{:S(2)}, u32[]{:S(2)}) collective-permute-start(bf16[2,176,2048]{2,1,0:T(8,128)(2,1)} %collective-permute-done.40), channel_id=1, source_target_pairs={{0,8},{1,9},{2,10},{3,11},{4,12},{5,13},{6,14},{7,15},{8,0},{9,1},... | collective-permute-start | bytes 4325384 | tf_op jit(solution)/shard_map/ppermute | solution.py:97
  845.5 63.0 %collective-permute-start.54 = (bf16[2,2,2,128,320]{3,2,1,0,4:T(2,128)(2,1)}, bf16[2,2,2,128,320]{3,2,1,0,4:T(2,128)(2,1)}, u32[]{:S(2)}, u32[]{:S(2)}) collective-permute-start(bf16[2,2,2,128,320]{3,2,1,0,4:T(2,128)(2,1)} %dynamic-slice_bitcast_fusion.4), channel_id=1, source_target_pairs={{0,16},{16,0},{1,17},{17,1},{2,18},{18,2},{3,19},{19,3},{4,20},{20... | collective-permute-start | bytes 1966088 | tf_op jit(solution)/shard_map/ppermute | solution.py:45
  871.9 14.6 %collective-permute-start.45 = (f32[4,3,320]{2,1,0:T(4,128)}, f32[4,3,320]{2,1,0:T(4,128)}, u32[]{:S(2)}, u32[]{:S(2)}) collective-permute-start(f32[4,3,320]{2,1,0:T(4,128)} %slice.423), channel_id=1, source_target_pairs={{4,0},{5,1},{6,2},{7,3},{12,8},{13,9},{14,10},{15,11},{20,16},{21,... | collective-permute-start | bytes 46088 | tf_op jit(solution)/shard_map/ppermute | solution.py:189
  886.2 18.2 %collective-permute-start.52 = (bf16[2,2,2,6400]{3,2,1,0:T(2,128)(2,1)}, bf16[2,2,2,6400]{3,2,1,0:T(2,128)(2,1)S(1)}, u32[]{:S(2)}, u32[]{:S(2)}) collective-permute-start(bf16[2,2,2,6400]{3,2,1,0:T(2,128)(2,1)} %fusion.103), channel_id=1, source_target_pairs={{0,16},{16,0},{1,17},{17,1},{2,18},{18,2},{3,19},{19,3},{4,20},{20... | collective-permute-start | bytes 307208 | tf_op jit(solution)/shard_map/ppermute | solution.py:45
  895.0 15.6 %collective-permute-start.46 = (bf16[4,176,2048]{2,1,0:T(8,128)(2,1)S(1)}, bf16[4,176,2048]{2,1,0:T(8,128)(2,1)S(1)}, u32[]{:S(2)}, u32[]{:S(2)}) collective-permute-start(bf16[4,176,2048]{2,1,0:T(8,128)(2,1)S(1)} %fusion.6), channel_id=1, source_target_pairs={{0,8},{1,9},{2,10},{3,11},{4,12},{5,13},{6,14},{7,15},{8,0},{9,1},... | collective-permute-start | bytes 8650760 | tf_op jit(solution)/shard_map/ppermute | solution.py:112
  903.2 30.7 %collective-permute-start.50 = (bf16[2,2,2,128,640]{4,3,2,1,0:T(8,128)(2,1)}, bf16[2,2,2,128,640]{4,3,2,1,0:T(8,128)(2,1)}, u32[]{:S(2)}, u32[]{:S(2)}) collective-permute-start(bf16[2,2,2,128,640]{4,3,2,1,0:T(8,128)(2,1)} %dynamic-slice_bitcast_fusion.3), channel_id=1, source_target_pairs={{0,16},{16,0},{1,17},{17,1},{2,18},{18,2},{3,19},{19,3},{4,20},{20... | collective-permute-start | bytes 3932168 | tf_op jit(solution)/shard_map/ppermute | solution.py:45
  910.5 17.0 %collective-permute-start.55 = (bf16[2,2,128,320]{2,1,0,3:T(2,128)(2,1)S(1)}, bf16[2,2,128,320]{2,1,0,3:T(2,128)(2,1)S(1)}, u32[]{:S(2)}, u32[]{:S(2)}) collective-permute-start(bf16[2,2,128,320]{2,1,0,3:T(2,128)(2,1)S(1)} %fusion.99), channel_id=1, source_target_pairs={{0,4},{4,0},{1,5},{5,1},{2,6},{6,2},{3,7},{7,3},{8,12},{12,8},{9,1... | collective-permute-start | bytes 983048 | tf_op jit(solution)/shard_map/ppermute | solution.py:45
  914.8 25.8 %collective-permute-start.47 = (bf16[2,176,2048]{2,1,0:T(8,128)(2,1)}, bf16[2,176,2048]{2,1,0:T(8,128)(2,1)}, u32[]{:S(2)}, u32[]{:S(2)}) collective-permute-start(bf16[2,176,2048]{2,1,0:T(8,128)(2,1)} %pad_maximum_fusion.20), channel_id=1, source_target_pairs={{0,2},{1,3},{2,0},{3,1},{4,6},{5,7},{6,4},{7,5},{8,9},{9,8},{10,11... | collective-permute-start | bytes 4325384 | tf_op jit(solution)/shard_map/ppermute | solution.py:115
  916.5 26.7 %all-to-all-start.7 = ((bf16[4,2,2,1600]{3,2,1,0:T(2,128)(2,1)}), bf16[4,2,2,1600]{3,2,1,0:T(2,128)(2,1)S(1)}, u32[]{:S(2)}, u32[]{:S(2)}) async-start(bf16[4,2,2,1600]{3,2,1,0:T(2,128)(2,1)} %convert_element_type.450), calls=%async_computation.7 | async-start | bytes 106496 | tf_op jit(solution)/shard_map/all_to_all | solution.py:418
  936.7 35.1 %collective-permute-start.51 = (bf16[2,2,128,640]{3,2,1,0:T(8,128)(2,1)}, bf16[2,2,128,640]{3,2,1,0:T(8,128)(2,1)}, u32[]{:S(2)}, u32[]{:S(2)}) collective-permute-start(bf16[2,2,128,640]{3,2,1,0:T(8,128)(2,1)} %fusion.95), channel_id=1, source_target_pairs={{0,4},{4,0},{1,5},{5,1},{2,6},{6,2},{3,7},{7,3},{8,12},{12,8},{9,1... | collective-permute-start | bytes 1966088 | tf_op jit(solution)/shard_map/ppermute | solution.py:45
  943.2 34.7 %collective-permute-start.48 = (bf16[176,2048]{1,0:T(8,128)(2,1)}, bf16[176,2048]{1,0:T(8,128)(2,1)}, u32[]{:S(2)}, u32[]{:S(2)}) collective-permute-start(bf16[176,2048]{1,0:T(8,128)(2,1)} %fusion.92), channel_id=1, source_target_pairs={{0,1},{1,0},{2,3},{3,2},{4,5},{5,4},{6,7},{7,6},{8,10},{9,11},{10,... | collective-permute-start | bytes 2162696 | tf_op jit(solution)/shard_map/ppermute | solution.py:118
  943.2 27.8 %all-to-all-start.8 = ((bf16[4,128,320]{1,2,0:T(8,128)(2,1)}), bf16[4,128,320]{1,2,0:T(8,128)(2,1)S(1)}, u32[]{:S(2)}, u32[]{:S(2)}) async-start(bf16[4,128,320]{1,2,0:T(8,128)(2,1)} %copy.186), calls=%async_computation.8 | async-start | bytes 655360 | tf_op jit(solution)/shard_map/all_to_all | solution.py:69
  977.7 130.1 %all-reduce.6.cloned.1.call-start = ((), (), s32[]{:S(2)}) async-start(), calls=%async_computation.12 | async-start | bytes 196608 | tf_op jit(solution)/shard_map/psum | solution.py:435
  986.1 127.6 %collective-permute-start.49 = (f32[176,2048]{1,0:T(8,128)}, f32[176,2048]{1,0:T(8,128)S(1)}, u32[]{:S(2)}, u32[]{:S(2)}) collective-permute-start(f32[176,2048]{1,0:T(8,128)} %get-tuple-element.143), channel_id=1, source_target_pairs={{0,1},{1,0},{2,3},{3,2},{4,5},{5,4},{6,7},{7,6},{8,9},{9,8},{10,11... | collective-permute-start | bytes 4325384 | tf_op jit(solution)/shard_map/ppermute | solution.py:445
  987.0 124.0 %collective-permute-start.30 = (bf16[176,2048]{1,0:T(8,128)(2,1)}, bf16[176,2048]{1,0:T(8,128)(2,1)}, u32[]{:S(2)}, u32[]{:S(2)}) collective-permute-start(bf16[176,2048]{1,0:T(8,128)(2,1)} %get-tuple-element.144), channel_id=1, source_target_pairs={{0,1},{1,0},{2,3},{3,2},{4,5},{5,4},{6,7},{7,6},{8,9},{9,8},{10,11... | collective-permute-start | bytes 2162696 | tf_op jit(solution)/shard_map/ppermute | solution.py:445
  (117 other events, 2998.2 us)
Sparse Core Ops, SparseCore 0:
  988.4 119.4 all-reduce.5

commit v2 on v1

--- a/solution.py
+++ b/solution.py
@@ -70,7 +70,8 @@
 
 
 class Tokens:
-    def __init__(self, sizes):
+    def __init__(self):
+        sizes = tuple(lax.axis_size(n) for n in AXES)
         self.core = swap_pairs(sizes, lambda a, b, c, d, e: (a, 1 - b, c, d, e))
         self.first = swap_pairs(
             sizes, lambda a, b, c, d, e: (a, b, c, d, 1 - e) if b == 0 else (a, b, c, 1 - d, e)
@@ -117,6 +118,758 @@
         keep_one = pick(one) + got[1].astype(F32)
         got = lax.ppermute(keep_one.astype(BF), AXES, self.first)
         return keep_own + got.astype(F32)
+
+
+MESH = pl.DeviceIdType.MESH
+ANY = pl.BlockSpec(memory_space=pl.ANY)
+VMEM = pl.BlockSpec(memory_space=pltpu.VMEM)
+VMEM_BYTES = 40 * 1024 * 1024
+
+
+def flip(index, by):
+    return 1 - index if by else index
+
+
+class Place:
+    def __init__(self):
+        self.dx, self.dc, self.zh, self.zl, self.mp = (lax.axis_index(n) for n in AXES)
+
+    def peer(self, dx=0, dc=0, zh=0, zl=0, mp=0):
+        return (
+            flip(self.dx, dx),
+            flip(self.dc, dc),
+            flip(self.zh, zh),
+            flip(self.zl, zl),
+            flip(self.mp, mp),
+        )
+
+    def block(self, dx=0, dc=0, zh=0, zl=0):
+        a, b, c, d, _ = self.peer(dx, dc, zh, zl)
+        return ((a * 2 + b) * 2 + c) * 2 + d
+
+    def slot(self, dc=0, zl=0):
+        return flip(self.dc, dc) * 2 + flip(self.zl, zl)
+
+    def rows(self, dc=0, mp=0, zl=0):
+        return (flip(self.dc, dc) * 2 + flip(self.mp, mp)) * 2 + flip(self.zl, zl)
+
+
+def greet(peers):
+    barrier = pltpu.get_barrier_semaphore()
+    for device in peers:
+        pl.semaphore_signal(barrier, inc=1, device_id=device, device_id_type=MESH)
+    pl.semaphore_wait(barrier, len(peers))
+
+
+class Links:
+    def __init__(self, send, recv, local):
+        self.send, self.recv, self.local = send, recv, local
+        self.n, self.m = 0, 0
+        self.sent, self.copies = [], []
+
+    def pair(self):
+        self.n += 1
+        return self.n - 1
+
+    def start(self, src, dst, at, device):
+        copy = pltpu.make_async_remote_copy(
+            src_ref=src,
+            dst_ref=dst,
+            send_sem=self.send.at[at],
+            recv_sem=self.recv.at[at],
+            device_id=device,
+            device_id_type=MESH,
+        )
+        copy.start()
+        self.sent.append(copy)
+
+    def arrived(self, ref, at):
+        pltpu.make_async_copy(ref, ref, self.recv.at[at]).wait()
+
+    def keep(self, src, dst):
+        copy = pltpu.make_async_copy(src, dst, self.local.at[self.m])
+        self.m += 1
+        copy.start()
+        return copy
+
+    def finish(self):
+        for copy in self.sent:
+            copy.wait_send()
+
+
+FLIPS = [(zh, dc, zl) for zh in (1, 0) for dc in (0, 1) for zl in (0, 1)]
+
+
+class WeightGather:
+    def __init__(self, place, links, source, target, unit):
+        self.place, self.links, self.target = place, links, target
+        self.at = {f: links.pair() for f in FLIPS}
+        self.cross = {(zh, dc): links.pair() for zh in (0, 1) for dc in (0, 1)}
+        self.source = source
+        self.kept = None
+
+    def begin(self, zhs=(1, 0)):
+        p = self.place
+        mine = p.block()
+        for f in FLIPS:
+            zh, dc, zl = f
+            if zh not in zhs:
+                continue
+            src, dst = self.source(p.slot(dc, zl)), self.target(mine, 1)
+            if f == (0, 0, 0):
+                self.kept = self.links.keep(src, dst)
+            else:
+                self.links.start(src, dst, self.at[f], p.peer(dc=dc, zh=zh, zl=zl))
+
+    def onward(self, zh):
+        p = self.place
+        for dc in (0, 1):
+            for zl in (0, 1):
+                if (zh, dc, zl) == (0, 0, 0):
+                    self.kept.wait()
+                else:
+                    self.links.arrived(
+                        self.target(p.block(dc=dc, zh=zh, zl=zl), 1), self.at[zh, dc, zl]
+                    )
+            two = self.target(p.block(dc=dc, zh=zh) // 2 * 2, 2)
+            self.links.start(two, two, self.cross[zh, dc], p.peer(dx=1))
+
+    def end(self):
+        p = self.place
+        for zh in (0, 1):
+            for dc in (0, 1):
+                two = self.target(p.block(dx=1, dc=dc, zh=zh) // 2 * 2, 2)
+                self.links.arrived(two, self.cross[zh, dc])
+
+
+def row_blocks(ref, unit, cols=None):
+    def target(first, count):
+        rows = pl.ds(pl.multiple_of(first * unit, unit), count * unit)
+        return ref.at[rows] if cols is None else ref.at[rows, cols]
+
+    return target
+
+
+def column_blocks(ref, unit):
+    return lambda first, count: ref.at[:, pl.ds(pl.multiple_of(first * unit, unit), count * unit)]
+
+
+def first_kernel(tok_ref, ig_ref, o_ref, all_ref, wig_ref, wo_ref, send, recv, local):
+    p = Place()
+    links = Links(send, recv, local)
+    drows = ig_ref.shape[1]
+    crows = wo_ref.shape[0]
+    greet(weight_peers(p))
+    gather = TokenGatherTwice(p, links, tok_ref, all_ref)
+    gather.begin()
+    w_ig = WeightGather(p, links, lambda j: ig_ref.at[j], row_blocks(wig_ref, drows), drows)
+    w_o = WeightGather(
+        p,
+        links,
+        lambda j: o_ref.at[pl.ds(pl.multiple_of(j * crows, 16), crows)],
+        column_blocks(wo_ref, o_ref.shape[1]),
+        drows,
+    )
+    w_ig.begin((0,))
+    w_ig.begin((1,))
+    w_o.begin((0,))
+    w_ig.onward(0)
+    w_o.begin((1,))
+    w_o.onward(0)
+    gather.forward()
+    gather.forward_core()
+    w_ig.onward(1)
+    w_o.onward(1)
+    gather.end()
+    w_ig.end()
+    w_o.end()
+    links.finish()
+
+
+class TokenGatherTwice:
+    def __init__(self, place, links, source, target):
+        self.place, self.links, self.source, self.target = place, links, source, target
+        self.z, self.y = links.pair(), links.pair()
+        self.core = {(mp, zl): links.pair() for mp in (0, 1) for zl in (0, 1)}
+
+    def begin(self):
+        p = self.place
+        self.kept = []
+        for mp in (0, 1):
+            at = p.rows(mp=mp)
+            src = self.source.at[flip(p.mp, mp)]
+            if mp == 0:
+                self.links.start(src, self.target.at[at], self.z, p.peer(zl=1))
+            self.links.start(src, self.target.at[at], self.core[mp, 0], p.peer(dc=1))
+            self.kept.append(self.links.keep(src, self.target.at[at]))
+
+    def forward(self):
+        p = self.place
+        far = self.target.at[p.rows(zl=1)]
+        self.links.arrived(far, self.z)
+        self.links.start(far, far, self.y, p.peer(mp=1))
+        self.links.start(far, far, self.core[0, 1], p.peer(dc=1))
+
+    def forward_core(self):
+        p = self.place
+        far = self.target.at[p.rows(mp=1, zl=1)]
+        self.links.arrived(far, self.y)
+        self.links.start(far, far, self.core[1, 1], p.peer(dc=1))
+
+    def end(self):
+        p = self.place
+        for (mp, zl), at in self.core.items():
+            self.links.arrived(self.target.at[p.rows(dc=1, mp=mp, zl=zl)], at)
+        for copy in self.kept:
+            copy.wait()
+
+
+class TokenGather:
+    def __init__(self, place, links, source, target):
+        self.place, self.links, self.source, self.target = place, links, source, target
+        self.z, self.y0, self.y1 = links.pair(), links.pair(), links.pair()
+        self.core = {(mp, zl): links.pair() for mp in (0, 1) for zl in (0, 1)}
+
+    def begin(self):
+        p = self.place
+        at = self.target.at[p.rows()]
+        self.links.start(self.source, at, self.z, p.peer(zl=1))
+        self.links.start(self.source, at, self.y0, p.peer(mp=1))
+        self.links.start(self.source, at, self.core[0, 0], p.peer(dc=1))
+        self.kept = self.links.keep(self.source, at)
+
+    def forward(self):
+        p = self.place
+        far = self.target.at[p.rows(zl=1)]
+        self.links.arrived(far, self.z)
+        self.links.start(far, far, self.y1, p.peer(mp=1))
+        self.links.start(far, far, self.core[0, 1], p.peer(dc=1))
+
+    def forward_core(self):
+        p = self.place
+        far = self.target.at[p.rows(mp=1)]
+        self.links.arrived(far, self.y0)
+        self.links.start(far, far, self.core[1, 0], p.peer(dc=1))
+        far = self.target.at[p.rows(mp=1, zl=1)]
+        self.links.arrived(far, self.y1)
+        self.links.start(far, far, self.core[1, 1], p.peer(dc=1))
+
+    def end(self):
+        p = self.place
+        for (mp, zl), at in self.core.items():
+            self.links.arrived(self.target.at[p.rows(dc=1, mp=mp, zl=zl)], at)
+        self.kept.wait()
+
+
+CHUNK = 16
+
+
+def chunks(count, body):
+    def step(i, carry):
+        body(pl.ds(pl.multiple_of(i * CHUNK, CHUNK), CHUNK))
+        return carry
+
+    lax.fori_loop(0, count // CHUNK, step, 0)
+
+
+class RowScatter:
+    def __init__(self, place, links, source, buffers):
+        self.place, self.links, self.source = place, links, source
+        self.mine, self.from_core, self.from_y, self.from_z, self.out = buffers
+        self.core = {(mp, zl): links.pair() for mp in (1, 0) for zl in (1, 0)}
+        self.y = {zl: links.pair() for zl in (1, 0)}
+        self.z = links.pair()
+
+    def begin(self):
+        p = self.place
+        self.kept = {}
+        for (mp, zl), at in self.core.items():
+            src = self.source.at[p.rows(dc=1, mp=mp, zl=zl)]
+            self.links.start(src, self.from_core.at[mp * 2 + zl], at, p.peer(dc=1))
+        for mp, zl in self.core:
+            src = self.source.at[p.rows(mp=mp, zl=zl)]
+            self.kept[mp, zl] = self.links.keep(src, self.mine.at[mp * 2 + zl])
+
+    def ready(self, mp, zl):
+        i = mp * 2 + zl
+        self.kept[mp, zl].wait()
+        self.links.arrived(self.from_core.at[i], self.core[mp, zl])
+        return i
+
+    def across_y(self):
+        p = self.place
+        for zl in (1, 0):
+            i = self.ready(1, zl)
+
+            def add(rows, i=i, zl=zl):
+                total = self.mine[i, rows, :].astype(F32) + self.from_core[i, rows, :].astype(F32)
+                self.out[zl, rows, :] = total.astype(BF)
+
+            chunks(self.mine.shape[1], add)
+            self.links.start(self.out.at[zl], self.from_y.at[zl], self.y[zl], p.peer(mp=1))
+
+    def across_z(self):
+        p = self.place
+        i = self.ready(0, 1)
+        self.links.arrived(self.from_y.at[1], self.y[1])
+
+        def add(rows):
+            total = self.mine[i, rows, :].astype(F32) + self.from_core[i, rows, :].astype(F32)
+            self.out[2, rows, :] = (total + self.from_y[1, rows, :].astype(F32)).astype(BF)
+
+        chunks(self.mine.shape[1], add)
+        self.links.start(self.out.at[2], self.from_z, self.z, p.peer(zl=1))
+
+    def arrive(self):
+        self.ready(0, 0)
+        self.links.arrived(self.from_y.at[0], self.y[0])
+        self.links.arrived(self.from_z, self.z)
+
+    def total(self, rows):
+        a = self.mine[0, rows, :].astype(F32) + self.from_core[0, rows, :].astype(F32)
+        b = self.from_y[0, rows, :].astype(F32) + self.from_z[rows, :].astype(F32)
+        return a + b
+
+
+def scatter_buffers(rows, width):
+    return [
+        pltpu.VMEM((4, rows, width), BF),
+        pltpu.VMEM((4, rows, width), BF),
+        pltpu.VMEM((2, rows, width), BF),
+        pltpu.VMEM((rows, width), BF),
+        pltpu.VMEM((3, rows, width), BF),
+    ]
+
+
+def group_peers(p):
+    return [p.peer(dc=1), p.peer(zl=1), p.peer(mp=1)]
+
+
+def weight_peers(p):
+    return [p.peer(dc=dc, zh=zh, zl=zl) for zh, dc, zl in FLIPS if (zh, dc, zl) != (0, 0, 0)] + [
+        p.peer(dx=1),
+        p.peer(mp=1),
+    ]
+
+
+def second_kernel(
+    part_ref, own_ref, gain_ref, cot_ref, gate_ref, up_ref, down_ref,
+    mid_ref, all_ref, dm_ref, wgu_ref, wd_ref,
+    mine, from_core, from_y, from_z, out, normed, send, recv, local,
+):
+    p = Place()
+    links = Links(send, recv, local)
+    drows, ff = gate_ref.shape[0], wd_ref.shape[0]
+    greet(weight_peers(p))
+    scatter = RowScatter(p, links, part_ref, (mine, from_core, from_y, from_z, out))
+    scatter.begin()
+
+    def wide(ref, at):
+        return WeightGather(
+            p,
+            links,
+            lambda j: ref.at[:, pl.ds(pl.multiple_of(j * ff, 128), ff)],
+            row_blocks(wgu_ref, drows, pl.ds(at, ff)),
+            drows,
+        )
+
+    w_g, w_u = wide(gate_ref, 0), wide(up_ref, ff)
+    w_d = WeightGather(
+        p,
+        links,
+        lambda j: down_ref.at[pl.ds(pl.multiple_of(j * ff, 16), ff)],
+        column_blocks(wd_ref, down_ref.shape[1]),
+        drows,
+    )
+    w_g.begin((0,))
+    w_g.begin((1,))
+    w_u.begin((0,))
+    w_d.begin((0,))
+    scatter.across_y()
+    w_u.begin((1,))
+    w_g.onward(0)
+    w_u.onward(0)
+    w_d.onward(0)
+    scatter.across_z()
+    scatter.arrive()
+
+    def normalise(rows):
+        value = own_ref[rows, :].astype(F32) + scatter.total(rows)
+        mid_ref[rows, :] = value
+        inv = lax.rsqrt(jnp.mean(value * value, axis=-1, keepdims=True) + EPSILON)
+        normed[rows, :] = (value * inv * gain_ref[...]).astype(BF)
+
+    chunks(own_ref.shape[0], normalise)
+    gather = TokenGather(p, links, normed, all_ref)
+    gather.begin()
+    w_d.begin((1,))
+    w_g.onward(1)
+    gather.forward()
+    adjoint = TokenGatherTwice(p, links, cot_ref, dm_ref)
+    adjoint.begin()
+    gather.forward_core()
+    w_u.onward(1)
+    adjoint.forward()
+    adjoint.forward_core()
+    w_d.onward(1)
+    gather.end()
+    adjoint.end()
+    w_g.end()
+    w_u.end()
+    w_d.end()
+    links.finish()
+
+
+class GradScatter:
+    def __init__(self, place, links, source, result, by_rows, buffers):
+        self.place, self.links, self.source, self.result = place, links, source, result
+        self.by_rows = by_rows
+        self.mine, self.from_x, self.to_z, self.from_z, self.sums = buffers
+        self.x = {(zh, dc): links.pair() for zh in (1, 0) for dc in (0, 1)}
+        self.z = {dc: links.pair() for dc in (0, 1)}
+        self.at = {(dc, zl): links.pair() for dc in (0, 1) for zl in (0, 1)}
+        self.kept = {}
+
+    def begin(self, zh):
+        p = self.place
+        for dc in (0, 1):
+            i = zh * 2 + dc
+            theirs = self.source(p.block(dx=1, dc=dc, zh=zh) // 2 * 2, 2)
+            self.links.start(theirs, self.from_x.at[i], self.x[zh, dc], p.peer(dx=1))
+            mine = self.source(p.block(dc=dc, zh=zh) // 2 * 2, 2)
+            self.kept[zh, dc] = self.links.keep(mine, self.mine.at[i])
+
+    def ready(self, zh, dc):
+        self.kept[zh, dc].wait()
+        self.links.arrived(self.from_x.at[zh * 2 + dc], self.x[zh, dc])
+        return zh * 2 + dc
+
+    def across(self, dc):
+        i = self.ready(1, dc)
+
+        def add(rows):
+            total = self.mine[i, rows, :].astype(F32) + self.from_x[i, rows, :].astype(F32)
+            self.to_z[dc, rows, :] = total.astype(BF)
+
+        chunks(self.mine.shape[1], add)
+        self.links.start(self.to_z.at[dc], self.from_z.at[dc], self.z[dc], self.place.peer(zh=1))
+
+    def last(self, dc):
+        p = self.place
+        i = self.ready(0, dc)
+        self.links.arrived(self.from_z.at[dc], self.z[dc])
+
+        def add(rows):
+            total = self.mine[i, rows, :].astype(F32) + self.from_x[i, rows, :].astype(F32)
+            self.sums[dc, rows, :] = (total + self.from_z[dc, rows, :].astype(F32)).astype(BF)
+
+        chunks(self.mine.shape[1], add)
+        for zl in (1, 0):
+            src = self.one(dc, flip(p.zl, zl))
+            dst = self.result.at[p.slot()]
+            if (dc, zl) == (0, 0):
+                self.own = self.links.keep(src, dst)
+            else:
+                self.links.start(src, dst, self.at[dc, zl], p.peer(dc=dc, zl=zl))
+
+    def one(self, dc, zl):
+        unit = self.result.shape[1] if self.by_rows else self.result.shape[2]
+        span = pl.ds(pl.multiple_of(zl * unit, unit), unit)
+        return self.sums.at[dc, span] if self.by_rows else self.sums.at[dc, :, span]
+
+    def end(self):
+        p = self.place
+        for (dc, zl), at in self.at.items():
+            if (dc, zl) == (0, 0):
+                self.own.wait()
+            else:
+                self.links.arrived(self.result.at[p.slot(dc, zl)], at)
+
+
+def grad_buffers(rows, columns):
+    return [
+        pltpu.VMEM((n, rows, columns), BF)
+        for n in (4, 4, 2, 2, 2)
+    ]
+
+
+def norm_back(value, gain, upstream):
+    inv = lax.rsqrt(jnp.mean(value * value, axis=-1, keepdims=True) + EPSILON)
+    scaled = value * inv
+    up = upstream * gain
+    inner = jnp.mean(up * scaled, axis=-1, keepdims=True)
+    return inv * (up - scaled * inner), upstream * scaled
+
+
+def fold(rows):
+    return rows[:8] + rows[8:]
+
+
+def third_kernel(
+    part_ref, mid_ref, dout_ref, gain_ref, gd_ref, ggu_ref,
+    dr1_ref, gain_out, all_ref, sd_ref, sgu_ref,
+    *scratch,
+):
+    p = Place()
+    links = Links(*scratch[-3:])
+    do = scratch[-4]
+    unit = sgu_ref.shape[1]
+    greet(weight_peers(p))
+    scatter = RowScatter(p, links, part_ref, scratch[:5])
+    down = GradScatter(p, links, column_blocks(gd_ref, unit), sd_ref, False, scratch[5:10])
+    wide = GradScatter(p, links, row_blocks(ggu_ref, unit), sgu_ref, True, scratch[10:15])
+    scatter.begin()
+    down.begin(1)
+    wide.begin(1)
+    scatter.across_y()
+    down.across(0)
+    down.across(1)
+    down.begin(0)
+    wide.across(0)
+    scatter.across_z()
+    scatter.arrive()
+    gain_out[...] = jnp.zeros_like(gain_out)
+
+    def back(rows):
+        part, gain = norm_back(mid_ref[rows, :], gain_ref[...], scatter.total(rows))
+        value = dout_ref[rows, :] + part
+        dr1_ref[rows, :] = value
+        do[rows, :] = value.astype(BF)
+        gain_out[...] += fold(gain)
+
+    chunks(mid_ref.shape[0], back)
+    gather = TokenGather(p, links, do, all_ref)
+    gather.begin()
+    wide.across(1)
+    wide.begin(0)
+    gather.forward()
+    down.last(0)
+    down.last(1)
+    gather.forward_core()
+    wide.last(0)
+    wide.last(1)
+    gather.end()
+    down.end()
+    wide.end()
+    links.finish()
+
+
+def fourth_kernel(
+    part_ref, own_ref, dr1_ref, gain_ref, go_ref, gig_ref, gg_ref,
+    dx_ref, gain_out, so_ref, sig_ref, sg_ref,
+    *scratch,
+):
+    p = Place()
+    links = Links(*scratch[-3:])
+    greet(weight_peers(p))
+    scatter = RowScatter(p, links, part_ref, scratch[:5])
+    out = GradScatter(
+        p, links, column_blocks(go_ref, so_ref.shape[2]), so_ref, False, scratch[5:10]
+    )
+    wide = GradScatter(
+        p, links, row_blocks(gig_ref, sig_ref.shape[1]), sig_ref, True, scratch[10:15]
+    )
+    gates = GradScatter(p, links, row_blocks(gg_ref, sg_ref.shape[1]), sg_ref, True, scratch[15:20])
+    grads = (out, wide, gates)
+    for g in grads:
+        g.begin(1)
+    scatter.begin()
+    for g in grads:
+        g.across(0)
+        g.across(1)
+        g.begin(0)
+    scatter.across_y()
+    for g in (out, gates):
+        g.last(0)
+        g.last(1)
+    scatter.across_z()
+    wide.last(0)
+    wide.last(1)
+    scatter.arrive()
+    gain_out[...] = jnp.zeros_like(gain_out)
+
+    def back(rows):
+        value = own_ref[rows, :].astype(F32)
+        part, gain = norm_back(value, gain_ref[...], scatter.total(rows))
+        dx_ref[rows, :] = dr1_ref[rows, :] + part
+        gain_out[...] += fold(gain)
+
+    chunks(own_ref.shape[0], back)
+    for g in grads:
+        g.end()
+    links.finish()
+
+
+def semaphores(pairs, local):
+    return [
+        pltpu.SemaphoreType.DMA((pairs,)),
+        pltpu.SemaphoreType.DMA((pairs,)),
+        pltpu.SemaphoreType.DMA((local,)),
+    ]
+
+
+def run_kernel(body, name, outs, out_specs, in_specs, scratch, ident, args):
+    return pl.pallas_call(
+        body,
+        name=name,
+        out_shape=[jax.ShapeDtypeStruct(*o) for o in outs],
+        in_specs=in_specs,
+        out_specs=out_specs,
+        scratch_shapes=scratch,
+        compiler_params=pltpu.CompilerParams(
+            collective_id=ident, has_side_effects=True, vmem_limit_bytes=VMEM_BYTES
+        ),
+    )(*args)
+
+
+def fetch_first(tokens, input_weight, gelu_weight, output_weight):
+    if not shape_fits():
+        return plain_fetch_first(tokens, input_weight, gelu_weight, output_weight)
+    rows, width = tokens.shape[1:]
+    drows, local = input_weight.shape[0], input_weight.shape[1] // 4
+    pairs = [v.reshape(drows, 4, local) for v in (input_weight, gelu_weight)]
+    ig = jnp.concatenate(pairs, axis=2).transpose(1, 0, 2)
+    return run_kernel(
+        first_kernel,
+        "fetch_first",
+        [((8, rows, width), BF), ((width, 2 * local), BF), ((local, width), BF)],
+        [ANY] * 3,
+        [ANY] * 3,
+        semaphores(32, 8),
+        1,
+        (tokens, ig, output_weight),
+    )
+
+
+def reduce_and_fetch(part, own, gain, dm, mlp_gate, mlp_up, mlp_down):
+    if not shape_fits():
+        return plain_reduce_and_fetch(part, own, gain, dm, mlp_gate, mlp_up, mlp_down)
+    rows, width = own.shape
+    ff = mlp_gate.shape[1] // 4
+    return run_kernel(
+        second_kernel,
+        "reduce_and_fetch",
+        [
+            ((rows, width), F32),
+            ((8, rows, width), BF),
+            ((8, rows, width), BF),
+            ((width, 2 * ff), BF),
+            ((ff, width), BF),
+        ],
+        [VMEM] + [ANY] * 4,
+        [ANY, VMEM, VMEM] + [ANY] * 4,
+        scatter_buffers(rows, width) + [pltpu.VMEM((rows, width), BF)] + semaphores(64, 16),
+        2,
+        (part.reshape(8, rows, width), own, gain, dm, mlp_gate, mlp_up, mlp_down),
+    )
+
+
+def reduce_and_return(part, middle, dout, gain, g_down, g_wide, drows):
+    if not shape_fits():
+        return plain_reduce_and_return(part, middle, dout, gain, g_down, g_wide, drows)
+    rows, width = middle.shape
+    ff = g_down.shape[0]
+    return run_kernel(
+        third_kernel,
+        "reduce_and_return",
+        [
+            ((rows, width), F32),
+            ((8, width), F32),
+            ((8, rows, width), BF),
+            ((4, ff, drows), BF),
+            ((4, drows, g_wide.shape[1]), BF),
+        ],
+        [VMEM, VMEM] + [ANY] * 3,
+        [ANY] + [VMEM] * 3 + [ANY] * 2,
+        scatter_buffers(rows, width)
+        + grad_buffers(ff, 2 * drows)
+        + grad_buffers(2 * drows, g_wide.shape[1])
+        + [pltpu.VMEM((rows, width), BF)]
+        + semaphores(40, 24),
+        3,
+        (part.reshape(8, rows, width), middle, dout, gain, g_down, g_wide),
+    )
+
+
+def return_last(part, own, dr1, gain, g_out, g_wide, g_gates, drows):
+    if not shape_fits():
+        return plain_return_last(part, own, dr1, gain, g_out, g_wide, g_gates, drows)
+    rows, width = own.shape
+    local, unit = g_out.shape[0], g_gates.shape[0] // 16
+    return run_kernel(
+        fourth_kernel,
+        "return_last",
+        [
+            ((rows, width), F32),
+            ((8, width), F32),
+            ((4, local, drows), BF),
+            ((4, drows, g_wide.shape[1]), BF),
+            ((4, unit, 128), BF),
+        ],
+        [VMEM, VMEM] + [ANY] * 3,
+        [ANY] + [VMEM] * 3 + [ANY] * 3,
+        scatter_buffers(rows, width)
+        + grad_buffers(local, 2 * drows)
+        + grad_buffers(2 * drows, g_wide.shape[1])
+        + grad_buffers(2 * unit, 128)
+        + semaphores(48, 32),
+        4,
+        (part.reshape(8, rows, width), own, dr1, gain, g_out, g_wide, g_gates),
+    )
+
+
+def shape_fits():
+    return all(lax.axis_size(n) == 2 for n in AXES)
+
+
+def plain_fetch_first(tokens, input_weight, gelu_weight, output_weight):
+    exchange = Tokens()
+    own = lax.dynamic_index_in_dim(tokens, exchange.mp, 0, keepdims=False)
+    return (
+        exchange.gather(own).reshape((8,) + own.shape),
+        fetch_weight([input_weight, gelu_weight], 4),
+        fetch_weight([output_weight.T], 4).T,
+    )
+
+
+def plain_reduce_and_fetch(part, own, gain, dm, mlp_gate, mlp_up, mlp_down):
+    exchange = Tokens()
+    middle = own.astype(F32) + exchange.scatter(part)
+    normed = (middle * inverse_rms(middle) * gain).astype(BF)
+    dm = lax.dynamic_index_in_dim(dm, exchange.mp, 0, keepdims=False)
+    return (
+        middle,
+        exchange.gather(normed).reshape((8,) + own.shape),
+        exchange.gather(dm).reshape((8,) + own.shape),
+        fetch_weight([mlp_gate, mlp_up], 4),
+        fetch_weight([mlp_down.T], 4).T,
+    )
+
+
+def plain_reduce_and_return(part, middle, dout, gain, g_down, g_wide, drows):
+    exchange = Tokens()
+    change, gain_rows = norm_back(middle, gain, exchange.scatter(part))
+    dr1 = dout + change
+    return (
+        dr1,
+        jnp.sum(gain_rows, axis=0, keepdims=True),
+        exchange.gather(dr1.astype(BF)).reshape((8,) + dr1.shape),
+        return_grad(g_down.T, drows).transpose(0, 2, 1),
+        return_grad(g_wide, drows),
+    )
+
+
+def plain_return_last(part, own, dr1, gain, g_out, g_wide, g_gates, drows):
+    exchange = Tokens()
+    change, gain_rows = norm_back(own.astype(F32), gain, exchange.scatter(part))
+    group = g_wide.shape[0] // drows
+    return (
+        dr1 + change,
+        jnp.sum(gain_rows, axis=0, keepdims=True),
+        return_grad(g_out.T, drows).transpose(0, 2, 1),
+        return_grad(g_wide, drows),
+        return_grad(g_gates, g_gates.shape[0] // group),
+    )
 
 
 def scan_body(reverse, a_ref, b_ref, p_ref, h_ref):
@@ -195,14 +948,6 @@
     return lax.rsqrt(jnp.mean(values * values, axis=-1, keepdims=True) + EPSILON)
 
 
-def norm_grad(values, gain, upstream):
-    inv = inverse_rms(values)
-    scaled = values * inv
-    up = upstream * gain
-    inner = jnp.mean(up * scaled, axis=-1, keepdims=True)
-    return inv * (up - scaled * inner), jnp.sum(upstream * scaled, axis=0)
-
-
 def gelu(v):
     return jax.nn.gelu(v, approximate=True)
 
@@ -246,7 +991,7 @@
     group = dxn * 2 * zhn * 2
     dc, zl, mp = (lax.axis_index(n) for n in ("dc", "zl", "mp"))
     slot = dc * 2 + zl
-    exchange = Tokens(sizes)
+    exchange = Tokens()
     length = tokens_in.shape[2]
     width = tokens_in.shape[3]
     local = input_weight.shape[1] // 4
@@ -255,43 +1000,42 @@
     piece = decay_gates.shape[1]
 
     own = lax.dynamic_index_in_dim(tokens_in[:, 0], mp, 0, keepdims=False)
-    own_cot = lax.dynamic_index_in_dim(cotangent[:, 0], mp, 0, keepdims=False).astype(F32)
-    source = lax.dynamic_index_in_dim(seq_source[:, 0], mp, 0, keepdims=False)
-    scale = jnp.sum(
-        jnp.where(jnp.arange(source_weight.shape[0], dtype=jnp.int32) == source, source_weight, 0.0)
-    )
-    dout = own_cot * scale
-    tokens = exchange.gather(own)
-    dm = exchange.gather(dout.astype(BF))
+    scales = jnp.stack(
+        [
+            jnp.sum(
+                jnp.where(
+                    jnp.arange(source_weight.shape[0], dtype=jnp.int32) == seq_source[m, 0],
+                    source_weight,
+                    0.0,
+                )
+            )
+            for m in range(2)
+        ]
+    )
+    douts = cotangent[:, 0].astype(F32) * scales[:, None, None]
+    dout = lax.dynamic_index_in_dim(douts, mp, 0, keepdims=False)
 
     small = jnp.concatenate([channel_params.reshape(-1), norm_gains.reshape(-1)])
-    small = lax.all_gather(small, ("dx", "dc", "zh", "zl"))
+    shards = ("dx", "dc", "zh", "zl")
+    small = lax.all_to_all(
+        jnp.broadcast_to(small[None], (group, small.size)), shards, 0, 0, tiled=True
+    )
     nch = channel_params.size
     channels = small[:, :nch].reshape(group, 8, -1).transpose(1, 0, 2).reshape(8, -1)
     channels = lax.dynamic_slice_in_dim(channels, slot * local, local, 1).astype(F32)
     gains = small[:, nch:].reshape(group, 2, -1).transpose(1, 0, 2).reshape(2, -1).astype(F32)
 
-    w_ig = fetch_weight([input_weight, gelu_weight], 4)
+    ff = mlp_gate.shape[1] // 4
+    tokens, w_ig, w_o = fetch_first(tokens_in[:, 0], input_weight, gelu_weight, output_weight)
+    tokens = tokens.reshape(-1, width)
+
     gates = jnp.stack([decay_gates, input_gates]).reshape(2, 4, heads, piece)
-    gates = gates.transpose(1, 0, 2, 3)
-    gates = lax.all_to_all(gates, ("dc", "zl"), 0, 0, tiled=True).reshape(2, 2, 2 * heads * piece)
-    gates = gather_blocks(gather_blocks(gates, "zh", 1), "dx", 0)
+    gates = gates.transpose(1, 0, 2, 3).reshape(2, 1, 2, 1, 2 * heads * piece)
+    gates = jnp.broadcast_to(gates, (2, zhn, 2, dxn, 2 * heads * piece))
+    gates = gates.transpose(3, 0, 1, 2, 4).reshape(group, 2 * heads * piece)
+    gates = lax.all_to_all(gates, shards, 0, 0, tiled=True)
     gates = gates.reshape(group, 2 * heads, piece).transpose(1, 0, 2)
     gates = gates.reshape(2, heads, BLOCK, BLOCK)
-    w_o = fetch_weight([output_weight.T], 4)
-    ff = mlp_gate.shape[1] // 4
-    half = ff // 2
-
-    gate4, up4, down4 = (v.reshape(drows, 4, ff) for v in (mlp_gate, mlp_up, mlp_down.T))
-    w_gu = []
-    for k in range(2):
-        cut = slice(k * half, (k + 1) * half)
-        w_gu.append(
-            fetch_weight(
-                [gate4[:, :, cut].reshape(drows, -1), up4[:, :, cut].reshape(drows, -1)], 4
-            )
-        )
-    w_d = fetch_weight([down4.reshape(drows, -1)], 4)
 
     wide = tokens.astype(F32)
     n1 = (wide * inverse_rms(wide) * gains[0]).astype(BF)
@@ -329,40 +1073,32 @@
     states = state + running * incoming[:, None]
     gelu_y, slope_y = gelu_both(gy)
     mixed = (gelu_y * states).astype(BF).reshape(-1, local)
-    middle = own.astype(F32) + exchange.scatter(dot(mixed, w_o, NT))
-    n2_own = (middle * inverse_rms(middle) * gains[1]).astype(BF)
-    n2 = exchange.gather(n2_own)
-
-    hidden, gates_pre = [], []
-    for k in range(2):
-        pre = dot(n2, w_gu[k], NN)
-        gm, up = pre[:, :half], pre[:, half:]
-        gates_pre.append((gm, up))
-        hidden.append((gelu(gm) * up).astype(BF))
-    hidden = jnp.concatenate(hidden, axis=1)
-    g_down = dot(dm, hidden, TN, BF)
-    share_down = return_grad(g_down, drows)
-    dhm = dot(dm, w_d, NN)
-    pair_grads, g_gu, dn2 = [], [], None
-    for k in range(2):
-        gm, up = gates_pre[k]
-        value, slope = gelu_both(gm)
-        d = dhm[:, k * half : (k + 1) * half]
-        pair = jnp.concatenate([(d * up * slope).astype(BF), (d * value).astype(BF)], axis=1)
-        pair_grads.append(pair)
-        term = dot(pair, w_gu[k], NT)
-        dn2 = term if dn2 is None else dn2 + term
-    share_gu = [return_grad(dot(n2, pair_grads[k], TN, BF), drows) for k in range(2)]
-    dn2_own = exchange.scatter(dn2)
-    part, gain_two = norm_grad(middle, gains[1], dn2_own)
-    dr1 = dout + part
-    do = exchange.gather(dr1.astype(BF))
-
-    result = middle + exchange.scatter(dot(hidden, w_d, NT))
+    middle, n2, dm, w_gu, w_d = reduce_and_fetch(
+        dot(mixed, w_o, NN, BF), own, gains[1:2], douts.astype(BF), mlp_gate, mlp_up, mlp_down
+    )
+    n2 = n2.reshape(-1, width)
+    dm = dm.reshape(-1, width)
+
+    pre = dot(n2, w_gu, NN)
+    gm, up = pre[:, :ff], pre[:, ff:]
+    value, slope = gelu_both(gm)
+    hidden = (value * up).astype(BF)
+    g_down = dot(hidden, dm, TN, BF)
+    dhm = dot(dm, w_d, NT)
+    dgm, dup = (dhm * up * slope).astype(BF), (dhm * value).astype(BF)
+    pair = jnp.concatenate([dgm, dup], axis=1)
+    g_wide = dot(n2, pair, TN, BF)
+    dr1, gain_two, do, share_down, share_wide = reduce_and_return(
+        dot(pair, w_gu, NT, BF), middle, dout, gains[1:2], g_down, g_wide, drows
+    )
+    gain_two = jnp.sum(gain_two, axis=0)
+    do = do.reshape(-1, width)
+
+    result = middle + exchange.scatter(dot(hidden, w_d, NN))
     result = result.astype(BF)
 
-    share_o = return_grad(dot(do, mixed, TN, BF), drows)
-    dz = dot(do, w_o, NN).reshape(4, 2 * length, local)
+    g_out = dot(mixed, do, TN, BF)
+    dz = dot(do, w_o, NT).reshape(4, 2 * length, local)
     dh = dz * gelu_y
     dgy = (dz * states * slope_y).astype(BF)
     ones = jnp.ones_like(decay[:, :1])
@@ -392,10 +1128,8 @@
         [jnp.zeros((4, 2 * length - 3, local), F32), back], axis=1
     )
     dboth = jnp.concatenate([dxb.astype(BF), dgy], axis=2).reshape(-1, 2 * local)
-    share_ig = return_grad(dot(n1, dboth, TN, BF), drows)
-    dn1_own = exchange.scatter(dot(dboth, w_ig, NT))
-    part, gain_one = norm_grad(own.astype(F32), gains[0], dn1_own)
-    dx_own = dr1 + part
+    g_wide_ig = dot(n1, dboth, TN, BF)
+    dn1 = dot(dboth, w_ig, NT, BF)
 
     g_gates = jnp.stack(
         [
@@ -411,11 +1145,22 @@
             for g in range(2)
         ]
     )
-    g_gates = g_gates.reshape(2 * heads, group, piece).transpose(1, 0, 2)
-    g_gates = g_gates.reshape(dxn, 2, zhn, 2, 2 * heads * piece)
-    g_gates = scatter_blocks(scatter_blocks(g_gates, "dx", 0), "zh", 1)
-    g_gates = g_gates.reshape(4, 2, heads, piece).astype(BF)
-    g_gates = lax.all_to_all(g_gates, ("dc", "zl"), 0, 0, tiled=True).astype(F32)
+    g_gates = g_gates.reshape(2 * heads, group, piece).transpose(1, 0, 2).reshape(group, -1)
+    count = g_gates.shape[1]
+    unit = (count + 2047) // 2048 * 16
+    g_gates = jnp.pad(g_gates, ((0, 0), (0, unit * 128 - count))).astype(BF)
+    dx_own, gain_one, share_o, share_ig, share_gates = return_last(
+        dn1,
+        own,
+        dr1,
+        gains[0:1],
+        g_out,
+        g_wide_ig,
+        g_gates.reshape(group * unit, 128),
+        drows,
+    )
+    gain_one = jnp.sum(gain_one, axis=0)
+    g_gates = share_gates.reshape(4, -1)[:, :count].astype(F32).reshape(4, 2, heads, piece)
     g_gates = g_gates.transpose(1, 0, 2, 3).reshape(2, 4 * heads, piece)
 
     channel_grad = jnp.stack(
@@ -427,19 +1172,17 @@
         ]
         + taps
     )
-    spot = (mp * 4 + slot).astype(jnp.int32)
-    table = jnp.where(
-        jnp.arange(8, dtype=jnp.int32)[:, None, None] == spot, channel_grad[None], 0.0
-    )
-    sums = jnp.concatenate([table.reshape(-1), gain_one, gain_two])
-    sums = lax.psum(sums, AXES)
-    share = lax.axis_index(("dx", "dc", "zh", "zl"))
-    table = sums[: table.size].reshape(2, 4, 8, local).transpose(0, 2, 1, 3)
-    table = lax.dynamic_index_in_dim(table.reshape(2, 8, 4 * local), mp, 0, keepdims=False)
     per = 4 * local // group
-    g_channels = lax.dynamic_slice_in_dim(table, share * per, per, 1).reshape(8, 1, per)
-    g_gains = sums[-2 * width :].reshape(2, width)
-    g_gains = lax.dynamic_slice_in_dim(g_gains, share * drows, drows, 1)
+    mine = channel_grad.reshape(8, group // 4, per).transpose(1, 0, 2)
+    mine = jnp.where(
+        jnp.arange(4, dtype=jnp.int32)[:, None, None, None] == slot, mine[None], 0.0
+    ).reshape(group, 8 * per)
+    both_gains = jnp.stack([gain_one, gain_two]).reshape(2, group, -1).transpose(1, 0, 2)
+    sums = jnp.concatenate([both_gains.reshape(group, -1), mine], axis=1)
+    sums = jnp.sum(lax.all_to_all(sums, shards, 0, 0, tiled=True), axis=0)
+    g_gains = sums[: 2 * drows].reshape(2, drows)
+    g_gains = g_gains + lax.ppermute(g_gains, "mp", [(0, 1), (1, 0)])
+    g_channels = sums[2 * drows :].reshape(8, 1, per)
 
     def both_batches(rows):
         other = lax.ppermute(rows, "mp", [(0, 1), (1, 0)])
@@ -453,11 +1196,6 @@
             share[:, :, at : at + count].astype(F32).transpose(1, 0, 2).reshape(drows, 4 * count)
         )
 
-    g_gate = jnp.stack([s[:, :, :half] for s in share_gu], axis=2)
-    g_up = jnp.stack([s[:, :, half:] for s in share_gu], axis=2)
-    g_gate, g_up = (
-        v.astype(F32).transpose(1, 0, 2, 3).reshape(drows, 4 * ff) for v in (g_gate, g_up)
-    )
     return (
         block_out,
         grad_tokens,
@@ -467,10 +1205,10 @@
         g_gates[1],
         g_channels,
         g_gains,
-        columns(share_o, 0, local).T,
-        g_gate,
-        g_up,
-        columns(share_down, 0, ff).T,
+        share_o.astype(F32).reshape(-1, drows),
+        columns(share_wide, 0, ff),
+        columns(share_wide, ff, ff),
+        share_down.astype(F32).reshape(-1, drows),
     )
 
 

time: 1130 us -> 841 us (0.74)
  Pallas kernels: 12.6 us -> 489 us
  waiting for transfers between devices: 480 us -> 51.4 us
  starting transfers between devices: 177 us -> 32.4 us
  local copies, waits for them, and re-layouts: 154 us -> 67.7 us
  other arithmetic: 146 us -> 73.5 us
  blocking collectives: 30 us -> 0 us
  between operations: 16.6 us -> 2.16 us
    pallas_call x0 -> x4, Pallas kernels: none -> 477 us  [run_kernel(): pl.pallas_call(body, name=name, out_shape=[jax.ShapeDtypeStruct(*o) for o...]
    ppermute x44 -> x1, waiting for transfers between devices: 303 us -> 0.01 us  [on_device(): g_gains = g_gains + lax.ppermute(g_gains, 'mp', [(0, 1), (1, 0)])]
    psum x1 -> x0, waiting for transfers between devices: 117 us -> none  [on_device(): sums = lax.psum(sums, AXES)]
    ppermute x44 -> x1, starting transfers between devices: 82.9 us -> 1 us  [on_device(): g_gains = g_gains + lax.ppermute(g_gains, 'mp', [(0, 1), (1, 0)])]
    all_to_all x12 -> x3, starting transfers between devices: 62 us -> 15.5 us  [the longest x1 7.32 us: on_device(): lax.all_to_all(jnp.broadcast_to(small[None], (group, small.size)), shards...]
    ppermute x4 -> x1, waiting for transfers between devices: 0.01 us -> 44.5 us  [scatter(): lax.ppermute(jnp.stack([pick(two), pick(both)]).astype(BF), AXES, self.se...]
    dynamic_update_slice x28 -> x0, local copies, waits for them, and re-layouts: 33.8 us -> none  [gather(): out = lax.dynamic_update_index_in_dim(out, block, dc * 4 + at, 0)]
    all_to_all x12 -> x3, waiting for transfers between devices: 32.3 us -> 0.01 us  [the longest x1 0.01 us: on_device(): gates = lax.all_to_all(gates, shards, 0, 0, tiled=True)]
  transfers between devices with their start and end apart: 75 -> 13, of which waited for: 26 -> 3; matrix products, arithmetic and copies ran while one was open for 29% -> 17% of each run, Pallas kernels for 1% -> 20%
where the time goes in v2:
time: 841 us; the launch traced here: 835 us
  Pallas kernels  489 us (58%)
  matrix products  118 us (14%)
  other arithmetic  73.5 us (9%)
  local copies, waits for them, and re-layouts  67.7 us (8%)
  waiting for transfers between devices  51.4 us (6%)
  starting transfers between devices  32.4 us (4%)
    pallas_call x4, Pallas kernels, run_kernel(): pl.pallas_call(body, name=name, out_shape=[jax.ShapeDtypeStruct(*o) for o...  477 us
    dot_general x15, matrix products, dot(): r = lax.dot_general(a, b, (dims, ((), ())), preferred_element_type=F32)  118 us
    ppermute x1, waiting for transfers between devices, scatter(): lax.ppermute(jnp.stack([pick(two), pick(both)]).astype(BF), AXES, self.se...  44.5 us
    unnamed x155, local copies, waits for them, and re-layouts  26.1 us
  transfers between devices with their start and end apart: 13, of which 3 were waited for; matrix products, arithmetic and copies ran while one was open for 17% of the time, Pallas kernels for 20%

profile of v2, /device:TPU:1, one launch (start us, length us, event | category | flops | bytes accessed | tf_op | source)
XLA Modules:
  0.0 834.9 jit_solution(9513170493599268342)
XLA Ops:
  4.2 7.3 all-to-all-start
  14.6 88.4 %fetch_first.1 = (bf16[8,176,2048]{2,1,0:T(8,128)(2,1)S(1)}, bf16[2048,640]{1,0:T(8,128)(2,1)S(1)}, bf16[320,2048]{1,0:T(8,128)(2,1)S(1)}) custom-call(bf16[2,176,2048]{2,1,0:T(8,128)(2,1)S(1)} %bitcast.193, bf16[4,128,640]{2,1,0:T(8,128)(2,1)S(1)} %maximum_bitcast_fusion.2.ig_ref, bf16[1280,128]{1,0:T(8,128)(2,1)S(1)} %copy-done.13), custom_call_target="tpu_custom_call" | custom-call | tf_op jit(solution)/shard_map/fetch_first/pallas_call | solution.py:712
  103.0 1.5 copy-done.14
  108.8 1.9 fusion.46
  110.7 1.4 pad_maximum_fusion.15
  112.0 3.0 convert_multiply_fusion.3
  115.8 1.8 reduce.22
  119.0 4.5 all-to-all-start.1
  124.7 4.2 fusion.1
  128.9 4.5 fusion.59
  133.4 1.9 copy-done.32
  136.3 2.3 copy.112
  139.3 4.4 collective-permute-start
  144.3 1.5 maximum_convert_fusion
  145.8 1.4 copy-done.19
  147.2 2.0 add_convert_fusion
  151.3 2.6 fusion.43
  154.1 4.7 convert_multiply_fusion.2
  158.8 6.2 shard_map.229
  165.0 3.0 copy.118
  168.0 4.8 collective-permute-start.1
  172.8 6.5 multiply_convert_fusion
  180.6 3.3 copy.110
  183.9 1.9 slice.283
  185.9 1.5 concatenate.57.refs_0_
  190.3 5.0 convolution_convert_fusion
  195.3 163.9 %reduce_and_fetch.1 = (f32[176,2048]{1,0:T(8,128)S(1)}, bf16[8,176,2048]{2,1,0:T(8,128)(2,1)}, bf16[8,176,2048]{2,1,0:T(8,128)(2,1)}, bf16[2048,1536]{1,0:T(8,128)(2,1)}, bf16[768,2048]{1,0:T(8,128)(2,1)S(1)}) custom-call(bf16[8,176,2048]{2,1,0:T(8,128)(2,1)} %bitcast.203, bf16[176,2048]{1,0:T(8,128)(2,1)S(1)} %dynamic-slice_bitcast_fusion.1.own_ref, ...), custom_call_target="tpu_custom_call" | custom-call | tf_op jit(solution)/shard_map/reduce_and_fetch/pallas_call | solution.py:712
  359.2 15.6 %fusion.60 = f32[1408,1536]{1,0:T(8,128)} fusion(bf16[1408,2048]{1,0:T(8,128)(2,1)} %bitcast.239, bf16[2048,1536]{1,0:T(8,128)(2,1)} %get-tuple-element.41), kind=kOutput, calls=%fused_computation.186 | convolution fusion | flops 8858370048 | bytes 20709376 | tf_op jit(solution)/shard_map/dot_general | solution.py:964
  374.8 11.4 %fusion.8 = (bf16[1408,768]{1,0:T(8,128)(2,1)S(1)}, bf16[1408,768]{1,0:T(8,128)(2,1)S(1)}, bf16[1408,768]{1,0:T(8,128)(2,1)S(1)}) fusion(f32[1408,1536]{1,0:T(8,128)} %fusion.60, bf16[1408,2048]{1,0:T(8,128)(2,1)} %bitcast.237, bf16[768,2048]{1,0:T(8,128)(2,1)S(1)} %get-tuple-element.42), kind=kOutput, calls=%fused_computation.19 | convolution fusion | flops 4456218624 | bytes 24051712 | tf_op jit(solution)/shard_map/dot_general | solution.py:964
  386.3 1.3 copy-done.66
  387.6 14.0 %convolution_convert_fusion.2.ggu_ref = bf16[2048,1536]{1,0:T(8,128)(2,1)} fusion(bf16[1408,2048]{1,0:T(8,128)(2,1)} %bitcast.240, bf16[1408,768]{1,0:T(8,128)(2,1)S(1)} %get-tuple-element.128, bf16[1408,768]{1,0:T(8,128)(2,1)S(1)} %get-tuple-element.127), kind=kOutput, calls=%fused_computation.7 | convolution fusion | flops 8870166528 | bytes 16384000 | tf_op jit(solution)/shard_map/dot_general | solution.py:964
  401.6 13.5 %convolution_convert_fusion.3 = bf16[1408,2048]{1,0:T(8,128)(2,1)} fusion(bf16[2048,1536]{1,0:T(8,128)(2,1)} %get-tuple-element.41, bf16[1408,768]{1,0:T(8,128)(2,1)} %copy-done.66, bf16[1408,768]{1,0:T(8,128)(2,1)S(1)} %get-tuple-element.127), kind=kOutput, calls=%fused_computation.8 | convolution fusion | flops 8869904384 | bytes 16384000 | tf_op jit(solution)/shard_map/dot_general | solution.py:964
  415.1 8.0 convolution_convert_fusion.4.gd_ref
  423.1 7.7 fusion.61
  430.9 142.6 %reduce_and_return.1 = (f32[176,2048]{1,0:T(8,128)S(1)}, f32[8,2048]{1,0:T(8,128)S(1)}, bf16[8,176,2048]{2,1,0:T(8,128)(2,1)}, bf16[4,768,128]{2,1,0:T(8,128)(2,1)S(1)}, bf16[4,128,1536]{2,1,0:T(8,128)(2,1)S(1)}) custom-call(bf16[8,176,2048]{2,1,0:T(8,128)(2,1)} %bitcast.204, f32[176,2048]{1,0:T(8,128)S(1)} %get-tuple-element.39.mid_ref, ...), custom_call_target="tpu_custom_call" | custom-call | tf_op jit(solution)/shard_map/reduce_and_return/pallas_call | solution.py:712
  573.6 9.8 %fusion.40 = (f32[4,352,320]{2,1,0:T(8,128)}, bf16[4,352,320]{2,1,0:T(8,128)(2,1)}) fusion(f32[4,352,320]{2,1,0:T(8,128)S(1)} %bitcast.196, f32[4,352,320]{2,1,0:T(8,128)S(1)} %get-tuple-element.126, bf16[4,352,2048]{2,1,0:T(8,128)(2,1)} %bitcast.235, bf16[320,2048]{1,0:T(8,128)(2,1)S(1)} %copy-done.18), kind=kOutput, calls=%fused_computation.105 | convolution fusion | flops 1855406080 | bytes 13385728 | tf_op jit(solution)/shard_map/dot_general | solution.py:964
  583.4 6.4 shard_map.230
  591.9 6.1 convolution_convert_fusion.6.go_ref
  598.0 1.9 convert_bitcast_fusion
  601.2 4.7 fusion.9
  605.9 1.9 copy.131
  607.8 1.6 copy.137
  609.4 3.0 copy.132
  612.4 3.2 copy.138
  616.7 7.2 convert_reduce_fusion
  623.9 5.3 convert_reduce_fusion.1
  630.3 5.2 multiply_reduce_fusion.1
  637.5 1.5 collective-permute-start.7
  649.1 6.5 convolution_convert_fusion.1
  655.6 7.2 convolution_convert_fusion.5.gig_ref
  662.9 82.0 %return_last.1 = (f32[176,2048]{1,0:T(8,128)S(1)}, f32[8,2048]{1,0:T(8,128)S(1)}, bf16[4,320,128]{2,1,0:T(8,128)(2,1)S(1)}, bf16[4,128,640]{2,1,0:T(8,128)(2,1)S(1)}, bf16[4,64,128]{2,1,0:T(8,128)(2,1)S(1)}) custom-call(bf16[8,176,2048]{2,1,0:T(8,128)(2,1)} %bitcast.205, bf16[176,2048]{1,0:T(8,128)(2,1)S(1)} %dynamic-slice_bitcast_fusion.1.own_ref, ...), custom_call_target="tpu_custom_call" | custom-call | tf_op jit(solution)/shard_map/return_last/pallas_call | solution.py:712
  746.4 3.7 all-to-all-start.2
  751.4 4.8 bitcast_add_fusion
  756.2 2.5 copy-done.24
  762.2 44.5 %collective-permute-done.3 = bf16[2,176,2048]{2,1,0:T(8,128)(2,1)} collective-permute-done((bf16[2,176,2048]{2,1,0:T(8,128)(2,1)}, bf16[2,176,2048]{2,1,0:T(8,128)(2,1)}, u32[]{:S(2)}, u32[]{:S(2)}) %collective-permute-start.3) | collective-permute-done | bytes 1441824 | tf_op jit(solution)/shard_map/ppermute | solution.py:116
  806.8 2.6 fusion.42
  809.4 1.5 collective-permute-start.4
  814.4 1.4 copy.128
  816.8 1.5 squeeze.67
  818.3 1.5 squeeze.68
  821.0 2.1 fusion.36
  823.7 1.6 select_bitcast_fusion.1
  825.3 1.8 maximum_bitcast_fusion
  827.1 6.3 collective-permute-done.5
  (264 shorter events, 54.0 us)
Async XLA Ops:
  3.4 11.1 %copy-start.4 = (bf16[2,1,176,2048]{3,2,1,0:T(8,128)(2,1)S(1)}, bf16[2,1,176,2048]{3,2,1,0:T(8,128)(2,1)}, u32[]{:S(2)}) copy-start(bf16[2,1,176,2048]{3,2,1,0:T(8,128)(2,1)} %param.14) | copy-start | bytes 4325380
  3.4 11.1 %copy-start.13 = (bf16[1280,128]{1,0:T(8,128)(2,1)S(1)}, bf16[1280,128]{1,0:T(8,128)(2,1)}, u32[]{:S(2)}) copy-start(bf16[1280,128]{1,0:T(8,128)(2,1)} %o_ref.1) | copy-start | bytes 983044
  4.2 114.8 %all-to-all-start = ((bf16[16,2,448]{2,1,0:T(2,128)(2,1)}), bf16[16,2,448]{2,1,0:T(2,128)(2,1)S(1)}, u32[]{:S(2)}, u32[]{:S(2)}) async-start(bf16[16,2,448]{2,1,0:T(2,128)(2,1)} %reshape.378), calls=%async_computation | async-start | bytes 65536 | tf_op jit(solution)/shard_map/all_to_all | solution.py:1020
  105.5 2.5 copy-start
  105.5 2.5 copy-start.54
  105.5 2.5 copy-start.55
  105.5 2.6 copy-start.63
  105.5 3.2 copy-start.65
  119.0 30.2 %all-to-all-start.1 = ((bf16[16,2,3200]{2,1,0:T(2,128)(2,1)}), bf16[16,2,3200]{2,1,0:T(2,128)(2,1)S(1)}, u32[]{:S(2)}, u32[]{:S(2)}) async-start(bf16[16,2,3200]{2,1,0:T(2,128)(2,1)} %reshape.380), calls=%async_computation.1 | async-start | bytes 409600 | tf_op jit(solution)/shard_map/all_to_all | solution.py:1036
  124.6 29.4 %copy-start.40 = (f32[320]{0:T(512)}, f32[320]{0:T(512)S(1)}, u32[]{:S(2)}) copy-start(f32[320]{0:T(512)S(1)} %get-tuple-element.114) | copy-start | bytes 3844
  124.6 29.4 %copy-start.42 = (f32[320]{0:T(512)}, f32[320]{0:T(512)S(1)}, u32[]{:S(2)}) copy-start(f32[320]{0:T(512)S(1)} %get-tuple-element.115) | copy-start | bytes 3844
  124.6 29.4 %copy-start.45 = (f32[320]{0:T(512)}, f32[320]{0:T(512)S(1)}, u32[]{:S(2)}) copy-start(f32[320]{0:T(512)S(1)} %get-tuple-element.111) | copy-start | bytes 3844
  124.6 29.4 %copy-start.47 = (f32[320]{0:T(512)}, f32[320]{0:T(512)S(1)}, u32[]{:S(2)}) copy-start(f32[320]{0:T(512)S(1)} %get-tuple-element.116) | copy-start | bytes 3844
  124.6 29.4 %copy-start.50 = (f32[320]{0:T(512)}, f32[320]{0:T(512)S(1)}, u32[]{:S(2)}) copy-start(f32[320]{0:T(512)S(1)} %get-tuple-element.109) | copy-start | bytes 3844
  124.7 4.2 copy-start.15
  139.3 5.0 collective-permute-start
  143.7 10.3 %copy-start.52 = (f32[320]{0:T(512)}, f32[320]{0:T(512)S(1)}, u32[]{:S(2)}) copy-start(f32[320]{0:T(512)S(1)} %fusion.44) | copy-start | bytes 3844
  151.3 2.7 copy-start.38
  151.3 2.8 copy-start.20
  154.0 4.8 copy-start.22
  168.0 11.3 %copy-start.33 = (f32[1408,640]{0,1:T(8,128)S(1)}, f32[1408,640]{0,1:T(8,128)}, u32[]{:S(2)}) copy-start(f32[1408,640]{0,1:T(8,128)} %copy-done.32) | copy-start | bytes 10813444
  168.0 19.3 %collective-permute-start.1 = (f32[4,320]{1,0:T(4,128)S(1)}, f32[4,320]{1,0:T(4,128)S(1)}, u32[]{:S(2)}, u32[]{:S(2)}) collective-permute-start(f32[4,320]{1,0:T(4,128)S(1)} %slice_bitcast_fusion.9), channel_id=1, source_target_pairs={{0,4},{1,5},{2,6},{3,7},{8,12},{9,13},{10,14},{11,15},{16,20},{17,... | collective-permute-start | bytes 15368 | tf_op jit(solution)/shard_map/ppermute | solution.py:929
  183.9 3.4 copy-start.31
  185.8 2.5 copy-start.27
  185.9 3.1 copy-start.28
  189.9 5.4 copy-start.35
  189.9 383.6 %copy-start.29 = (f32[4,352,320]{2,1,0:T(8,128)}, f32[4,352,320]{2,1,0:T(8,128)S(1)}, u32[]{:S(2)}) copy-start(f32[4,352,320]{2,1,0:T(8,128)S(1)} %get-tuple-element.126) | copy-start | bytes 5406724
  190.3 5.0 copy-start.3
  190.3 5.0 copy-start.10
  190.3 5.0 copy-start.11
  190.3 5.0 copy-start.12
  359.2 71.7 %copy-start.1 = (f32[176,2048]{1,0:T(8,128)}, f32[176,2048]{1,0:T(8,128)S(1)}, u32[]{:S(2)}) copy-start(f32[176,2048]{1,0:T(8,128)S(1)} %get-tuple-element.39.mid_ref) | copy-start | bytes 4325380
  573.5 9.9 %copy-start.5 = (bf16[4,128,1536]{2,1,0:T(8,128)(2,1)}, bf16[4,128,1536]{2,1,0:T(8,128)(2,1)S(1)}, u32[]{:S(2)}) copy-start(bf16[4,128,1536]{2,1,0:T(8,128)(2,1)S(1)} %get-tuple-element.54) | copy-start | bytes 4718596
  573.5 9.9 %copy-start.7 = (f32[176,2048]{1,0:T(8,128)}, f32[176,2048]{1,0:T(8,128)S(1)}, u32[]{:S(2)}) copy-start(f32[176,2048]{1,0:T(8,128)S(1)} %get-tuple-element.47.dr1_ref) | copy-start | bytes 4325380
  583.4 8.5 %copy-start.36 = (bf16[4,352,320]{2,1,0:T(8,128)(2,1)S(1)}, bf16[4,352,320]{2,1,0:T(8,128)(2,1)}, u32[]{:S(2)}) copy-start(bf16[4,352,320]{2,1,0:T(8,128)(2,1)} %copy-done.35) | copy-start | bytes 2703364
  590.6 26.0 %collective-permute-start.6 = (f32[4,320]{1,0:T(4,128)S(1)}, f32[4,320]{1,0:T(4,128)S(1)}, u32[]{:S(2)}, u32[]{:S(2)}) collective-permute-start(f32[4,320]{1,0:T(4,128)S(1)} %bitcast.233), channel_id=1, source_target_pairs={{4,0},{5,1},{6,2},{7,3},{12,8},{13,9},{14,10},{15,11},{20,16},{21,... | collective-permute-start | bytes 15368 | tf_op jit(solution)/shard_map/ppermute | solution.py:929
  591.9 6.1 copy-start.6
  612.4 4.2 copy-start.21
  612.4 4.3 copy-start.41
  612.4 4.3 copy-start.43
  612.4 4.3 copy-start.46
  612.4 4.3 copy-start.48
  612.4 4.3 copy-start.51
  612.4 4.3 copy-start.53
  615.6 135.8 %collective-permute-start.2 = (bf16[4,176,2048]{2,1,0:T(8,128)(2,1)}, bf16[4,176,2048]{2,1,0:T(8,128)(2,1)}, u32[]{:S(2)}, u32[]{:S(2)}) collective-permute-start(bf16[4,176,2048]{2,1,0:T(8,128)(2,1)} %fusion.9), channel_id=1, source_target_pairs={{0,8},{1,9},{2,10},{3,11},{4,12},{5,13},{6,14},{7,15},{8,0},{9,1},... | collective-permute-start | bytes 8650760 | tf_op jit(solution)/shard_map/ppermute | solution.py:113
  616.7 7.2 copy-start.23
  616.7 7.2 copy-start.30
  623.9 5.3 copy-start.34
  636.8 2.8 copy-start.25
  637.5 8.7 %collective-permute-start.7 = (f32[4,3,320]{2,1,0:T(4,128)}, f32[4,3,320]{2,1,0:T(4,128)}, u32[]{:S(2)}, u32[]{:S(2)}) collective-permute-start(f32[4,3,320]{2,1,0:T(4,128)} %slice.289), channel_id=1, source_target_pairs={{4,0},{5,1},{6,2},{7,3},{12,8},{13,9},{14,10},{15,11},{20,16},{21,... | collective-permute-start | bytes 46088 | tf_op jit(solution)/shard_map/ppermute | solution.py:942
  639.0 2.1 copy-start.58
  639.0 2.5 copy-start.64
  639.6 6.6 copy-start.26
  655.6 7.2 copy-start.8
  655.6 7.2 copy-start.9
  662.8 82.1 %copy-start.49 = (f32[2048]{0:T(1024)S(1)}, f32[2048]{0:T(1024)}, u32[]{:S(2)}) copy-start(f32[2048]{0:T(1024)} %reduce_sum.130) | copy-start | bytes 24580
  746.4 15.8 %all-to-all-start.2 = ((f32[16,1,896]{2,1,0:T(1,128)}), f32[16,1,896]{2,1,0:T(1,128)S(1)}, u32[]{:S(2)}, u32[]{:S(2)}) async-start(f32[16,1,896]{2,1,0:T(1,128)} %all_to_all.22), calls=%async_computation.2 | async-start | bytes 114688 | tf_op jit(solution)/shard_map/all_to_all | solution.py:1182
  750.1 73.6 %collective-permute-start.8 = (f32[176,2048]{1,0:T(8,128)S(1)}, f32[176,2048]{1,0:T(8,128)}, u32[]{:S(2)}, u32[]{:S(2)}) collective-permute-start(f32[176,2048]{1,0:T(8,128)S(1)} %get-tuple-element.48), channel_id=1, source_target_pairs={{0,1},{1,0},{2,3},{3,2},{4,5},{5,4},{6,7},{7,6},{8,9},{9,8},{10,11... | collective-permute-start | bytes 4325384 | tf_op jit(solution)/shard_map/ppermute | solution.py:1188
  756.2 2.5 copy-start.24
  760.2 46.6 %collective-permute-start.3 = (bf16[2,176,2048]{2,1,0:T(8,128)(2,1)}, bf16[2,176,2048]{2,1,0:T(8,128)(2,1)}, u32[]{:S(2)}, u32[]{:S(2)}) collective-permute-start(bf16[2,176,2048]{2,1,0:T(8,128)(2,1)} %pad_maximum_fusion.6), channel_id=1, source_target_pairs={{0,2},{1,3},{2,0},{3,1},{4,6},{5,7},{6,4},{7,5},{8,9},{9,8},{10,11... | collective-permute-start | bytes 4325384 | tf_op jit(solution)/shard_map/ppermute | solution.py:116
  809.4 11.6 %collective-permute-start.4 = (bf16[176,2048]{1,0:T(8,128)(2,1)}, bf16[176,2048]{1,0:T(8,128)(2,1)}, u32[]{:S(2)}, u32[]{:S(2)}) collective-permute-start(bf16[176,2048]{1,0:T(8,128)(2,1)} %fusion.42), channel_id=1, source_target_pairs={{0,1},{1,0},{2,3},{3,2},{4,5},{5,4},{6,7},{7,6},{8,10},{9,11},{10,... | collective-permute-start | bytes 2162696 | tf_op jit(solution)/shard_map/ppermute | solution.py:119
  810.9 9.5 %collective-permute-start.9 = (f32[2,128]{1,0:T(2,128)S(1)}, f32[2,128]{1,0:T(2,128)S(1)}, u32[]{:S(2)}, u32[]{:S(2)}) collective-permute-start(f32[2,128]{1,0:T(2,128)S(1)} %slice_bitcast_fusion.10), channel_id=1, source_target_pairs={{0,1},{1,0},{2,3},{3,2},{4,5},{5,4},{6,7},{7,6},{8,9},{9,8},{10,11... | collective-permute-start | bytes 3080 | tf_op jit(solution)/shard_map/ppermute | solution.py:1184
  813.3 7.7 copy-start.2
  823.2 10.2 %collective-permute-start.5 = (bf16[176,2048]{1,0:T(8,128)(2,1)S(1)}, bf16[176,2048]{1,0:T(8,128)(2,1)S(1)}, u32[]{:S(2)}, u32[]{:S(2)}) collective-permute-start(bf16[176,2048]{1,0:T(8,128)(2,1)S(1)} %fusion.36), channel_id=1, source_target_pairs={{0,1},{1,0},{2,3},{3,2},{4,5},{5,4},{6,7},{7,6},{8,9},{9,8},{10,11... | collective-permute-start | bytes 2162696 | tf_op jit(solution)/shard_map/ppermute | solution.py:1188
  (16 other events, 24.4 us)

commit v3 on v2

--- a/solution.py
+++ b/solution.py
@@ -1,3 +1,5 @@
+import functools
+
 import jax
 import jax.numpy as jnp
 import numpy as np
@@ -123,7 +125,6 @@
 MESH = pl.DeviceIdType.MESH
 ANY = pl.BlockSpec(memory_space=pl.ANY)
 VMEM = pl.BlockSpec(memory_space=pltpu.VMEM)
-VMEM_BYTES = 40 * 1024 * 1024
 
 
 def flip(index, by):
@@ -208,12 +209,12 @@
         self.source = source
         self.kept = None
 
-    def begin(self, zhs=(1, 0)):
+    def begin(self, zhs=(1, 0), dcs=(0, 1)):
         p = self.place
         mine = p.block()
         for f in FLIPS:
             zh, dc, zl = f
-            if zh not in zhs:
+            if zh not in zhs or dc not in dcs:
                 continue
             src, dst = self.source(p.slot(dc, zl)), self.target(mine, 1)
             if f == (0, 0, 0):
@@ -221,9 +222,9 @@
             else:
                 self.links.start(src, dst, self.at[f], p.peer(dc=dc, zh=zh, zl=zl))
 
-    def onward(self, zh):
+    def onward(self, zh, dcs=(0, 1)):
         p = self.place
-        for dc in (0, 1):
+        for dc in dcs:
             for zl in (0, 1):
                 if (zh, dc, zl) == (0, 0, 0):
                     self.kept.wait()
@@ -261,7 +262,6 @@
     crows = wo_ref.shape[0]
     greet(weight_peers(p))
     gather = TokenGatherTwice(p, links, tok_ref, all_ref)
-    gather.begin()
     w_ig = WeightGather(p, links, lambda j: ig_ref.at[j], row_blocks(wig_ref, drows), drows)
     w_o = WeightGather(
         p,
@@ -270,15 +270,16 @@
         column_blocks(wo_ref, o_ref.shape[1]),
         drows,
     )
+    w_ig.begin((1,))
     w_ig.begin((0,))
-    w_ig.begin((1,))
     w_o.begin((0,))
+    gather.begin()
     w_ig.onward(0)
+    w_o.onward(0)
     w_o.begin((1,))
-    w_o.onward(0)
+    w_ig.onward(1)
     gather.forward()
     gather.forward_core()
-    w_ig.onward(1)
     w_o.onward(1)
     gather.end()
     w_ig.end()
@@ -325,14 +326,19 @@
 
 
 class TokenGather:
-    def __init__(self, place, links, source, target):
-        self.place, self.links, self.source, self.target = place, links, source, target
+    def __init__(self, place, links, source, target, span):
+        self.place, self.links = place, links
+        self.span = pl.ds(*span)
+        self.source, self.target = source.at[self.span], target
         self.z, self.y0, self.y1 = links.pair(), links.pair(), links.pair()
         self.core = {(mp, zl): links.pair() for mp in (0, 1) for zl in (0, 1)}
 
+    def block(self, **where):
+        return self.target.at[self.place.rows(**where), self.span]
+
     def begin(self):
         p = self.place
-        at = self.target.at[p.rows()]
+        at = self.block()
         self.links.start(self.source, at, self.z, p.peer(zl=1))
         self.links.start(self.source, at, self.y0, p.peer(mp=1))
         self.links.start(self.source, at, self.core[0, 0], p.peer(dc=1))
@@ -340,90 +346,126 @@
 
     def forward(self):
         p = self.place
-        far = self.target.at[p.rows(zl=1)]
+        far = self.block(zl=1)
         self.links.arrived(far, self.z)
         self.links.start(far, far, self.y1, p.peer(mp=1))
         self.links.start(far, far, self.core[0, 1], p.peer(dc=1))
 
     def forward_core(self):
         p = self.place
-        far = self.target.at[p.rows(mp=1)]
+        far = self.block(mp=1)
         self.links.arrived(far, self.y0)
         self.links.start(far, far, self.core[1, 0], p.peer(dc=1))
-        far = self.target.at[p.rows(mp=1, zl=1)]
+        far = self.block(mp=1, zl=1)
         self.links.arrived(far, self.y1)
         self.links.start(far, far, self.core[1, 1], p.peer(dc=1))
 
     def end(self):
-        p = self.place
         for (mp, zl), at in self.core.items():
-            self.links.arrived(self.target.at[p.rows(dc=1, mp=mp, zl=zl)], at)
+            self.links.arrived(self.block(dc=1, mp=mp, zl=zl), at)
         self.kept.wait()
 
 
 CHUNK = 16
 
 
-def chunks(count, body):
+def chunks(count, body, most=11, first=0):
+    n = count // CHUNK
+    per = max(k for k in range(1, most + 1) if n % k == 0)
+
     def step(i, carry):
-        body(pl.ds(pl.multiple_of(i * CHUNK, CHUNK), CHUNK))
+        for k in range(per):
+            body(pl.ds(pl.multiple_of(first + (i * per + k) * CHUNK, CHUNK), CHUNK))
         return carry
 
-    lax.fori_loop(0, count // CHUNK, step, 0)
+    if n == per:
+        step(0, 0)
+    else:
+        lax.fori_loop(0, n // per, step, 0)
+
+
+def halves(rows):
+    first = (rows // 2 + CHUNK - 1) // CHUNK * CHUNK
+    return [(0, first), (first, rows - first)]
 
 
 class RowScatter:
-    def __init__(self, place, links, source, buffers):
+    def __init__(self, place, links, source, buffers, parts=None):
         self.place, self.links, self.source = place, links, source
-        self.mine, self.from_core, self.from_y, self.from_z, self.out = buffers
-        self.core = {(mp, zl): links.pair() for mp in (1, 0) for zl in (1, 0)}
-        self.y = {zl: links.pair() for zl in (1, 0)}
-        self.z = links.pair()
+        self.mine, self.from_core, self.from_y, self.from_z, self.out = buffers[:5]
+        self.to_core = buffers[5] if len(buffers) > 5 else None
+        self.parts = parts or [(0, self.mine.shape[1])]
+        self.blocks = [(mp, zl) for mp in (1, 0) for zl in (1, 0)]
+        n = range(len(self.parts))
+        self.core = {(h, block): links.pair() for h in n for block in self.blocks}
+        self.y = {(h, zl): links.pair() for h in n for zl in (1, 0)}
+        self.z = {h: links.pair() for h in n}
 
     def begin(self):
         p = self.place
         self.kept = {}
-        for (mp, zl), at in self.core.items():
-            src = self.source.at[p.rows(dc=1, mp=mp, zl=zl)]
-            self.links.start(src, self.from_core.at[mp * 2 + zl], at, p.peer(dc=1))
-        for mp, zl in self.core:
-            src = self.source.at[p.rows(mp=mp, zl=zl)]
-            self.kept[mp, zl] = self.links.keep(src, self.mine.at[mp * 2 + zl])
-
-    def ready(self, mp, zl):
+        for mp, zl in self.blocks:
+            i, block = mp * 2 + zl, p.rows(dc=1, mp=mp, zl=zl)
+            if self.to_core is None:
+                src = self.source.at[block]
+            else:
+                self.to_core[i] = self.source(block).astype(BF)
+                src = self.to_core.at[i]
+            for h, part in enumerate(self.parts):
+                at = pl.ds(*part)
+                self.links.start(
+                    src.at[at], self.from_core.at[i, at], self.core[h, (mp, zl)], p.peer(dc=1)
+                )
+        for mp, zl in self.blocks:
+            i, block = mp * 2 + zl, p.rows(mp=mp, zl=zl)
+            if self.to_core is None:
+                self.kept[mp, zl] = self.links.keep(self.source.at[block], self.mine.at[i])
+            else:
+                self.mine[i] = self.source(block).astype(BF)
+
+    def ready(self, mp, zl, h):
         i = mp * 2 + zl
-        self.kept[mp, zl].wait()
-        self.links.arrived(self.from_core.at[i], self.core[mp, zl])
+        if h == 0 and self.kept:
+            self.kept[mp, zl].wait()
+        at = pl.ds(*self.parts[h])
+        self.links.arrived(self.from_core.at[i, at], self.core[h, (mp, zl)])
         return i
 
-    def across_y(self):
+    def across_y(self, h=0):
         p = self.place
+        first, count = self.parts[h]
+        at = pl.ds(first, count)
         for zl in (1, 0):
-            i = self.ready(1, zl)
+            i = self.ready(1, zl, h)
 
             def add(rows, i=i, zl=zl):
                 total = self.mine[i, rows, :].astype(F32) + self.from_core[i, rows, :].astype(F32)
                 self.out[zl, rows, :] = total.astype(BF)
 
-            chunks(self.mine.shape[1], add)
-            self.links.start(self.out.at[zl], self.from_y.at[zl], self.y[zl], p.peer(mp=1))
-
-    def across_z(self):
+            chunks(count, add, first=first)
+            self.links.start(
+                self.out.at[zl, at], self.from_y.at[zl, at], self.y[h, zl], p.peer(mp=1)
+            )
+
+    def across_z(self, h=0):
         p = self.place
-        i = self.ready(0, 1)
-        self.links.arrived(self.from_y.at[1], self.y[1])
+        first, count = self.parts[h]
+        at = pl.ds(first, count)
+        i = self.ready(0, 1, h)
+        self.links.arrived(self.from_y.at[1, at], self.y[h, 1])
 
         def add(rows):
             total = self.mine[i, rows, :].astype(F32) + self.from_core[i, rows, :].astype(F32)
             self.out[2, rows, :] = (total + self.from_y[1, rows, :].astype(F32)).astype(BF)
 
-        chunks(self.mine.shape[1], add)
-        self.links.start(self.out.at[2], self.from_z, self.z, p.peer(zl=1))
-
-    def arrive(self):
-        self.ready(0, 0)
-        self.links.arrived(self.from_y.at[0], self.y[0])
-        self.links.arrived(self.from_z, self.z)
+        chunks(count, add, first=first)
+        self.links.start(self.out.at[2, at], self.from_z.at[at], self.z[h], p.peer(zl=1))
+
+    def arrive(self, h=0):
+        at = pl.ds(*self.parts[h])
+        self.ready(0, 0, h)
+        self.links.arrived(self.from_y.at[0, at], self.y[h, 0])
+        self.links.arrived(self.from_z.at[at], self.z[h])
 
     def total(self, rows):
         a = self.mine[0, rows, :].astype(F32) + self.from_core[0, rows, :].astype(F32)
@@ -431,14 +473,14 @@
         return a + b
 
 
-def scatter_buffers(rows, width):
+def scatter_buffers(rows, width, products=False):
     return [
         pltpu.VMEM((4, rows, width), BF),
         pltpu.VMEM((4, rows, width), BF),
         pltpu.VMEM((2, rows, width), BF),
         pltpu.VMEM((rows, width), BF),
         pltpu.VMEM((3, rows, width), BF),
-    ]
+    ] + ([pltpu.VMEM((4, rows, width), BF)] if products else [])
 
 
 def group_peers(p):
@@ -453,129 +495,143 @@
 
 
 def second_kernel(
-    part_ref, own_ref, gain_ref, cot_ref, gate_ref, up_ref, down_ref,
-    mid_ref, all_ref, dm_ref, wgu_ref, wd_ref,
-    mine, from_core, from_y, from_z, out, normed, send, recv, local,
+    mixed_ref, wo_ref, own_ref, gain_ref, up_ref, down_ref,
+    mid_ref, all_ref, wu_ref, wd_ref,
+    *scratch,
 ):
     p = Place()
-    links = Links(send, recv, local)
-    drows, ff = gate_ref.shape[0], wd_ref.shape[0]
+    links = Links(*scratch[-3:])
+    normed = scratch[-4]
+    rows, channels = own_ref.shape[0], wo_ref.shape[0]
     greet(weight_peers(p))
-    scatter = RowScatter(p, links, part_ref, (mine, from_core, from_y, from_z, out))
-    scatter.begin()
-
-    def wide(ref, at):
-        return WeightGather(
-            p,
-            links,
-            lambda j: ref.at[:, pl.ds(pl.multiple_of(j * ff, 128), ff)],
-            row_blocks(wgu_ref, drows, pl.ds(at, ff)),
-            drows,
-        )
-
-    w_g, w_u = wide(gate_ref, 0), wide(up_ref, ff)
+
+    def project(b):
+        at = pl.ds(pl.multiple_of(b * rows, 16), rows)
+        return dot(mixed_ref[at, :channels], wo_ref[...], NN)
+
+    parts = halves(rows)
+    scatter = RowScatter(p, links, project, scratch[:6], parts)
+    w_u = slot_columns(p, links, up_ref, wu_ref)
     w_d = WeightGather(
         p,
         links,
-        lambda j: down_ref.at[pl.ds(pl.multiple_of(j * ff, 16), ff)],
+        lambda j: down_ref.at[pl.ds(pl.multiple_of(j * wd_ref.shape[0], 16), wd_ref.shape[0])],
         column_blocks(wd_ref, down_ref.shape[1]),
-        drows,
-    )
-    w_g.begin((0,))
-    w_g.begin((1,))
+        down_ref.shape[1],
+    )
+    gathers = [TokenGather(p, links, normed, all_ref, part) for part in parts]
+    scatter.begin()
+    w_u.begin((1,))
     w_u.begin((0,))
+    scatter.across_y(0)
+    scatter.across_y(1)
     w_d.begin((0,))
-    scatter.across_y()
-    w_u.begin((1,))
-    w_g.onward(0)
     w_u.onward(0)
+
+    def normalise(at):
+        value = own_ref[at, :].astype(F32) + scatter.total(at)
+        mid_ref[at, :] = value
+        inv = lax.rsqrt(jnp.mean(value * value, axis=-1, keepdims=True) + EPSILON)
+        normed[at, :] = (value * inv * gain_ref[...]).astype(BF)
+
+    def middle(h):
+        scatter.arrive(h)
+        chunks(parts[h][1], normalise, first=parts[h][0])
+        gathers[h].begin()
+
+    scatter.across_z(0)
     w_d.onward(0)
-    scatter.across_z()
-    scatter.arrive()
-
-    def normalise(rows):
-        value = own_ref[rows, :].astype(F32) + scatter.total(rows)
-        mid_ref[rows, :] = value
-        inv = lax.rsqrt(jnp.mean(value * value, axis=-1, keepdims=True) + EPSILON)
-        normed[rows, :] = (value * inv * gain_ref[...]).astype(BF)
-
-    chunks(own_ref.shape[0], normalise)
-    gather = TokenGather(p, links, normed, all_ref)
-    gather.begin()
+    scatter.across_z(1)
+    middle(0)
     w_d.begin((1,))
-    w_g.onward(1)
-    gather.forward()
-    adjoint = TokenGatherTwice(p, links, cot_ref, dm_ref)
-    adjoint.begin()
-    gather.forward_core()
+    middle(1)
+    gathers[0].forward()
     w_u.onward(1)
-    adjoint.forward()
-    adjoint.forward_core()
+    gathers[1].forward()
+    gathers[0].forward_core()
+    gathers[1].forward_core()
     w_d.onward(1)
-    gather.end()
-    adjoint.end()
-    w_g.end()
+    for gather in gathers:
+        gather.end()
     w_u.end()
     w_d.end()
     links.finish()
 
 
+def slot_columns(p, links, source, result):
+    count = result.shape[1]
+    return WeightGather(
+        p,
+        links,
+        lambda j: source.at[:, pl.ds(pl.multiple_of(j * count, 128), count)],
+        row_blocks(result, source.shape[0]),
+        source.shape[0],
+    )
+
+
 class GradScatter:
-    def __init__(self, place, links, source, result, by_rows, buffers):
-        self.place, self.links, self.source, self.result = place, links, source, result
-        self.by_rows = by_rows
-        self.mine, self.from_x, self.to_z, self.from_z, self.sums = buffers
+    FAR = [(1, 0, 1), (1, 1, 1)], [(1, 0, 0), (1, 1, 0)]
+    NEAR = [(0, 0, 1), (0, 1, 1)], [(0, 0, 0), (0, 1, 0)]
+    ORDER = FAR[0] + NEAR[0] + FAR[1] + NEAR[1]
+    EARLY = FAR[0] + FAR[1] + NEAR[0] + NEAR[1]
+
+    def __init__(self, place, links, left, right, buffers, order=ORDER):
+        self.order = order
+        self.place, self.links, self.left, self.right = place, links, left, right
+        self.to_x, self.from_x, self.to_z, self.from_z, self.sums, self.result = buffers[:6]
+        self.columns = buffers[6] if len(buffers) > 6 else None
+        self.rows = self.to_x.shape[1]
         self.x = {(zh, dc): links.pair() for zh in (1, 0) for dc in (0, 1)}
         self.z = {dc: links.pair() for dc in (0, 1)}
         self.at = {(dc, zl): links.pair() for dc in (0, 1) for zl in (0, 1)}
-        self.kept = {}
+        self.count = 0
+        self.load()
+
+    def load(self):
+        if self.count < 8 and self.columns is not None:
+            dx, dc, zh = self.order[self.count]
+            first = self.place.block(dx=dx, dc=dc, zh=zh) // 2
+            columns = pl.ds(pl.multiple_of(first * self.rows, self.rows), self.rows)
+            self.loading = self.links.keep(
+                self.left.at[:, columns], self.columns.at[self.count % 2]
+            )
+
+    def product(self, dx=0, dc=0, zh=0):
+        assert self.order[self.count] == (dx, dc, zh)
+        self.loading.wait()
+        self.count += 1
+        self.load()
+        return dot(self.columns[(self.count - 1) % 2], self.right[...], TN)
 
     def begin(self, zh):
-        p = self.place
         for dc in (0, 1):
             i = zh * 2 + dc
-            theirs = self.source(p.block(dx=1, dc=dc, zh=zh) // 2 * 2, 2)
-            self.links.start(theirs, self.from_x.at[i], self.x[zh, dc], p.peer(dx=1))
-            mine = self.source(p.block(dc=dc, zh=zh) // 2 * 2, 2)
-            self.kept[zh, dc] = self.links.keep(mine, self.mine.at[i])
-
-    def ready(self, zh, dc):
-        self.kept[zh, dc].wait()
-        self.links.arrived(self.from_x.at[zh * 2 + dc], self.x[zh, dc])
-        return zh * 2 + dc
+            self.to_x[i] = self.product(dx=1, dc=dc, zh=zh).astype(BF)
+            self.links.start(
+                self.to_x.at[i], self.from_x.at[i], self.x[zh, dc], self.place.peer(dx=1)
+            )
 
     def across(self, dc):
-        i = self.ready(1, dc)
-
-        def add(rows):
-            total = self.mine[i, rows, :].astype(F32) + self.from_x[i, rows, :].astype(F32)
-            self.to_z[dc, rows, :] = total.astype(BF)
-
-        chunks(self.mine.shape[1], add)
+        mine = self.product(dc=dc, zh=1)
+        self.links.arrived(self.from_x.at[2 + dc], self.x[1, dc])
+        self.to_z[dc] = (mine + self.from_x[2 + dc].astype(F32)).astype(BF)
         self.links.start(self.to_z.at[dc], self.from_z.at[dc], self.z[dc], self.place.peer(zh=1))
 
     def last(self, dc):
         p = self.place
-        i = self.ready(0, dc)
+        mine = self.product(dc=dc, zh=0)
+        self.links.arrived(self.from_x.at[dc], self.x[0, dc])
         self.links.arrived(self.from_z.at[dc], self.z[dc])
-
-        def add(rows):
-            total = self.mine[i, rows, :].astype(F32) + self.from_x[i, rows, :].astype(F32)
-            self.sums[dc, rows, :] = (total + self.from_z[dc, rows, :].astype(F32)).astype(BF)
-
-        chunks(self.mine.shape[1], add)
+        total = mine + self.from_x[dc].astype(F32) + self.from_z[dc].astype(F32)
+        self.sums[dc] = total.astype(BF)
+        unit = self.rows // 2
         for zl in (1, 0):
-            src = self.one(dc, flip(p.zl, zl))
+            src = self.sums.at[dc, pl.ds(pl.multiple_of(flip(p.zl, zl) * unit, unit), unit)]
             dst = self.result.at[p.slot()]
             if (dc, zl) == (0, 0):
                 self.own = self.links.keep(src, dst)
             else:
                 self.links.start(src, dst, self.at[dc, zl], p.peer(dc=dc, zl=zl))
-
-    def one(self, dc, zl):
-        unit = self.result.shape[1] if self.by_rows else self.result.shape[2]
-        span = pl.ds(pl.multiple_of(zl * unit, unit), unit)
-        return self.sums.at[dc, span] if self.by_rows else self.sums.at[dc, :, span]
 
     def end(self):
         p = self.place
@@ -586,11 +642,20 @@
                 self.links.arrived(self.result.at[p.slot(dc, zl)], at)
 
 
-def grad_buffers(rows, columns):
-    return [
-        pltpu.VMEM((n, rows, columns), BF)
-        for n in (4, 4, 2, 2, 2)
-    ]
+class Ready(GradScatter):
+    def product(self, dx=0, dc=0, zh=0):
+        first = self.place.block(dx=dx, dc=dc, zh=zh) // 2
+        return self.left[pl.ds(pl.multiple_of(first * self.rows, self.rows), self.rows), :].astype(
+            F32
+        )
+
+
+def grad_buffers(rows, columns, tokens=None):
+    return (
+        [pltpu.VMEM((n, rows, columns), BF) for n in (4, 4, 2, 2, 2)]
+        + [pltpu.VMEM((4, rows // 2, columns), BF)]
+        + ([pltpu.VMEM((2, tokens, rows), BF)] if tokens else [])
+    )
 
 
 def norm_back(value, gain, upstream):
@@ -606,28 +671,33 @@
 
 
 def third_kernel(
-    part_ref, mid_ref, dout_ref, gain_ref, gd_ref, ggu_ref,
-    dr1_ref, gain_out, all_ref, sd_ref, sgu_ref,
+    wg_ref, wu_ref, wd_ref, mid_ref, dout_ref, gain_ref, dm_ref, hidden_ref, n2_ref, dgm_ref,
+    dup_ref,
+    dr1_ref, gain_out, all_ref, gate_out, down_out, part_out,
     *scratch,
 ):
     p = Place()
     links = Links(*scratch[-3:])
     do = scratch[-4]
-    unit = sgu_ref.shape[1]
+    rows_of = mid_ref.shape[0]
     greet(weight_peers(p))
-    scatter = RowScatter(p, links, part_ref, scratch[:5])
-    down = GradScatter(p, links, column_blocks(gd_ref, unit), sd_ref, False, scratch[5:10])
-    wide = GradScatter(p, links, row_blocks(ggu_ref, unit), sgu_ref, True, scratch[10:15])
+
+    def product(b):
+        at = pl.ds(pl.multiple_of(b * rows_of, 16), rows_of)
+        return dot(dgm_ref[at, :], wg_ref[...], NT) + dot(dup_ref[at, :], wu_ref[...], NT)
+
+    parts = halves(rows_of)
+    scatter = RowScatter(p, links, product, scratch[:6], parts)
+    down = GradScatter(p, links, dm_ref, hidden_ref, scratch[6:13])
+    gate = GradScatter(p, links, n2_ref, dgm_ref, scratch[13:20])
+    gathers = [TokenGather(p, links, do, all_ref, part) for part in parts]
     scatter.begin()
     down.begin(1)
-    wide.begin(1)
-    scatter.across_y()
+    scatter.across_y(0)
+    scatter.across_y(1)
+    gate.begin(1)
     down.across(0)
     down.across(1)
-    down.begin(0)
-    wide.across(0)
-    scatter.across_z()
-    scatter.arrive()
     gain_out[...] = jnp.zeros_like(gain_out)
 
     def back(rows):
@@ -637,67 +707,174 @@
         do[rows, :] = value.astype(BF)
         gain_out[...] += fold(gain)
 
-    chunks(mid_ref.shape[0], back)
-    gather = TokenGather(p, links, do, all_ref)
-    gather.begin()
-    wide.across(1)
-    wide.begin(0)
-    gather.forward()
+    def middle(h):
+        scatter.arrive(h)
+        chunks(parts[h][1], back, first=parts[h][0])
+        gathers[h].begin()
+
+    scatter.across_z(0)
+    down.begin(0)
+    gate.across(0)
+    scatter.across_z(1)
+    middle(0)
+    gate.across(1)
+    gate.begin(0)
+    middle(1)
+    gathers[0].forward()
+    gathers[1].forward()
+    out = scratch[0]
+    writes = []
+    for b in range(8):
+        if b >= 4:
+            writes[b - 4].wait()
+        at = pl.ds(b * rows_of, rows_of)
+        out[b % 4] = dot(hidden_ref[at, :], wd_ref[...], NN, BF)
+        writes.append(links.keep(out.at[b % 4], part_out.at[b]))
     down.last(0)
     down.last(1)
-    gather.forward_core()
-    wide.last(0)
-    wide.last(1)
-    gather.end()
+    gathers[0].forward_core()
+    gate.last(0)
+    gathers[1].forward_core()
+    gate.last(1)
+    for gather in gathers:
+        gather.end()
     down.end()
-    wide.end()
+    ff = down.result.shape[2]
+    for j in range(4):
+        down_out[j * ff : (j + 1) * ff, :] = down.result[j].astype(F32).T
+    gate.end()
+    for j in range(4):
+        gate_out[:, j * ff : (j + 1) * ff] = gate.result[j].astype(F32)
+    for write in writes[4:]:
+        write.wait()
     links.finish()
 
 
 def fourth_kernel(
-    part_ref, own_ref, dr1_ref, gain_ref, go_ref, gig_ref, gg_ref,
-    dx_ref, gain_out, so_ref, sig_ref, sg_ref,
+    wig_ref, own_ref, dr1_ref, gain_ref, do_ref, mixed_ref, n1_ref, dboth_ref, gg_ref,
+    dx_ref, gain_out, in_out, gelu_out, out_out, gates_out,
     *scratch,
 ):
     p = Place()
     links = Links(*scratch[-3:])
+    dx_send, dx_recv = scratch[-5:-3]
     greet(weight_peers(p))
-    scatter = RowScatter(p, links, part_ref, scratch[:5])
-    out = GradScatter(
-        p, links, column_blocks(go_ref, so_ref.shape[2]), so_ref, False, scratch[5:10]
-    )
-    wide = GradScatter(
-        p, links, row_blocks(gig_ref, sig_ref.shape[1]), sig_ref, True, scratch[10:15]
-    )
-    gates = GradScatter(p, links, row_blocks(gg_ref, sg_ref.shape[1]), sg_ref, True, scratch[15:20])
-    grads = (out, wide, gates)
-    for g in grads:
-        g.begin(1)
+    rows_of = own_ref.shape[0]
+
+    def product(b):
+        at = pl.ds(pl.multiple_of(b * rows_of, 16), rows_of)
+        return dot(dboth_ref[at, :], wig_ref[...], NT)
+
+    parts = halves(rows_of)
+    scatter = RowScatter(p, links, product, scratch[:6], parts)
+    out = GradScatter(p, links, do_ref, mixed_ref, scratch[6:13])
+    wide = GradScatter(p, links, n1_ref, dboth_ref, scratch[13:20])
+    gates = Ready(p, links, gg_ref, None, scratch[20:26])
+    out.begin(1)
     scatter.begin()
-    for g in grads:
+    wide.begin(1)
+    scatter.across_y(0)
+    gates.begin(1)
+    scatter.across_y(1)
+    for g in (out, wide, gates):
         g.across(0)
         g.across(1)
         g.begin(0)
-    scatter.across_y()
+    gain_out[...] = jnp.zeros_like(gain_out)
+
+    def back(rows):
+        value = own_ref[rows, :].astype(F32)
+        part, gain = norm_back(value, gain_ref[...], scatter.total(rows))
+        total = dr1_ref[rows, :] + part
+        dx_ref[p.mp, rows, :] = total
+        dx_send[rows, :] = total.astype(BF)
+        gain_out[...] += fold(gain)
+
+    sent = []
+
+    def middle(h):
+        scatter.arrive(h)
+        chunks(parts[h][1], back, first=parts[h][0])
+        span, at = pl.ds(*parts[h]), links.pair()
+        links.start(dx_send.at[span], dx_recv.at[span], at, p.peer(mp=1))
+        sent.append((span, at))
+
+    scatter.across_z(0)
+    scatter.across_z(1)
+    middle(0)
     for g in (out, gates):
         g.last(0)
         g.last(1)
-    scatter.across_z()
+    middle(1)
     wide.last(0)
     wide.last(1)
-    scatter.arrive()
-    gain_out[...] = jnp.zeros_like(gain_out)
-
-    def back(rows):
-        value = own_ref[rows, :].astype(F32)
-        part, gain = norm_back(value, gain_ref[...], scatter.total(rows))
-        dx_ref[rows, :] = dr1_ref[rows, :] + part
-        gain_out[...] += fold(gain)
-
-    chunks(own_ref.shape[0], back)
-    for g in grads:
-        g.end()
+    local = out.result.shape[2]
+    out.end()
+    for j in range(4):
+        out_out[j * out_out.shape[0] // 4 : (j + 1) * out_out.shape[0] // 4, :] = (
+            out.result[j].astype(F32).T[: out_out.shape[0] // 4]
+        )
+    gates.end()
+    gates_out[...] = gates.result[...]
+    wide.end()
+    two = wide.result.shape[2]
+    left = lax.broadcasted_iota(jnp.int32, (1, two), 1) < two // 2
+    for j in (0, 2):
+        a, b = (wide.result[j + i].astype(F32) for i in (0, 1))
+        span = slice(j * two // 2, (j + 2) * two // 2)
+        in_out[:, span] = jnp.where(left, a, pltpu.roll(b, two // 2, 1))
+        gelu_out[:, span] = jnp.where(left, pltpu.roll(a, two // 2, 1), b)
+    for span, at in sent:
+        links.arrived(dx_recv.at[span], at)
+    dx_ref[1 - p.mp] = dx_recv[...].astype(F32)
     links.finish()
+
+
+def mlp_kernel(
+    n2_ref, dm_ref, wg_ref, wu_ref, wd_ref, hidden_ref, dgm_ref, dup_ref, pre, upp, dhm
+):
+    count, rows, width = n2_ref.shape
+    n2 = n2_ref[...].reshape(count * rows, width)
+    pre[...] = dot(n2, wg_ref[...], NN)
+    upp[...] = dot(n2, wu_ref[...], NN)
+    dhm[...] = dot(dm_ref[...].reshape(count * rows, width), wd_ref[...], NT)
+
+    def body(at):
+        up, d = upp[at, :], dhm[at, :]
+        value, slope = gelu_both(pre[at, :])
+        hidden_ref[at, :] = (value * up).astype(BF)
+        dgm_ref[at, :] = (d * up * slope).astype(BF)
+        dup_ref[at, :] = (d * value).astype(BF)
+
+    chunks(count * rows, body)
+
+
+def feed_forward(n2, dm, w_g, w_u, w_d):
+    blocks, rows, width = n2.shape
+    ff = w_d.shape[0]
+    if not shape_fits():
+        n2, dm = n2.reshape(-1, width), dm.reshape(-1, width)
+        pre, d = dot(n2, w_g, NN), dot(dm, w_d, NT)
+        gm, up = pre, dot(n2, w_u, NN)
+        value, slope = gelu_both(gm)
+        return (value * up).astype(BF), (d * up * slope).astype(BF), (d * value).astype(BF)
+    two = pl.BlockSpec((2, rows, width), lambda i: (i, 0, 0))
+    flat = pl.BlockSpec((2 * rows, ff), lambda i: (i, 0))
+    whole = lambda v: pl.BlockSpec(v.shape, lambda i: (0, 0))
+    total = blocks * rows
+    return pl.pallas_call(
+        mlp_kernel,
+        name="feed_forward",
+        grid=(blocks // 2,),
+        in_specs=[two, two, whole(w_g), whole(w_u), whole(w_d)],
+        out_specs=[flat] * 3,
+        out_shape=[jax.ShapeDtypeStruct((total, ff), BF)] * 3,
+        scratch_shapes=[pltpu.VMEM((2 * rows, ff), F32)] * 3,
+        compiler_params=pltpu.CompilerParams(vmem_limit_bytes=48 * 1024 * 1024),
+        cost_estimate=pl.CostEstimate(
+            flops=2 * total * width * ff * 3, bytes_accessed=total * width * 4, transcendentals=0
+        ),
+    )(n2, dm, w_g, w_u, w_d)
 
 
 def semaphores(pairs, local):
@@ -708,7 +885,7 @@
     ]
 
 
-def run_kernel(body, name, outs, out_specs, in_specs, scratch, ident, args):
+def run_kernel(body, name, outs, out_specs, in_specs, scratch, ident, args, mib=40):
     return pl.pallas_call(
         body,
         name=name,
@@ -717,7 +894,7 @@
         out_specs=out_specs,
         scratch_shapes=scratch,
         compiler_params=pltpu.CompilerParams(
-            collective_id=ident, has_side_effects=True, vmem_limit_bytes=VMEM_BYTES
+            collective_id=ident, has_side_effects=True, vmem_limit_bytes=mib * 1024 * 1024
         ),
     )(*args)
 
@@ -741,34 +918,30 @@
     )
 
 
-def reduce_and_fetch(part, own, gain, dm, mlp_gate, mlp_up, mlp_down):
+def reduce_and_fetch(mixed, w_o, own, gain, mlp_up, mlp_down):
     if not shape_fits():
-        return plain_reduce_and_fetch(part, own, gain, dm, mlp_gate, mlp_up, mlp_down)
+        return plain_reduce_and_fetch(mixed, w_o, own, gain, mlp_up, mlp_down)
     rows, width = own.shape
-    ff = mlp_gate.shape[1] // 4
+    ff = mlp_up.shape[1] // 4
     return run_kernel(
         second_kernel,
         "reduce_and_fetch",
-        [
-            ((rows, width), F32),
-            ((8, rows, width), BF),
-            ((8, rows, width), BF),
-            ((width, 2 * ff), BF),
-            ((ff, width), BF),
-        ],
-        [VMEM] + [ANY] * 4,
-        [ANY, VMEM, VMEM] + [ANY] * 4,
-        scatter_buffers(rows, width) + [pltpu.VMEM((rows, width), BF)] + semaphores(64, 16),
+        [((rows, width), F32), ((8, rows, width), BF), ((width, ff), BF), ((ff, width), BF)],
+        [VMEM] + [ANY] * 3,
+        [VMEM] * 4 + [ANY] * 2,
+        scatter_buffers(rows, width, True) + [pltpu.VMEM((rows, width), BF)] + semaphores(64, 16),
         2,
-        (part.reshape(8, rows, width), own, gain, dm, mlp_gate, mlp_up, mlp_down),
-    )
-
-
-def reduce_and_return(part, middle, dout, gain, g_down, g_wide, drows):
+        (mixed, w_o, own, gain, mlp_up, mlp_down),
+    )
+
+
+def reduce_and_return(weights, middle, dout, gain, dm, hidden, n2, dgm, dup, drows):
     if not shape_fits():
-        return plain_reduce_and_return(part, middle, dout, gain, g_down, g_wide, drows)
+        return plain_reduce_and_return(
+            weights, middle, dout, gain, dm, hidden, n2, dgm, dup, drows
+        )
     rows, width = middle.shape
-    ff = g_down.shape[0]
+    ff = hidden.shape[1]
     return run_kernel(
         third_kernel,
         "reduce_and_return",
@@ -776,45 +949,49 @@
             ((rows, width), F32),
             ((8, width), F32),
             ((8, rows, width), BF),
-            ((4, ff, drows), BF),
-            ((4, drows, g_wide.shape[1]), BF),
+            ((drows, 4 * ff), F32),
+            ((4 * ff, drows), F32),
+            ((8, rows, width), BF),
         ],
-        [VMEM, VMEM] + [ANY] * 3,
-        [ANY] + [VMEM] * 3 + [ANY] * 2,
-        scatter_buffers(rows, width)
-        + grad_buffers(ff, 2 * drows)
-        + grad_buffers(2 * drows, g_wide.shape[1])
+        [VMEM, VMEM, ANY] + [VMEM] * 2 + [ANY],
+        [VMEM] * 6 + [ANY, VMEM] * 2 + [VMEM],
+        scatter_buffers(rows, width, True)
+        + grad_buffers(2 * drows, ff, 8 * rows) * 2
         + [pltpu.VMEM((rows, width), BF)]
-        + semaphores(40, 24),
+        + semaphores(56, 48),
         3,
-        (part.reshape(8, rows, width), middle, dout, gain, g_down, g_wide),
-    )
-
-
-def return_last(part, own, dr1, gain, g_out, g_wide, g_gates, drows):
+        (*weights, middle, dout, gain, dm, hidden, n2, dgm, dup),
+        61,
+    )
+
+
+def return_last(w_ig, own, dr1, gain, do, mixed, n1, dboth, g_gates, drows):
     if not shape_fits():
-        return plain_return_last(part, own, dr1, gain, g_out, g_wide, g_gates, drows)
+        return plain_return_last(w_ig, own, dr1, gain, do, mixed, n1, dboth, g_gates, drows)
     rows, width = own.shape
-    local, unit = g_out.shape[0], g_gates.shape[0] // 16
+    local, unit = dboth.shape[1] // 2, g_gates.shape[0] // 16
     return run_kernel(
         fourth_kernel,
         "return_last",
         [
-            ((rows, width), F32),
+            ((2, rows, width), F32),
             ((8, width), F32),
-            ((4, local, drows), BF),
-            ((4, drows, g_wide.shape[1]), BF),
+            ((drows, 4 * local), F32),
+            ((drows, 4 * local), F32),
+            ((4 * local, drows), F32),
             ((4, unit, 128), BF),
         ],
-        [VMEM, VMEM] + [ANY] * 3,
-        [ANY] + [VMEM] * 3 + [ANY] * 3,
-        scatter_buffers(rows, width)
-        + grad_buffers(local, 2 * drows)
-        + grad_buffers(2 * drows, g_wide.shape[1])
+        [VMEM] * 6,
+        [VMEM] * 4 + [ANY, VMEM] * 2 + [VMEM],
+        scatter_buffers(rows, width, True)
+        + grad_buffers(2 * drows, mixed.shape[1], 8 * rows)
+        + grad_buffers(2 * drows, 2 * local, 8 * rows)
         + grad_buffers(2 * unit, 128)
-        + semaphores(48, 32),
+        + [pltpu.VMEM((rows, width), BF)] * 2
+        + semaphores(64, 48),
         4,
-        (part.reshape(8, rows, width), own, dr1, gain, g_out, g_wide, g_gates),
+        (w_ig, own, dr1, gain, do, mixed, n1, dboth, g_gates),
+        60,
     )
 
 
@@ -832,42 +1009,61 @@
     )
 
 
-def plain_reduce_and_fetch(part, own, gain, dm, mlp_gate, mlp_up, mlp_down):
+def plain_reduce_and_fetch(mixed, w_o, own, gain, mlp_up, mlp_down):
     exchange = Tokens()
-    middle = own.astype(F32) + exchange.scatter(part)
+    middle = own.astype(F32) + exchange.scatter(dot(mixed, w_o, NN, BF))
     normed = (middle * inverse_rms(middle) * gain).astype(BF)
-    dm = lax.dynamic_index_in_dim(dm, exchange.mp, 0, keepdims=False)
     return (
         middle,
         exchange.gather(normed).reshape((8,) + own.shape),
-        exchange.gather(dm).reshape((8,) + own.shape),
-        fetch_weight([mlp_gate, mlp_up], 4),
+        fetch_weight([mlp_up], 4),
         fetch_weight([mlp_down.T], 4).T,
     )
 
 
-def plain_reduce_and_return(part, middle, dout, gain, g_down, g_wide, drows):
+def columns(share, at, count):
+    return share[:, :, at : at + count].astype(F32).transpose(1, 0, 2).reshape(-1, 4 * count)
+
+
+def both_batches(rows):
+    mp = lax.axis_index("mp")
+    other = lax.ppermute(rows, "mp", [(0, 1), (1, 0)])
+    return jnp.stack([jnp.where(mp == 0, rows, other), jnp.where(mp == 0, other, rows)])
+
+
+def plain_reduce_and_return(weights, middle, dout, gain, dm, hidden, n2, dgm, dup, drows):
     exchange = Tokens()
-    change, gain_rows = norm_back(middle, gain, exchange.scatter(part))
+    w_g, w_u, w_d = weights
+    ff = hidden.shape[1]
+    total = exchange.scatter((dot(dgm, w_g, NT) + dot(dup, w_u, NT)).astype(BF))
+    change, gain_rows = norm_back(middle, gain, total)
     dr1 = dout + change
+    gate = return_grad(dot(n2, dgm, TN, BF), drows)
+    down = return_grad(dot(dm, hidden, TN, BF), drows)
     return (
         dr1,
         jnp.sum(gain_rows, axis=0, keepdims=True),
         exchange.gather(dr1.astype(BF)).reshape((8,) + dr1.shape),
-        return_grad(g_down.T, drows).transpose(0, 2, 1),
-        return_grad(g_wide, drows),
-    )
-
-
-def plain_return_last(part, own, dr1, gain, g_out, g_wide, g_gates, drows):
+        columns(gate, 0, ff),
+        columns(down, 0, ff).T,
+        dot(hidden, w_d, NN, BF).reshape((8,) + dr1.shape),
+    )
+
+
+def plain_return_last(w_ig, own, dr1, gain, do, mixed, n1, dboth, g_gates, drows):
     exchange = Tokens()
-    change, gain_rows = norm_back(own.astype(F32), gain, exchange.scatter(part))
-    group = g_wide.shape[0] // drows
+    local = dboth.shape[1] // 2
+    total = exchange.scatter(dot(dboth, w_ig, NT, BF))
+    change, gain_rows = norm_back(own.astype(F32), gain, total)
+    group = n1.shape[1] // drows
+    wide = return_grad(dot(n1, dboth, TN, BF), drows)
+    out = return_grad(dot(do, mixed, TN, BF), drows)
     return (
-        dr1 + change,
+        both_batches(dr1 + change),
         jnp.sum(gain_rows, axis=0, keepdims=True),
-        return_grad(g_out.T, drows).transpose(0, 2, 1),
-        return_grad(g_wide, drows),
+        columns(wide, 0, local),
+        columns(wide, local, local),
+        columns(out, 0, local).T,
         return_grad(g_gates, g_gates.shape[0] // group),
     )
 
@@ -970,6 +1166,558 @@
 TN = ((0,), (0,))
 
 
+LANES = 384
+
+
+def minus_expm1(v):
+    series = 1.0 + v / 8.0
+    for k in (7.0, 6.0, 5.0, 4.0, 3.0, 2.0):
+        series = 1.0 + v * (1.0 / k) * series
+    return jnp.where(v > -0.4, -v * series, 1.0 - jnp.exp(v))
+
+
+def pad_lanes(v, fill=0.0):
+    return jnp.pad(v, ((0, 0), (0, LANES - v.shape[1])), constant_values=fill)
+
+
+def loop(count, body, unroll=1):
+    def step(i, carry):
+        body(i)
+        return carry
+
+    lax.fori_loop(0, count, step, 0, unroll=unroll)
+
+
+def tile_scan(a, b, row, reverse):
+    for step in (1, 2, 4):
+        inside = row < 8 - step if reverse else row >= step
+        shift = 8 - step if reverse else step
+        sa = jnp.where(inside, pltpu.roll(a, shift, 0), 1.0)
+        sb = jnp.where(inside, pltpu.roll(b, shift, 0), 0.0)
+        b = b + a * sb
+        a = a * sa
+    return a, b
+
+
+def eight(i):
+    return pl.multiple_of(i * 8, 8)
+
+
+def recur_forward_kernel(
+    tok_ref, wig_ref, blocks_ref, ch_ref, gain_ref, cot_ref, gate_ref,
+    n1_out, xs, gy, u, siga, sigi, decay, states, mixed, dm_ref, wg_ref,
+    run, logits, n1, both, halo, ends, inc, tok, sems, send, recv, local_sems,
+):
+    p = Place()
+    links = Links(send, recv, local_sems)
+    rows, local = tok_ref.shape[1], wig_ref.shape[1] // 2
+    zh = p.zh
+    greet(weight_peers(p))
+    w_g = slot_columns(p, links, gate_ref, wg_ref)
+    adjoint = TokenGatherTwice(p, links, cot_ref, dm_ref)
+    w_g.begin((1,), (0,))
+    w_g.begin((0,))
+    adjoint.begin()
+
+    def read(b):
+        return pltpu.make_async_copy(tok_ref.at[b], tok.at[b % 2], sems.at[4 + b % 2])
+
+    read(0).start()
+    lane = lax.broadcasted_iota(jnp.int32, (1, LANES), 1)
+    real = lane < local
+
+    def project(b):
+        read(b).wait()
+
+        @pl.when(b < 7)
+        def _():
+            read(b + 1).start()
+
+        def normalise(at):
+            value = tok[b % 2, at, :].astype(F32)
+            inv = lax.rsqrt(jnp.mean(value * value, axis=-1, keepdims=True) + EPSILON)
+            n1[b % 2, at, :] = (value * inv * gain_ref[...]).astype(BF)
+
+        def write(i, at):
+            return pltpu.make_async_copy(n1.at[i], n1_out.at[at], sems.at[i])
+
+        @pl.when(b >= 2)
+        def _():
+            write(b % 2, b - 2).wait()
+
+        chunks(rows, normalise)
+        write(b % 2, b).start()
+        both[...] = dot(n1[b % 2], wig_ref[...], NN)
+        seg, zl = b // 2, b % 2
+
+        def split(at):
+            v = both[at, :]
+            xb = jnp.where(real, v[:, :LANES], 0.0).astype(BF).astype(F32)
+            xs[seg, pl.ds(pl.multiple_of(8 + zl * rows + at.start, 8), CHUNK), :] = xb
+            rest = pltpu.roll(v, v.shape[1] - local, 1)[:, :LANES]
+            gy[b, at, :] = jnp.where(real, rest, 0.0)
+
+        chunks(rows, split)
+
+    loop(8, project)
+    for b in (6, 7):
+        pltpu.make_async_copy(n1.at[b % 2], n1_out.at[b], sems.at[b % 2]).wait()
+
+    def to_partner(src, dst):
+        at = links.pair()
+        links.start(src, dst, at, p.peer(zh=1))
+        return at
+
+    at = to_partner(xs.at[:, pl.ds(2 * rows, 8)], halo)
+    w_g.onward(0)
+    adjoint.forward()
+    links.arrived(halo, at)
+    w_g.begin((1,), (1,))
+    row = lax.broadcasted_iota(jnp.int32, (8, LANES), 0)
+    soft = ch_ref[0:1, :]
+
+    def head(seg):
+        xs[seg, 0:8, :] = jnp.where(zh == 1, halo[seg], 0.0)
+
+    loop(4, head)
+
+    def convolve(b):
+        seg, zl = b // 2, b % 2
+
+        def body(at):
+            v = xs[seg, pl.ds(pl.multiple_of(zl * rows + at.start, 8), CHUNK + 8), :]
+            total = ch_ref[3:4, :] + ch_ref[4:5, :] * v[8:]
+            for k in (1, 2, 3):
+                total = total + ch_ref[4 + k : 5 + k, :] * pltpu.roll(v, k, 0)[8:]
+            u[b, at, :] = total.astype(BF)
+
+        chunks(rows, body)
+        logits[b] = dot(u[b], blocks_ref[...], NN)
+
+    loop(8, convolve)
+
+    def tile(i, carry, zl):
+        at = pl.ds(eight(i), 8)
+        out = []
+        for seg in range(4):
+            b = seg * 2 + zl
+            cp, ch = carry[seg]
+            sa = jax.nn.sigmoid(logits[b, at, :LANES] + ch_ref[1:2, :])
+            si = jax.nn.sigmoid(logits[b, at, LANES:] + ch_ref[2:3, :])
+            log_decay = -DECAY_SCALE * sa * soft
+            a = jnp.exp(log_decay)
+            drive = jnp.sqrt(minus_expm1(2.0 * log_decay)) * si * u[b, at, :].astype(F32)
+            siga[b, at, :] = sa
+            sigi[b, at, :] = si
+            decay[b, at, :] = a
+            pa, h = tile_scan(a, drive, row, False)
+            h = h + pa * ch
+            pa = pa * cp
+            run[b, at, :] = pa
+            states[seg, pl.ds(pl.multiple_of(8 + zl * rows + i * 8, 8), 8), :] = h
+            out.append((pa[7:8, :], h[7:8, :]))
+        return tuple(out)
+
+    carry = ((jnp.ones((1, LANES), F32), jnp.zeros((1, LANES), F32)),) * 4
+    for zl in range(2):
+        carry = lax.fori_loop(0, rows // 8, functools.partial(tile, zl=zl), carry)
+    ends[...] = jnp.zeros_like(ends)
+    for seg in range(4):
+        ends[seg : seg + 1, :] = carry[seg][1]
+    at = to_partner(ends, inc)
+    adjoint.forward_core()
+    w_g.onward(1, (0,))
+    links.arrived(inc, at)
+
+    def finish(b):
+        seg, zl = b // 2, b % 2
+        start = jnp.where(zh == 1, inc[pl.ds(seg, 1), :], 0.0)
+
+        @pl.when(zl == 0)
+        def _():
+            states[seg, 0:8, :] = jnp.broadcast_to(start, (8, LANES))
+
+        def state(at):
+            there = pl.ds(pl.multiple_of(8 + zl * rows + at.start, 8), CHUNK)
+            h = states[seg, there, :] + run[b, at, :] * start
+            states[seg, there, :] = h
+            v = gy[b, at, :]
+            t = jnp.tanh(0.7978845608028654 * (v + 0.044715 * v * v * v))
+            mixed[b, at, :] = (0.5 * v * (1.0 + t) * h).astype(BF)
+
+        chunks(rows, state)
+
+    loop(8, finish)
+    w_g.onward(1, (1,))
+    adjoint.end()
+    w_g.end()
+    links.finish()
+
+
+def recur_backward_kernel(
+    do_ref, wo_ref, blocks_ref, ch_ref,
+    xs, gy, u, siga, sigi, decay, states, rows_ref, mid_ref, n2_ref, dup_ref,
+    dboth_out, gb_out, ch_out, block_out, up_out,
+    dh, after, dgy, dlog_ref, du, dboth, halo, ends, inc, do, final, sems,
+    *scratch,
+):
+    p = Place()
+    links = Links(*scratch[-3:])
+    rows, local = do_ref.shape[1], wo_ref.shape[0]
+    zh = p.zh
+    greet(weight_peers(p))
+    scatter = RowScatter(p, links, rows_ref, scratch[:5])
+    up = GradScatter(p, links, n2_ref, dup_ref, scratch[5:12], GradScatter.EARLY)
+
+    def read(b):
+        return pltpu.make_async_copy(do_ref.at[b], do.at[b % 2], sems.at[4 + b % 2])
+
+    read(0).start()
+    up.begin(1)
+    scatter.begin()
+    ch_out[...] = jnp.zeros_like(ch_out)
+    gb_out[...] = jnp.zeros_like(gb_out)
+    soft = ch_ref[0:1, :]
+
+    def to_partner(src, dst):
+        at = links.pair()
+        links.start(src, dst, at, p.peer(zh=1))
+        return at
+
+    def upstream(b):
+        seg, zl = b // 2, b % 2
+        dh[b, :, local:] = jnp.zeros((rows, LANES - local), F32)
+        read(b).wait()
+
+        @pl.when(b < 7)
+        def _():
+            read(b + 1).start()
+
+        dh[b, :, :local] = dot(do[b % 2], wo_ref[...], NT)
+
+        def split(at):
+            value, slope = gelu_both(gy[b, at, :])
+            dz = dh[b, at, :]
+            h = states[seg, pl.ds(pl.multiple_of(8 + zl * rows + at.start, 8), CHUNK), :]
+            dh[b, at, :] = dz * value
+            dgy[b, at, :] = (dz * h * slope).astype(BF)
+
+        chunks(rows, split)
+
+    loop(8, upstream)
+    scatter.across_y()
+    up.begin(0)
+    row = lax.broadcasted_iota(jnp.int32, (8, LANES), 0)
+    one = jnp.ones((1, LANES), F32)
+    ends[...] = jnp.zeros_like(ends)
+
+    def tile(i, carry, zl):
+        at = pl.ds(eight(rows // 8 - 1 - i), 8)
+        out = []
+        for seg in range(4):
+            b = seg * 2 + zl
+            cp, cg, following = carry[seg]
+            a = decay[b, at, :]
+            shifted = jnp.where(row == 7, following, pltpu.roll(a, 7, 0))
+            pa, g = tile_scan(shifted, dh[b, at, :], row, True)
+            g = g + pa * cg
+            pa = pa * cp
+            dh[b, at, :] = g
+            after[b, at, :] = pa
+            out.append((pa[0:1, :], g[0:1, :], a[0:1, :]))
+        return tuple(out)
+
+    carry = ((one, jnp.zeros((1, LANES), F32), one),) * 4
+    for zl in (1, 0):
+        carry = lax.fori_loop(0, rows // 8, functools.partial(tile, zl=zl), carry)
+    for seg in range(4):
+        ends[seg : seg + 1, :] = carry[seg][1] * carry[seg][2]
+    at = to_partner(ends, inc)
+    links.arrived(inc, at)
+    up.across(0)
+    scatter.across_z()
+
+    def gradients(b):
+        seg, zl = b // 2, b % 2
+        later = jnp.where(zh == 0, inc[pl.ds(seg, 1), :], 0.0)
+
+        def body(at):
+            window = states[seg, pl.ds(pl.multiple_of(zl * rows + at.start, 8), CHUNK + 8), :]
+            previous = pltpu.roll(window, 1, 0)[8:]
+            g = dh[b, at, :] + after[b, at, :] * later
+            sa, si, a = siga[b, at, :], sigi[b, at, :], decay[b, at, :]
+            uf = u[b, at, :].astype(F32)
+            root = jnp.sqrt(minus_expm1((-2.0 * DECAY_SCALE) * sa * soft))
+            gu = g * uf
+            gr = g * root
+            d_log = a * (g * previous - gu * si * a / root)
+            d_log = jnp.where(real, d_log, 0.0)
+            dra = (d_log * (-DECAY_SCALE * soft) * sa * (1.0 - sa)).astype(BF)
+            dri = (gr * uf * si * (1.0 - si)).astype(BF)
+            du[seg, pl.ds(pl.multiple_of(zl * rows + at.start, 8), CHUNK), :] = gr * si
+            dlog_ref[at, :LANES] = dra
+            dlog_ref[at, LANES:] = dri
+            for k, v in enumerate((d_log * sa, dra.astype(F32), dri.astype(F32))):
+                sums[k] = sums[k] + fold(v)
+
+        sums = [jnp.zeros((8, LANES), F32) for _ in range(3)]
+        chunks(rows, body)
+        for k in range(3):
+            ch_out[k] += sums[k]
+        d = dlog_ref[...]
+        there = pl.ds(pl.multiple_of(zl * rows, 8), rows)
+        du[seg, there, :] += dot(d, blocks_ref[...], NT)
+        gb_out[...] += dot(u[b], d, TN)
+
+    lane = lax.broadcasted_iota(jnp.int32, (1, LANES), 1)
+    real = lane < local
+    loop(8, gradients)
+    at = to_partner(du.at[:, pl.ds(0, 8)], halo)
+    up.across(1)
+
+    def write(i, at, src, dst, base):
+        return pltpu.make_async_copy(src.at[i], dst.at[at], sems.at[base + i])
+
+    def convolve(i, zl):
+        seg = i
+        b = i * 2 + zl
+        slot = i % 2
+
+        @pl.when(i >= 2)
+        def _():
+            write(slot, b - 4, dboth, dboth_out, 0).wait()
+
+        def body(at):
+            start = pl.multiple_of(zl * rows + at.start, 8)
+            v = du[seg, pl.ds(start, CHUNK + 8), :]
+            x = xs[seg, pl.ds(start, CHUNK + 8), :]
+            here = v[:CHUNK]
+            total = ch_ref[4:5, :] * here
+            sums[0] = sums[0] + fold(here)
+            sums[1] = sums[1] + fold(here * x[8:])
+            for k in (1, 2, 3):
+                total = total + ch_ref[4 + k : 5 + k, :] * pltpu.roll(v, CHUNK + 8 - k, 0)[:CHUNK]
+                sums[1 + k] = sums[1 + k] + fold(here * pltpu.roll(x, k, 0)[8:])
+            wide = 2 * local - LANES
+            zeros = jnp.zeros((CHUNK, wide), F32)
+            left = jnp.concatenate([total, zeros], axis=1)
+            right = jnp.concatenate([dgy[b, at, :].astype(F32), zeros], axis=1)
+            dboth[slot, at, :] = (left + pltpu.roll(right, local, 1)).astype(BF)
+
+        sums = [jnp.zeros((8, LANES), F32) for _ in range(5)]
+        chunks(rows, body)
+        for k in range(5):
+            ch_out[3 + k] += sums[k]
+        write(slot, b, dboth, dboth_out, 0).start()
+
+    def drain(zl):
+        for i in (2, 3):
+            write(i % 2, i * 2 + zl, dboth, dboth_out, 0).wait()
+
+    loop(4, functools.partial(convolve, zl=0))
+    drain(0)
+    up.last(0)
+    links.arrived(halo, at)
+
+    def tail(seg):
+        du[seg, pl.ds(2 * rows, 8), :] = jnp.where(zh == 0, halo[seg], 0.0)
+
+    loop(4, tail)
+    loop(4, functools.partial(convolve, zl=1))
+    drain(1)
+    up.last(1)
+    scatter.arrive()
+
+    def add(at):
+        final[at, :] = (mid_ref[at, :] + scatter.total(at)).astype(BF)
+
+    chunks(rows, add)
+    at = links.pair()
+    links.start(final, block_out.at[p.mp], at, p.peer(mp=1))
+    kept = links.keep(final, block_out.at[p.mp])
+    up.end()
+    ff = up.result.shape[2]
+    for j in range(4):
+        up_out[:, j * ff : (j + 1) * ff] = up.result[j].astype(F32)
+    kept.wait()
+    links.arrived(block_out.at[1 - p.mp], at)
+    links.finish()
+
+
+def recur_forward(tokens, w_ig, blocks, channels, gain, dm, mlp_gate):
+    if not shape_fits():
+        return plain_recur_forward(tokens, w_ig, blocks, channels, gain, dm, mlp_gate)
+    ff, drows = mlp_gate.shape[1] // 4, mlp_gate.shape[0]
+    rows, width = tokens.shape[1:]
+    local = w_ig.shape[1] // 2
+    soft = jax.nn.softplus(-channels[0:1])
+    table = jnp.concatenate([soft, channels[1:]], axis=0)
+    table = pad_lanes(table)
+    wide = jnp.concatenate(
+        [jnp.pad(blocks[:, g * local : (g + 1) * local], ((0, LANES - local),) * 2) for g in (0, 1)],
+        axis=1,
+    )
+    f, h = (8, rows, LANES), (4, 2 * rows + 8, LANES)
+    n1, *saved = run_kernel(
+        recur_forward_kernel,
+        "recur_forward",
+        [(tokens.shape, BF), (h, F32), (f, F32), (f, BF)]
+        + [(f, F32)] * 3
+        + [(h, F32), (f, BF), (tokens.shape, BF), ((width, ff), BF)],
+        [ANY] + [VMEM] * 8 + [ANY] * 2,
+        [ANY] + [VMEM] * 4 + [ANY] * 2,
+        [
+            pltpu.VMEM(f, F32),
+            pltpu.VMEM((8, rows, 2 * LANES), F32),
+            pltpu.VMEM((2, rows, width), BF),
+            pltpu.VMEM((rows, 2 * local), F32),
+            pltpu.VMEM((4, 8, LANES), F32),
+            pltpu.VMEM((8, LANES), F32),
+            pltpu.VMEM((8, LANES), F32),
+            pltpu.VMEM((2, rows, width), BF),
+        ]
+        + semaphores(6, 2)[:1]
+        + semaphores(24, 8),
+        5,
+        (tokens, w_ig, wide, table, gain, dm, mlp_gate),
+        56,
+    )
+    *saved, mixed, dm, w_g = saved
+    return n1.reshape(-1, width), mixed.reshape(-1, LANES), (table, wide, *saved), dm, w_g
+
+
+def recur_backward(do, saved, w_o, channels, out_part, middle, n2, dup, drows):
+    if not shape_fits():
+        return plain_recur_backward(do, saved, w_o, channels, out_part, middle, n2, dup, drows)
+    ff = dup.shape[1]
+    table, wide, xs, gy, u, siga, sigi, decay, states = saved
+    rows, width = do.shape[1:]
+    local = w_o.shape[0]
+    f, h = (8, rows, LANES), (4, 2 * rows + 8, LANES)
+    dboth, g_blocks, sums, block_out, g_up = run_kernel(
+        recur_backward_kernel,
+        "recur_backward",
+        [
+            ((8, rows, 2 * local), BF),
+            ((LANES, 2 * LANES), F32),
+            ((8, 8, LANES), F32),
+            ((2, rows, width), BF),
+            ((drows, 4 * ff), F32),
+        ],
+        [ANY] + [VMEM] * 2 + [ANY, VMEM],
+        [ANY] + [VMEM] * 10 + [ANY, VMEM, ANY, VMEM],
+        [
+            pltpu.VMEM(f, F32),
+            pltpu.VMEM(f, F32),
+            pltpu.VMEM(f, BF),
+            pltpu.VMEM((rows, 2 * LANES), BF),
+            pltpu.VMEM(h, F32),
+            pltpu.VMEM((2, rows, 2 * local), BF),
+            pltpu.VMEM((4, 8, LANES), F32),
+            pltpu.VMEM((8, LANES), F32),
+            pltpu.VMEM((8, LANES), F32),
+            pltpu.VMEM((2, rows, width), BF),
+            pltpu.VMEM((rows, width), BF),
+        ]
+        + semaphores(6, 2)[:1]
+        + scatter_buffers(rows, width)
+        + grad_buffers(2 * drows, ff, 8 * rows)
+        + semaphores(32, 24),
+        6,
+        (do, w_o, wide, table, xs, gy, u, siga, sigi, decay, states)
+        + (out_part, middle, n2, dup),
+        61,
+    )
+    sums = jnp.sum(sums, axis=1)[:, :local]
+    dlam = sums[0] * DECAY_SCALE * jax.nn.sigmoid(-channels[0])
+    g_blocks = jnp.concatenate(
+        [g_blocks[:local, g * LANES : g * LANES + local] for g in (0, 1)], axis=1
+    )
+    return (
+        dboth.reshape(-1, 2 * local),
+        g_blocks,
+        jnp.concatenate([dlam[None], sums[1:]], axis=0),
+        block_out,
+        g_up,
+    )
+
+
+def plain_recur_forward(tokens, w_ig, blocks, channels, gain, dm, mlp_gate):
+    length, local, width = tokens.shape[1], w_ig.shape[1] // 2, tokens.shape[2]
+    wide = tokens.reshape(-1, width).astype(F32)
+    n1 = (wide * inverse_rms(wide) * gain).astype(BF)
+    both = dot(n1, w_ig, NN)
+    xb = both[:, :local].astype(BF).reshape(4, 2 * length, local)
+    gy = both[:, local:].reshape(4, 2 * length, local)
+    rim = from_behind(xb[:, -3:], 1)
+    padded = jnp.concatenate([rim, xb], axis=1).astype(F32)
+    conv = channels[3]
+    for k in range(4):
+        conv = conv + channels[4 + k] * padded[:, 3 - k : 3 - k + 2 * length]
+    u = conv.astype(BF)
+    logits = dot(u.reshape(-1, local), blocks, NN).reshape(4, 2 * length, 2 * local)
+    sig_a = jax.nn.sigmoid(logits[..., :local] + channels[1])
+    sig_i = jax.nn.sigmoid(logits[..., local:] + channels[2])
+    log_decay = -DECAY_SCALE * sig_a * jax.nn.softplus(-channels[0])
+    decay = jnp.exp(log_decay)
+    root = jnp.sqrt(-jnp.expm1(2.0 * log_decay))
+    running, state = local_scan(decay, root * sig_i * u.astype(F32), False)
+    incoming = carried(running[:, -1], state[:, -1], False)
+    states = state + running * incoming[:, None]
+    gelu_y, slope_y = gelu_both(gy)
+    mixed = (gelu_y * states).astype(BF).reshape(-1, local)
+    saved = (blocks, padded, u, sig_a, sig_i, decay, root, running, incoming, states)
+    exchange = Tokens()
+    dm = exchange.gather(lax.dynamic_index_in_dim(dm, exchange.mp, 0, keepdims=False))
+    return (
+        n1,
+        mixed,
+        saved + (gelu_y, slope_y),
+        dm.reshape(8, length, width),
+        fetch_weight([mlp_gate], 4),
+    )
+
+
+def plain_recur_backward(do, saved, w_o, channels, out_part, middle, n2, dup, drows):
+    blocks, padded, u, sig_a, sig_i, decay, root, running, incoming, states = saved[:10]
+    gelu_y, slope_y = saved[10:]
+    length, local, width = do.shape[1], w_o.shape[0], do.shape[2]
+    dz = dot(do.reshape(-1, width), w_o, NT).reshape(4, 2 * length, local)
+    dh = dz * gelu_y
+    dgy = (dz * states * slope_y).astype(BF)
+    ones = jnp.ones_like(decay[:, :1])
+    after, adjoint = local_scan(jnp.concatenate([decay[:, 1:], ones], axis=1), dh, True)
+    later = carried(running[:, -1], decay[:, 0] * adjoint[:, 0], True)
+    adjoint = adjoint + after * later[:, None]
+    previous = jnp.concatenate([incoming[:, None], states[:, :-1]], axis=1)
+    soft, uf = jax.nn.softplus(-channels[0]), u.astype(F32)
+    d_root = adjoint * sig_i * uf
+    d_log = adjoint * previous * decay - d_root * decay * decay / root
+    dra = (d_log * (-DECAY_SCALE * soft) * sig_a * (1.0 - sig_a)).astype(BF)
+    dri = (adjoint * root * uf * sig_i * (1.0 - sig_i)).astype(BF)
+    dlam = jnp.sum(d_log * sig_a, axis=(0, 1)) * DECAY_SCALE * jax.nn.sigmoid(-channels[0])
+    dlogits = jnp.concatenate([dra, dri], axis=2).reshape(-1, 2 * local)
+    g_blocks = dot(u.reshape(-1, local), dlogits, TN)
+    du = adjoint * root * sig_i + dot(dlogits, blocks, NT).reshape(4, 2 * length, local)
+    zeros = jnp.zeros((4, 3, local), F32)
+    spread = jnp.concatenate([zeros, du, zeros], axis=1)
+    dpad = jnp.zeros((4, 2 * length + 3, local), F32)
+    taps = []
+    for k in range(4):
+        dpad = dpad + channels[4 + k] * spread[:, k : k + 2 * length + 3]
+        taps.append(jnp.sum(du * padded[:, 3 - k : 3 - k + 2 * length], axis=(0, 1)))
+    back = from_behind(dpad[:, :3], -1)
+    dxb = dpad[:, 3:] + jnp.concatenate(
+        [jnp.zeros((4, 2 * length - 3, local), F32), back], axis=1
+    )
+    dboth = jnp.concatenate([dxb.astype(BF), dgy], axis=2).reshape(-1, 2 * local)
+    sums = [jnp.sum(v.astype(F32), axis=(0, 1)) for v in (dra, dri, du)]
+    result = (middle + Tokens().scatter(out_part.reshape(-1, width))).astype(BF)
+    g_up = columns(return_grad(dot(n2, dup, TN, BF), drows), 0, dup.shape[1])
+    small = jnp.stack([dlam] + sums + taps)
+    return dboth, g_blocks, small, both_batches(result), g_up
+
+
 def on_device(
     tokens_in,
     cotangent,
@@ -991,8 +1739,6 @@
     group = dxn * 2 * zhn * 2
     dc, zl, mp = (lax.axis_index(n) for n in ("dc", "zl", "mp"))
     slot = dc * 2 + zl
-    exchange = Tokens()
-    length = tokens_in.shape[2]
     width = tokens_in.shape[3]
     local = input_weight.shape[1] // 4
     heads = decay_gates.shape[0] // 4
@@ -1027,7 +1773,6 @@
 
     ff = mlp_gate.shape[1] // 4
     tokens, w_ig, w_o = fetch_first(tokens_in[:, 0], input_weight, gelu_weight, output_weight)
-    tokens = tokens.reshape(-1, width)
 
     gates = jnp.stack([decay_gates, input_gates]).reshape(2, 4, heads, piece)
     gates = gates.transpose(1, 0, 2, 3).reshape(2, 1, 2, 1, 2 * heads * piece)
@@ -1037,17 +1782,6 @@
     gates = gates.reshape(group, 2 * heads, piece).transpose(1, 0, 2)
     gates = gates.reshape(2, heads, BLOCK, BLOCK)
 
-    wide = tokens.astype(F32)
-    n1 = (wide * inverse_rms(wide) * gains[0]).astype(BF)
-    both = dot(n1, w_ig, NN)
-    xb = both[:, :local].astype(BF).reshape(4, 2 * length, local)
-    gy = both[:, local:].reshape(4, 2 * length, local)
-    rim = from_behind(xb[:, -3:], 1)
-    padded = jnp.concatenate([rim, xb], axis=1).astype(F32)
-    conv = channels[3]
-    for k in range(4):
-        conv = conv + channels[4 + k] * padded[:, 3 - k : 3 - k + 2 * length]
-    u = conv.astype(BF)
     zero = jnp.zeros((BLOCK, BLOCK), BF)
     blocks = jnp.concatenate(
         [
@@ -1058,78 +1792,21 @@
         ],
         axis=0,
     )
-    u2 = u.reshape(-1, local)
-    logits = dot(u2, blocks, NN).reshape(4, 2 * length, 2 * local)
-    sig_a = jax.nn.sigmoid(logits[..., :local] + channels[1])
-    sig_i = jax.nn.sigmoid(logits[..., local:] + channels[2])
-    soft = jax.nn.softplus(-channels[0])
-    log_decay = -DECAY_SCALE * sig_a * soft
-    decay = jnp.exp(log_decay)
-    root = jnp.sqrt(-jnp.expm1(2.0 * log_decay))
-    uf = u.astype(F32)
-    drive = root * sig_i * uf
-    running, state = local_scan(decay, drive, False)
-    incoming = carried(running[:, -1], state[:, -1], False)
-    states = state + running * incoming[:, None]
-    gelu_y, slope_y = gelu_both(gy)
-    mixed = (gelu_y * states).astype(BF).reshape(-1, local)
-    middle, n2, dm, w_gu, w_d = reduce_and_fetch(
-        dot(mixed, w_o, NN, BF), own, gains[1:2], douts.astype(BF), mlp_gate, mlp_up, mlp_down
-    )
-    n2 = n2.reshape(-1, width)
-    dm = dm.reshape(-1, width)
-
-    pre = dot(n2, w_gu, NN)
-    gm, up = pre[:, :ff], pre[:, ff:]
-    value, slope = gelu_both(gm)
-    hidden = (value * up).astype(BF)
-    g_down = dot(hidden, dm, TN, BF)
-    dhm = dot(dm, w_d, NT)
-    dgm, dup = (dhm * up * slope).astype(BF), (dhm * value).astype(BF)
-    pair = jnp.concatenate([dgm, dup], axis=1)
-    g_wide = dot(n2, pair, TN, BF)
-    dr1, gain_two, do, share_down, share_wide = reduce_and_return(
-        dot(pair, w_gu, NT, BF), middle, dout, gains[1:2], g_down, g_wide, drows
+    n1, mixed, saved, dm, w_g = recur_forward(
+        tokens, w_ig, blocks, channels, gains[0:1], douts.astype(BF), mlp_gate
+    )
+    middle, n2, w_u, w_d = reduce_and_fetch(mixed, w_o, own, gains[1:2], mlp_up, mlp_down)
+
+    hidden, dgm, dup = feed_forward(n2, dm, w_g, w_u, w_d)
+    n2, dm = n2.reshape(-1, width), dm.reshape(-1, width)
+    dr1, gain_two, do, g_gate, g_down, out_part = reduce_and_return(
+        (w_g, w_u, w_d), middle, dout, gains[1:2], dm, hidden, n2, dgm, dup, drows
     )
     gain_two = jnp.sum(gain_two, axis=0)
-    do = do.reshape(-1, width)
-
-    result = middle + exchange.scatter(dot(hidden, w_d, NN))
-    result = result.astype(BF)
-
-    g_out = dot(mixed, do, TN, BF)
-    dz = dot(do, w_o, NT).reshape(4, 2 * length, local)
-    dh = dz * gelu_y
-    dgy = (dz * states * slope_y).astype(BF)
-    ones = jnp.ones_like(decay[:, :1])
-    after, adjoint = local_scan(jnp.concatenate([decay[:, 1:], ones], axis=1), dh, True)
-    later = carried(running[:, -1], decay[:, 0] * adjoint[:, 0], True)
-    adjoint = adjoint + after * later[:, None]
-    previous = jnp.concatenate([incoming[:, None], states[:, :-1]], axis=1)
-    d_root = adjoint * sig_i * uf
-    d_sig_i = adjoint * root * uf
-    du0 = adjoint * root * sig_i
-    d_log = adjoint * previous * decay - d_root * decay * decay / root
-    dra = (d_log * (-DECAY_SCALE * soft) * sig_a * (1.0 - sig_a)).astype(BF)
-    dri = (d_sig_i * sig_i * (1.0 - sig_i)).astype(BF)
-    dlam = jnp.sum(d_log * sig_a, axis=(0, 1)) * DECAY_SCALE * jax.nn.sigmoid(-channels[0])
-    dlogits = jnp.concatenate([dra, dri], axis=2).reshape(-1, 2 * local)
-    g_blocks = dot(u2, dlogits, TN)
-    du = du0 + dot(dlogits, blocks, NT).reshape(4, 2 * length, local)
-    zeros = jnp.zeros((4, 3, local), F32)
-    spread = jnp.concatenate([zeros, du, zeros], axis=1)
-    dpad = jnp.zeros((4, 2 * length + 3, local), F32)
-    taps = []
-    for k in range(4):
-        dpad = dpad + channels[4 + k] * spread[:, k : k + 2 * length + 3]
-        taps.append(jnp.sum(du * padded[:, 3 - k : 3 - k + 2 * length], axis=(0, 1)))
-    back = from_behind(dpad[:, :3], -1)
-    dxb = dpad[:, 3:] + jnp.concatenate(
-        [jnp.zeros((4, 2 * length - 3, local), F32), back], axis=1
-    )
-    dboth = jnp.concatenate([dxb.astype(BF), dgy], axis=2).reshape(-1, 2 * local)
-    g_wide_ig = dot(n1, dboth, TN, BF)
-    dn1 = dot(dboth, w_ig, NT, BF)
+
+    dboth, g_blocks, channel_grad, block_out, g_up = recur_backward(
+        do, saved, w_o, channels, out_part, middle, n2, dup, drows
+    )
 
     g_gates = jnp.stack(
         [
@@ -1149,13 +1826,15 @@
     count = g_gates.shape[1]
     unit = (count + 2047) // 2048 * 16
     g_gates = jnp.pad(g_gates, ((0, 0), (0, unit * 128 - count))).astype(BF)
-    dx_own, gain_one, share_o, share_ig, share_gates = return_last(
-        dn1,
+    grad_tokens, gain_one, g_input, g_gelu, g_output, share_gates = return_last(
+        w_ig,
         own,
         dr1,
         gains[0:1],
-        g_out,
-        g_wide_ig,
+        do.reshape(-1, width),
+        mixed,
+        n1,
+        dboth,
         g_gates.reshape(group * unit, 128),
         drows,
     )
@@ -1163,52 +1842,31 @@
     g_gates = share_gates.reshape(4, -1)[:, :count].astype(F32).reshape(4, 2, heads, piece)
     g_gates = g_gates.transpose(1, 0, 2, 3).reshape(2, 4 * heads, piece)
 
-    channel_grad = jnp.stack(
-        [
-            dlam,
-            jnp.sum(dra.astype(F32), axis=(0, 1)),
-            jnp.sum(dri.astype(F32), axis=(0, 1)),
-            jnp.sum(du, axis=(0, 1)),
-        ]
-        + taps
-    )
     per = 4 * local // group
     mine = channel_grad.reshape(8, group // 4, per).transpose(1, 0, 2)
     mine = jnp.where(
         jnp.arange(4, dtype=jnp.int32)[:, None, None, None] == slot, mine[None], 0.0
-    ).reshape(group, 8 * per)
+    ).reshape(group, 1, 8 * per)
+    mine = jnp.where(jnp.arange(2, dtype=jnp.int32)[None, :, None] == mp, mine, 0.0)
     both_gains = jnp.stack([gain_one, gain_two]).reshape(2, group, -1).transpose(1, 0, 2)
-    sums = jnp.concatenate([both_gains.reshape(group, -1), mine], axis=1)
-    sums = jnp.sum(lax.all_to_all(sums, shards, 0, 0, tiled=True), axis=0)
+    both_gains = jnp.broadcast_to(both_gains.reshape(group, 1, -1), (group, 2, 2 * drows))
+    sums = jnp.concatenate([both_gains, mine], axis=2).reshape(2 * group, -1)
+    sums = jnp.sum(lax.all_to_all(sums, AXES, 0, 0, tiled=True), axis=0)
     g_gains = sums[: 2 * drows].reshape(2, drows)
-    g_gains = g_gains + lax.ppermute(g_gains, "mp", [(0, 1), (1, 0)])
     g_channels = sums[2 * drows :].reshape(8, 1, per)
-
-    def both_batches(rows):
-        other = lax.ppermute(rows, "mp", [(0, 1), (1, 0)])
-        return jnp.stack([jnp.where(mp == 0, rows, other), jnp.where(mp == 0, other, rows)])
-
-    block_out = both_batches(result)[:, None]
-    grad_tokens = both_batches(dx_own)[:, None]
-
-    def columns(share, at, count):
-        return (
-            share[:, :, at : at + count].astype(F32).transpose(1, 0, 2).reshape(drows, 4 * count)
-        )
-
     return (
-        block_out,
-        grad_tokens,
-        columns(share_ig, 0, local),
-        columns(share_ig, local, local),
+        block_out[:, None],
+        grad_tokens[:, None],
+        g_input,
+        g_gelu,
         g_gates[0],
         g_gates[1],
         g_channels,
         g_gains,
-        share_o.astype(F32).reshape(-1, drows),
-        columns(share_wide, 0, ff),
-        columns(share_wide, ff, ff),
-        share_down.astype(F32).reshape(-1, drows),
+        g_output,
+        g_gate,
+        g_up,
+        g_down,
     )
 
 

time: 841 us -> 717 us (0.85)
  Pallas kernels: 489 us -> 620 us
  matrix products: 118 us -> 0 us
  other arithmetic: 73.5 us -> 16.8 us
  waiting for transfers between devices: 51.4 us -> 11.4 us
  local copies, waits for them, and re-layouts: 67.7 us -> 44.3 us
  starting transfers between devices: 32.4 us -> 17.3 us
    pallas_call x4 -> x6, Pallas kernels: 477 us -> 596 us  [run_kernel(): pl.pallas_call(body, name=name, out_shape=[jax.ShapeDtypeStruct(*o) for o...]
    dot_general x15 -> x0, matrix products: 118 us -> none  [dot(): r = lax.dot_general(a, b, (dims, ((), ())), preferred_element_type=F32)]
    ppermute x10 -> x0, waiting for transfers between devices: 51.4 us -> none  [the longest x1 44.5 us: scatter(): lax.ppermute(jnp.stack([pick(two), pick(both)]).astype(BF), AXES, self.se...]
    convert_element_type x8 -> x0, other arithmetic: 20.9 us -> none  [the longest x2 10.7 us: on_device(): n1 = (wide * inverse_rms(wide) * gains[0]).astype(BF)]
    ppermute x10 -> x0, starting transfers between devices: 17 us -> none  [the longest x2 6.08 us: carried(): return lax.ppermute(state, 'zh', [(1, 0)] if reverse else [(0, 1)])]
    reduce_sum x5 -> x2, other arithmetic: 14.3 us -> 1.01 us  [the longest x1 0.92 us: recur_backward(): sums = jnp.sum(sums, axis=1)[:, :local]]
    pallas_call x2 -> x1, Pallas kernels: 12.5 us -> 24 us  [feed_forward(): pl.pallas_call(mlp_kernel, name='feed_forward', grid=(blocks // 2,), in_s...]
    slice x8 -> x4, local copies, waits for them, and re-layouts: 11.3 us -> 0.75 us  [the longest x1 0.61 us: on_device(): gains[1:2]]
  transfers between devices with their start and end apart: 13 -> 3, of which waited for: 3 -> 2; matrix products, arithmetic and copies ran while one was open for 17% -> 3% of each run, Pallas kernels for 20% -> 10%
where the time goes in v3:
time: 717 us; the launch traced here: 711 us
  Pallas kernels  620 us (86%)
  local copies, waits for them, and re-layouts  44.3 us (6%)
  starting transfers between devices  17.3 us (2%)
  other arithmetic  16.8 us (2%)
  waiting for transfers between devices  11.4 us (2%)
    pallas_call x6, Pallas kernels, run_kernel(): pl.pallas_call(body, name=name, out_shape=[jax.ShapeDtypeStruct(*o) for o...  596 us
    unnamed x71, local copies, waits for them, and re-layouts  30.1 us
    pallas_call x1, Pallas kernels, feed_forward(): pl.pallas_call(mlp_kernel, name='feed_forward', grid=(blocks // 2,), in_s...  24 us
  transfers between devices with their start and end apart: 3, of which 2 were waited for; matrix products, arithmetic and copies ran while one was open for 3% of the time, Pallas kernels for 10%

profile of v3, /device:TPU:1, one launch (start us, length us, event | category | flops | bytes accessed | tf_op | source)
XLA Modules:
  0.0 710.8 jit_solution(10768528489850018793)
XLA Ops:
  0.7 0.8 reshape.178
  1.5 0.7 pad_maximum_fusion.3
  2.2 0.5 broadcast.61
  2.7 0.8 reduce.5
  3.5 0.7 reshape.201
  4.2 7.3 %all-to-all-start.1 = ((bf16[16,2,448]{2,1,0:T(2,128)(2,1)}), bf16[16,2,448]{2,1,0:T(2,128)(2,1)S(1)}, u32[]{:S(2)}, u32[]{:S(2)}) async-start(bf16[16,2,448]{2,1,0:T(2,128)(2,1)} %reshape.201), calls=%async_computation.1 | async-start | bytes 65536 | tf_op jit(solution)/shard_map/all_to_all | solution.py:1766
  11.6 1.3 fusion.9
  12.9 0.8 stack.63
  13.6 0.8 stack.64
  14.4 1.2 copy.60
  16.0 0.9 copy.63
  17.0 1.9 fusion.4
  18.9 1.4 pad_maximum_fusion.4
  20.3 3.3 convert_multiply_fusion
  23.6 1.2 dynamic-slice_bitcast_fusion.dout_ref
  25.8 1.8 reduce.4
  27.7 0.7 reshape.199
  28.4 1.4 copy-done.7
  29.8 74.6 %fetch_first.1 = (bf16[8,176,2048]{2,1,0:T(8,128)(2,1)S(1)}, bf16[2048,640]{1,0:T(8,128)(2,1)S(1)}, bf16[320,2048]{1,0:T(8,128)(2,1)S(1)}) custom-call(bf16[2,176,2048]{2,1,0:T(8,128)(2,1)S(1)} %bitcast.94, bf16[4,128,640]{2,1,0:T(8,128)(2,1)S(1)} %maximum_bitcast_fusion.ig_ref, bf16[1280,128]{1,0:T(8,128)(2,1)S(1)} %copy-done.14), custom_call_target="tpu_custom_call" | custom-call | tf_op jit(solution)/shard_map/fetch_first/pallas_call | solution.py:889
  104.4 1.5 copy-done
  105.9 2.5 copy-done.2
  108.4 6.1 all-to-all-start
  115.0 0.6 select_maximum_fusion.ch_ref
  115.6 0.6 slice_bitcast_fusion.8
  116.3 6.3 all-to-all-done
  122.7 1.2 reduce.1
  123.9 0.3 reshape.176
  124.9 0.9 fusion.2.blocks_ref
  125.8 79.5 %recur_forward.1 = (bf16[8,176,2048]{2,1,0:T(8,128)(2,1)}, f32[4,360,384]{2,1,0:T(8,128)}, f32[8,176,384]{2,1,0:T(8,128)}, bf16[8,176,384]{2,1,0:T(8,128)(2,1)},...) custom-call(bf16[8,176,2048]{2,1,0:T(8,128)(2,1)} %copy-done.2, ...), custom_call_target="tpu_custom_call" | custom-call | tf_op jit(solution)/shard_map/recur_forward/pallas_call | solution.py:889
  205.4 1.2 copy-done.5
  206.6 117.3 %reduce_and_fetch.1 = (f32[176,2048]{1,0:T(8,128)S(1)}, bf16[8,176,2048]{2,1,0:T(8,128)(2,1)}, bf16[2048,768]{1,0:T(8,128)(2,1)S(1)}, bf16[768,2048]{1,0:T(8,128)(2,1)S(1)}) custom-call(bf16[1408,384]{1,0:T(8,128)(2,1)S(1)} %bitcast.93, bf16[320,2048]{1,0:T(8,128)(2,1)S(1)} %get-tuple-element.54.wo_ref, ...), custom_call_target="tpu_custom_call" | custom-call | tf_op jit(solution)/shard_map/reduce_and_fetch/pallas_call | solution.py:889
  323.9 1.1 copy-done.3
  325.0 1.6 copy-done.8
  326.6 1.7 copy-done.9
  328.4 24.0 %feed_forward.1 = (bf16[1408,768]{1,0:T(8,128)(2,1)S(1)}, bf16[1408,768]{1,0:T(8,128)(2,1)S(1)}, bf16[1408,768]{1,0:T(8,128)(2,1)}) custom-call(bf16[8,176,2048]{2,1,0:T(8,128)(2,1)} %get-tuple-element.59.n2_ref, bf16[8,176,2048]{2,1,0:T(8,128)(2,1)} %get-tuple-element.58.dm_ref, bf16[2048,768]{1,0:T(8,128)(2,1)} %get-tuple-element.52.wg_ref, ...), custom_call_target="tpu_custom_call" | custom-call | flops 13287555072 | bytes 11534336 | tf_op jit(solution)/shard_map/feed_forward/pallas_call | solution.py:865
  352.3 1.3 copy-done.10
  353.7 1.3 copy-done.11
  355.0 134.5 %reduce_and_return.1 = (f32[176,2048]{1,0:T(8,128)}, f32[8,2048]{1,0:T(8,128)}, bf16[8,176,2048]{2,1,0:T(8,128)(2,1)}, f32[128,3072]{1,0:T(8,128)}, f32[3072,128]{1,0:T(8,128)}, /*index=5*/bf16[8,176,2048]{2,1,0:T(8,128)(2,1)}) custom-call(bf16[2048,768]{1,0:T(8,128)(2,1)} %get-tuple-element.52.wg_ref, bf16[2048,768]{1,0:T(8,128)(2,1)} %copy-done.8, ...), custom_call_target="tpu_custom_call" | custom-call | tf_op jit(solution)/shard_map/reduce_and_return/pallas_call | solution.py:889
  489.6 96.4 %recur_backward.1 = (bf16[8,176,640]{2,1,0:T(8,128)(2,1)}, f32[384,768]{1,0:T(8,128)}, f32[8,8,384]{2,1,0:T(8,128)}, bf16[2,176,2048]{2,1,0:T(8,128)(2,1)}, f32[128,3072]{1,0:T(8,128)}) custom-call(bf16[8,176,2048]{2,1,0:T(8,128)(2,1)} %get-tuple-element.63.do_ref, bf16[320,2048]{1,0:T(8,128)(2,1)} %copy-done.4, bf16[384,768]{1,0:T(8,128)(2,1)} %fusion.2.blocks_ref, ...), custom_call_target="tpu_custom_call" | custom-call | tf_op jit(solution)/shard_map/recur_backward/pallas_call | solution.py:889
  586.0 0.9 reduce_sum.58
  587.5 1.3 convert.28
  589.1 0.3 reshape.188
  589.7 0.8 reshape.190.gg_ref
  590.5 93.3 %return_last.1 = (f32[2,176,2048]{2,1,0:T(8,128)}, f32[8,2048]{1,0:T(8,128)}, f32[128,1280]{1,0:T(8,128)}, f32[128,1280]{1,0:T(8,128)}, f32[1280,128]{1,0:T(8,128)}, /*index=5*/bf16[4,64,128]{2,1,0:T(8,128)(2,1)}) custom-call(bf16[2048,640]{1,0:T(8,128)(2,1)} %copy-done, bf16[176,2048]{1,0:T(8,128)(2,1)} %copy-done.1, ...), custom_call_target="tpu_custom_call" | custom-call | tf_op jit(solution)/shard_map/return_last/pallas_call | solution.py:889
  683.8 0.9 reduce_sum.56
  684.8 0.7 all_to_all.22
  685.5 3.9 all-to-all-start.2
  689.4 0.9 copy.83
  690.6 0.7 squeeze.49
  691.2 0.7 squeeze.48
  691.9 5.1 all-to-all-done.2
  697.0 0.6 slice_bitcast_fusion.10
  697.6 0.7 reshape.193
  698.3 2.6 copy.94
  700.9 1.6 copy.95
  702.5 0.8 copy.96
  703.3 0.5 copy-done.22
  703.8 0.8 copy.97
  704.7 0.8 copy.98
  705.5 1.1 copy.99
  706.7 0.8 copy-done.19
  707.5 1.1 copy.100
  708.6 0.8 copy-done.17
  709.5 1.1 copy.101
  (106 shorter events, 4.4 us)
Async XLA Ops:
  0.6 15.2 %copy-start.24 = (bf16[128,1280]{1,0:T(8,128)(2,1)S(1)}, bf16[128,1280]{1,0:T(8,128)(2,1)}, u32[]{:S(2)}) copy-start(bf16[128,1280]{1,0:T(8,128)(2,1)} %param.19) | copy-start | bytes 983044
  2.1 14.8 %copy-start.26 = (f32[8]{0:T(128)S(1)}, f32[8]{0:T(128)}, u32[]{:S(2)}) copy-start(f32[8]{0:T(128)} %param.17) | copy-start | bytes 100
  2.2 18.1 %copy-start.6 = (bf16[2,1,176,2048]{3,2,1,0:T(8,128)(2,1)S(1)}, bf16[2,1,176,2048]{3,2,1,0:T(8,128)(2,1)}, u32[]{:S(2)}) copy-start(bf16[2,1,176,2048]{3,2,1,0:T(8,128)(2,1)} %param.14) | copy-start | bytes 4325380
  4.2 104.2 %all-to-all-start.1 = ((bf16[16,2,448]{2,1,0:T(2,128)(2,1)}), bf16[16,2,448]{2,1,0:T(2,128)(2,1)S(1)}, u32[]{:S(2)}, u32[]{:S(2)}) async-start(bf16[16,2,448]{2,1,0:T(2,128)(2,1)} %reshape.201), calls=%async_computation.1 | async-start | bytes 65536 | tf_op jit(solution)/shard_map/all_to_all | solution.py:1766
  20.3 185.0 %copy-start.1 = (bf16[176,2048]{1,0:T(8,128)(2,1)}, bf16[176,2048]{1,0:T(8,128)(2,1)S(1)}, u32[]{:S(2)}) copy-start(bf16[176,2048]{1,0:T(8,128)(2,1)S(1)} %dynamic-slice_bitcast_fusion.1.own_ref) | copy-start | bytes 2162692
  23.6 1.3 copy-start.20
  24.9 3.5 copy-start.14
  28.4 1.4 copy-start.7
  104.4 1.5 copy-start
  105.9 2.5 copy-start.2
  108.4 96.9 %copy-start.4 = (bf16[320,2048]{1,0:T(8,128)(2,1)}, bf16[320,2048]{1,0:T(8,128)(2,1)S(1)}, u32[]{:S(2)}) copy-start(bf16[320,2048]{1,0:T(8,128)(2,1)S(1)} %get-tuple-element.54.wo_ref) | copy-start | bytes 3932164
  108.4 14.1 %all-to-all-start = ((bf16[16,2,3200]{2,1,0:T(2,128)(2,1)}), bf16[16,2,3200]{2,1,0:T(2,128)(2,1)S(1)}, u32[]{:S(2)}, u32[]{:S(2)}) async-start(bf16[16,2,3200]{2,1,0:T(2,128)(2,1)} %reshape.199), calls=%async_computation | async-start | bytes 409600 | tf_op jit(solution)/shard_map/all_to_all | solution.py:1781
  116.3 89.1 %copy-start.15 = (f32[1,2048]{1,0:T(1,128)}, f32[1,2048]{1,0:T(1,128)S(1)}, u32[]{:S(2)}) copy-start(f32[1,2048]{1,0:T(1,128)S(1)} %get-tuple-element.152.gain_ref) | copy-start | bytes 24580
  125.8 79.5 %copy-start.12 = (bf16[128,3072]{1,0:T(8,128)(2,1)S(1)}, bf16[128,3072]{1,0:T(8,128)(2,1)}, u32[]{:S(2)}) copy-start(bf16[128,3072]{1,0:T(8,128)(2,1)} %up_ref.1) | copy-start | bytes 2359300
  125.8 79.5 %copy-start.13 = (bf16[3072,128]{1,0:T(8,128)(2,1)S(1)}, bf16[3072,128]{1,0:T(8,128)(2,1)}, u32[]{:S(2)}) copy-start(bf16[3072,128]{1,0:T(8,128)(2,1)} %down_ref.1) | copy-start | bytes 2359300
  205.4 1.2 copy-start.5
  323.9 1.1 copy-start.3
  325.0 1.6 copy-start.8
  326.6 1.7 copy-start.9
  352.3 1.3 copy-start.10
  353.7 1.3 copy-start.11
  489.5 97.4 %copy-start.25 = (f32[8,2048]{1,0:T(8,128)S(1)}, f32[8,2048]{1,0:T(8,128)}, u32[]{:S(2)}) copy-start(f32[8,2048]{1,0:T(8,128)} %get-tuple-element.82) | copy-start | bytes 196612
  685.5 11.4 %all-to-all-start.2 = ((f32[32,1,896]{2,1,0:T(1,128)}), f32[32,1,896]{2,1,0:T(1,128)S(1)}, u32[]{:S(2)}, u32[]{:S(2)}) async-start(f32[32,1,896]{2,1,0:T(1,128)} %all_to_all.22), calls=%async_computation.2 | async-start | bytes 229376 | tf_op jit(solution)/shard_map/all_to_all | solution.py:1854
  691.2 9.7 %copy-start.16 = (f32[2,176,2048]{2,1,0:T(8,128)S(1)}, f32[2,176,2048]{2,1,0:T(8,128)}, u32[]{:S(2)}) copy-start(f32[2,176,2048]{2,1,0:T(8,128)} %get-tuple-element.77) | copy-start | bytes 8650756
  700.9 1.6 copy-start.23
  702.5 1.3 copy-start.22
  702.5 2.2 copy-start.21
  703.8 1.7 copy-start.18
  705.5 2.0 copy-start.19
  707.5 2.0 copy-start.17

commit v4 on v3

--- a/solution.py
+++ b/solution.py
@@ -16,6 +16,7 @@
 AXES = ("dx", "dc", "zh", "zl", "mp")
 BF = jnp.bfloat16
 F32 = jnp.float32
+LANES = 384
 
 
 def swap_pairs(sizes, partner):
@@ -255,7 +256,11 @@
     return lambda first, count: ref.at[:, pl.ds(pl.multiple_of(first * unit, unit), count * unit)]
 
 
-def first_kernel(tok_ref, ig_ref, o_ref, all_ref, wig_ref, wo_ref, send, recv, local):
+def first_kernel(
+    weight_ref, source_ref, tok_ref, cot_ref, ig_ref, o_ref, gates_ref, small_ref, gate_ref,
+    all_ref, wig_ref, wo_ref, wide_ref, ch_ref, gains_ref, dms_ref, dout_ref, own_ref, wg_ref,
+    pieces, smalls, dm, send, recv, local,
+):
     p = Place()
     links = Links(send, recv, local)
     drows = ig_ref.shape[1]
@@ -270,21 +275,91 @@
         column_blocks(wo_ref, o_ref.shape[1]),
         drows,
     )
+    unit = gates_ref.shape[1]
+    w_g = WeightGather(p, links, lambda j: gates_ref.at[j], row_blocks(pieces, unit), unit)
+    w_s = WeightGather(p, links, lambda j: small_ref, row_blocks(smalls, 16), 16)
+    w_gate = slot_columns(p, links, gate_ref, wg_ref)
+    adjoint = TokenGatherTwice(p, links, dm, dms_ref)
+    w_s.begin()
     w_ig.begin((1,))
     w_ig.begin((0,))
+    w_g.begin((0,))
     w_o.begin((0,))
     gather.begin()
+    own = links.keep(tok_ref.at[p.mp], own_ref)
+    scales = [weight_ref[source_ref[m, 0]] for m in range(2)]
+    for m in range(2):
+
+        def scale(rows, m=m):
+            value = cot_ref[m, rows, :].astype(F32) * scales[m]
+            dm[m, rows, :] = value.astype(BF)
+
+            @pl.when(p.mp == m)
+            def _():
+                dout_ref[rows, :] = value
+
+        chunks(cot_ref.shape[1], scale, 1)
     w_ig.onward(0)
+    w_s.onward(0)
+    w_g.onward(0)
     w_o.onward(0)
+    w_g.begin((1,))
     w_o.begin((1,))
+    w_gate.begin((0,))
+    w_s.onward(1)
+    gather.forward()
     w_ig.onward(1)
-    gather.forward()
+    w_gate.begin((1,))
+    adjoint.begin()
     gather.forward_core()
+    w_gate.onward(0)
+    w_g.onward(1)
     w_o.onward(1)
+    adjoint.forward()
+    w_gate.onward(1, (0,))
+    adjoint.forward_core()
+    w_s.end()
+    count = small_channels(local_channels=crows)
+    table = jnp.zeros((8, LANES), F32)
+    for k in range(4):
+        at = pl.ds(pl.multiple_of((p.slot() * 4 + k) * 16, 16), 16)
+        rows = smalls[at, :].astype(F32)[:8]
+        rows = jnp.concatenate([rows, jnp.zeros((8, LANES - 128), F32)], axis=1)
+        table = table + (pltpu.roll(rows, k * count, 1) if k else rows)
+    ch_ref[...] = table
+    for k in range(16):
+        rows = smalls[k * 16 : (k + 1) * 16, :].astype(F32)
+        gains_ref[:, k * 128 : (k + 1) * 128] = rows[8:10]
+    w_g.end()
+    size = crows // 2
+    per = size // 16
+    total = jnp.zeros(wide_ref.shape, F32)
+    row = lax.broadcasted_iota(jnp.int32, (LANES, pieces.shape[0]), 0)
+    column = lax.broadcasted_iota(jnp.int32, (LANES, pieces.shape[0]), 1)
+    source = lax.broadcasted_iota(jnp.int32, (LANES, 2 * LANES), 0)
+    target = lax.broadcasted_iota(jnp.int32, (LANES, 2 * LANES), 1)
+    for h in range(2):
+        r = column % 32 - h * 16
+        wanted = (r >= 0) & (r < per) & (row == h * size + column // 32 * per + r)
+        rows = dot(jnp.where(wanted, 1.0, 0.0).astype(BF), pieces[...], NN, BF)
+        gate = target // LANES
+        wanted = (source == target - gate * LANES - h * size + gate * size) & (
+            (source >= gate * size) & (source < (gate + 1) * size)
+        )
+        total = total + dot(rows, jnp.where(wanted, 1.0, 0.0).astype(BF), NN)
+    wide_ref[...] = total.astype(BF)
+    w_gate.onward(1, (1,))
+    own.wait()
     gather.end()
+    adjoint.end()
+    w_gate.end()
     w_ig.end()
     w_o.end()
     links.finish()
+
+
+def small_channels(local_channels):
+    return local_channels // 4
 
 
 class TokenGatherTwice:
@@ -396,15 +471,17 @@
         self.to_core = buffers[5] if len(buffers) > 5 else None
         self.parts = parts or [(0, self.mine.shape[1])]
         self.blocks = [(mp, zl) for mp in (1, 0) for zl in (1, 0)]
+        self.kept = {}
         n = range(len(self.parts))
         self.core = {(h, block): links.pair() for h in n for block in self.blocks}
         self.y = {(h, zl): links.pair() for h in n for zl in (1, 0)}
         self.z = {h: links.pair() for h in n}
 
-    def begin(self):
+    def begin(self, mps=(1, 0)):
         p = self.place
-        self.kept = {}
         for mp, zl in self.blocks:
+            if mp not in mps:
+                continue
             i, block = mp * 2 + zl, p.rows(dc=1, mp=mp, zl=zl)
             if self.to_core is None:
                 src = self.source.at[block]
@@ -416,8 +493,7 @@
                 self.links.start(
                     src.at[at], self.from_core.at[i, at], self.core[h, (mp, zl)], p.peer(dc=1)
                 )
-        for mp, zl in self.blocks:
-            i, block = mp * 2 + zl, p.rows(mp=mp, zl=zl)
+            block = p.rows(mp=mp, zl=zl)
             if self.to_core is None:
                 self.kept[mp, zl] = self.links.keep(self.source.at[block], self.mine.at[i])
             else:
@@ -520,11 +596,12 @@
         down_ref.shape[1],
     )
     gathers = [TokenGather(p, links, normed, all_ref, part) for part in parts]
-    scatter.begin()
     w_u.begin((1,))
+    scatter.begin((1,))
     w_u.begin((0,))
     scatter.across_y(0)
     scatter.across_y(1)
+    scatter.begin((0,))
     w_d.begin((0,))
     w_u.onward(0)
 
@@ -671,15 +748,19 @@
 
 
 def third_kernel(
-    wg_ref, wu_ref, wd_ref, mid_ref, dout_ref, gain_ref, dm_ref, hidden_ref, n2_ref, dgm_ref,
+    wg_ref, wu_ref, wd_in, mid_in, dout_in, gain_ref, dm_ref, hidden_ref, n2_ref, dgm_ref,
     dup_ref,
     dr1_ref, gain_out, all_ref, gate_out, down_out, part_out,
     *scratch,
 ):
     p = Place()
     links = Links(*scratch[-3:])
-    do = scratch[-4]
+    do, wd_ref, mid_ref, dout_ref = scratch[-7:-3]
     rows_of = mid_ref.shape[0]
+    staged = [
+        links.keep(src, dst)
+        for src, dst in ((mid_in, mid_ref), (dout_in, dout_ref), (wd_in, wd_ref))
+    ]
     greet(weight_peers(p))
 
     def product(b):
@@ -691,14 +772,17 @@
     down = GradScatter(p, links, dm_ref, hidden_ref, scratch[6:13])
     gate = GradScatter(p, links, n2_ref, dgm_ref, scratch[13:20])
     gathers = [TokenGather(p, links, do, all_ref, part) for part in parts]
-    scatter.begin()
+    scatter.begin((1,))
     down.begin(1)
     scatter.across_y(0)
     scatter.across_y(1)
+    scatter.begin((0,))
     gate.begin(1)
     down.across(0)
     down.across(1)
     gain_out[...] = jnp.zeros_like(gain_out)
+    for copy in staged:
+        copy.wait()
 
     def back(rows):
         part, gain = norm_back(mid_ref[rows, :], gain_ref[...], scatter.total(rows))
@@ -770,12 +854,13 @@
     out = GradScatter(p, links, do_ref, mixed_ref, scratch[6:13])
     wide = GradScatter(p, links, n1_ref, dboth_ref, scratch[13:20])
     gates = Ready(p, links, gg_ref, None, scratch[20:26])
+    scatter.begin((1,))
     out.begin(1)
-    scatter.begin()
+    scatter.across_y(0)
+    scatter.across_y(1)
     wide.begin(1)
-    scatter.across_y(0)
+    scatter.begin((0,))
     gates.begin(1)
-    scatter.across_y(1)
     for g in (out, wide, gates):
         g.across(0)
         g.across(1)
@@ -899,22 +984,53 @@
     )(*args)
 
 
-def fetch_first(tokens, input_weight, gelu_weight, output_weight):
+def fetch_first(
+    tokens, cotangent, seq_source, source_weight, input_weight, gelu_weight, output_weight,
+    decay_gates, input_gates, channel_params, norm_gains, mlp_gate,
+):
+    args = (
+        tokens, cotangent, seq_source, source_weight, input_weight, gelu_weight, output_weight,
+        decay_gates, input_gates, channel_params, norm_gains, mlp_gate,
+    )
     if not shape_fits():
-        return plain_fetch_first(tokens, input_weight, gelu_weight, output_weight)
+        return plain_fetch_first(*args)
     rows, width = tokens.shape[1:]
     drows, local = input_weight.shape[0], input_weight.shape[1] // 4
     pairs = [v.reshape(drows, 4, local) for v in (input_weight, gelu_weight)]
     ig = jnp.concatenate(pairs, axis=2).transpose(1, 0, 2)
+    per = decay_gates.shape[1] // BLOCK
+    gates = [v.reshape(8, per, BLOCK) for v in (decay_gates, input_gates)]
+    gates = jnp.concatenate(gates, axis=2)
+    gates = jnp.pad(gates, ((0, 0), (0, 16 - per), (0, LANES - 2 * BLOCK))).reshape(4, 32, LANES)
+    small = jnp.pad(channel_params[:, 0], ((0, 0), (0, drows - channel_params.shape[2])))
+    small = jnp.pad(jnp.concatenate([small, norm_gains], axis=0), ((0, 6), (0, 0)))
+    smem = pl.BlockSpec(memory_space=pltpu.SMEM)
     return run_kernel(
         first_kernel,
         "fetch_first",
-        [((8, rows, width), BF), ((width, 2 * local), BF), ((local, width), BF)],
-        [ANY] * 3,
-        [ANY] * 3,
-        semaphores(32, 8),
+        [
+            ((8, rows, width), BF),
+            ((width, 2 * local), BF),
+            ((local, width), BF),
+            ((LANES, 2 * LANES), BF),
+            ((8, LANES), F32),
+            ((2, width), F32),
+            ((8, rows, width), BF),
+            ((rows, width), F32),
+            ((rows, width), BF),
+            ((width, mlp_gate.shape[1] // 4), BF),
+        ],
+        [ANY] * 3 + [VMEM] * 3 + [ANY, VMEM, ANY, ANY],
+        [smem, smem, ANY, VMEM] + [ANY] * 5,
+        [
+            pltpu.VMEM((512, LANES), BF),
+            pltpu.VMEM((256, 128), BF),
+            pltpu.VMEM((2, rows, width), BF),
+        ]
+        + semaphores(80, 16),
         1,
-        (tokens, ig, output_weight),
+        (source_weight, seq_source, tokens, cotangent, ig, output_weight, gates, small, mlp_gate),
+        61,
     )
 
 
@@ -954,11 +1070,12 @@
             ((8, rows, width), BF),
         ],
         [VMEM, VMEM, ANY] + [VMEM] * 2 + [ANY],
-        [VMEM] * 6 + [ANY, VMEM] * 2 + [VMEM],
+        [VMEM] * 2 + [ANY] * 3 + [VMEM] + [ANY, VMEM] * 2 + [VMEM],
         scatter_buffers(rows, width, True)
         + grad_buffers(2 * drows, ff, 8 * rows) * 2
-        + [pltpu.VMEM((rows, width), BF)]
-        + semaphores(56, 48),
+        + [pltpu.VMEM((rows, width), BF), pltpu.VMEM((ff, width), BF)]
+        + [pltpu.VMEM((rows, width), F32)] * 2
+        + semaphores(56, 56),
         3,
         (*weights, middle, dout, gain, dm, hidden, n2, dgm, dup),
         61,
@@ -999,13 +1116,54 @@
     return all(lax.axis_size(n) == 2 for n in AXES)
 
 
-def plain_fetch_first(tokens, input_weight, gelu_weight, output_weight):
+def plain_fetch_first(
+    tokens, cotangent, seq_source, source_weight, input_weight, gelu_weight, output_weight,
+    decay_gates, input_gates, channel_params, norm_gains, mlp_gate,
+):
     exchange = Tokens()
-    own = lax.dynamic_index_in_dim(tokens, exchange.mp, 0, keepdims=False)
+    dxn, zhn, mp = lax.axis_size("dx"), lax.axis_size("zh"), exchange.mp
+    group = dxn * 2 * zhn * 2
+    local = input_weight.shape[1] // 4
+    heads, piece = decay_gates.shape[0] // 4, decay_gates.shape[1]
+    shards = ("dx", "dc", "zh", "zl")
+    own = lax.dynamic_index_in_dim(tokens, mp, 0, keepdims=False)
+    sources = jnp.arange(source_weight.shape[0], dtype=jnp.int32)
+    scales = jnp.sum(jnp.where(seq_source == sources[None], source_weight[None], 0.0), axis=1)
+    douts = cotangent.astype(F32) * scales[:, None, None]
+    small = jnp.concatenate([channel_params.reshape(-1), norm_gains.reshape(-1)])
+    small = lax.all_to_all(
+        jnp.broadcast_to(small[None], (group, small.size)), shards, 0, 0, tiled=True
+    )
+    nch = channel_params.size
+    channels = small[:, :nch].reshape(group, 8, -1).transpose(1, 0, 2).reshape(8, -1)
+    slot = exchange.dc * 2 + exchange.zl
+    channels = lax.dynamic_slice_in_dim(channels, slot * local, local, 1).astype(F32)
+    gains = small[:, nch:].reshape(group, 2, -1).transpose(1, 0, 2).reshape(2, -1).astype(F32)
+    gates = jnp.stack([decay_gates, input_gates]).reshape(2, 4, heads, piece)
+    gates = gates.transpose(1, 0, 2, 3).reshape(2, 1, 2, 1, 2 * heads * piece)
+    gates = jnp.broadcast_to(gates, (2, zhn, 2, dxn, 2 * heads * piece))
+    gates = gates.transpose(3, 0, 1, 2, 4).reshape(group, 2 * heads * piece)
+    gates = lax.all_to_all(gates, shards, 0, 0, tiled=True)
+    gates = gates.reshape(group, 2 * heads, piece).transpose(1, 0, 2)
+    gates = gates.reshape(2, heads, BLOCK, BLOCK)
+    zero = jnp.zeros((BLOCK, BLOCK), BF)
+    blocks = [
+        [gates[g, h] if k == h else zero for g in range(2) for k in range(heads)]
+        for h in range(heads)
+    ]
     return (
         exchange.gather(own).reshape((8,) + own.shape),
         fetch_weight([input_weight, gelu_weight], 4),
         fetch_weight([output_weight.T], 4).T,
+        jnp.concatenate([jnp.concatenate(v, axis=1) for v in blocks], axis=0),
+        channels,
+        gains,
+        exchange.gather(lax.dynamic_index_in_dim(douts, mp, 0, keepdims=False).astype(BF)).reshape(
+            (8,) + own.shape
+        ),
+        lax.dynamic_index_in_dim(douts, mp, 0, keepdims=False),
+        own,
+        fetch_weight([mlp_gate], 4),
     )
 
 
@@ -1166,18 +1324,11 @@
 TN = ((0,), (0,))
 
 
-LANES = 384
-
-
 def minus_expm1(v):
     series = 1.0 + v / 8.0
     for k in (7.0, 6.0, 5.0, 4.0, 3.0, 2.0):
         series = 1.0 + v * (1.0 / k) * series
     return jnp.where(v > -0.4, -v * series, 1.0 - jnp.exp(v))
-
-
-def pad_lanes(v, fill=0.0):
-    return jnp.pad(v, ((0, 0), (0, LANES - v.shape[1])), constant_values=fill)
 
 
 def loop(count, body, unroll=1):
@@ -1204,20 +1355,16 @@
 
 
 def recur_forward_kernel(
-    tok_ref, wig_ref, blocks_ref, ch_ref, gain_ref, cot_ref, gate_ref,
-    n1_out, xs, gy, u, siga, sigi, decay, states, mixed, dm_ref, wg_ref,
-    run, logits, n1, both, halo, ends, inc, tok, sems, send, recv, local_sems,
+    tok_ref, wig_ref, blocks_ref, ch_ref, gain_ref,
+    n1_out, xs_out, gy_out, u_out, siga_out, sigi_out, decay_out, states, mixed,
+    xs, gy, u, siga, sigi, decay, run, logits, n1, both, halo, ends, inc, tok, sems,
+    send, recv, local_sems,
 ):
     p = Place()
     links = Links(send, recv, local_sems)
     rows, local = tok_ref.shape[1], wig_ref.shape[1] // 2
     zh = p.zh
-    greet(weight_peers(p))
-    w_g = slot_columns(p, links, gate_ref, wg_ref)
-    adjoint = TokenGatherTwice(p, links, cot_ref, dm_ref)
-    w_g.begin((1,), (0,))
-    w_g.begin((0,))
-    adjoint.begin()
+    greet([p.peer(zh=1)])
 
     def read(b):
         return pltpu.make_async_copy(tok_ref.at[b], tok.at[b % 2], sems.at[4 + b % 2])
@@ -1269,10 +1416,8 @@
         return at
 
     at = to_partner(xs.at[:, pl.ds(2 * rows, 8)], halo)
-    w_g.onward(0)
-    adjoint.forward()
+    kept = [links.keep(gy, gy_out)]
     links.arrived(halo, at)
-    w_g.begin((1,), (1,))
     row = lax.broadcasted_iota(jnp.int32, (8, LANES), 0)
     soft = ch_ref[0:1, :]
 
@@ -1297,7 +1442,7 @@
     loop(8, convolve)
 
     def tile(i, carry, zl):
-        at = pl.ds(eight(i), 8)
+        at = pl.ds(pl.multiple_of(i * CHUNK, CHUNK), CHUNK)
         out = []
         for seg in range(4):
             b = seg * 2 + zl
@@ -1310,23 +1455,26 @@
             siga[b, at, :] = sa
             sigi[b, at, :] = si
             decay[b, at, :] = a
-            pa, h = tile_scan(a, drive, row, False)
-            h = h + pa * ch
-            pa = pa * cp
-            run[b, at, :] = pa
-            states[seg, pl.ds(pl.multiple_of(8 + zl * rows + i * 8, 8), 8), :] = h
-            out.append((pa[7:8, :], h[7:8, :]))
+            for k in range(2):
+                pa, h = tile_scan(a[k * 8 : k * 8 + 8], drive[k * 8 : k * 8 + 8], row, False)
+                h = h + pa * ch
+                pa = pa * cp
+                run[b, pl.ds(eight(i * 2 + k), 8), :] = pa
+                there = pl.ds(pl.multiple_of(8 + zl * rows + i * CHUNK + k * 8, 8), 8)
+                states[seg, there, :] = h
+                cp, ch = pa[7:8, :], h[7:8, :]
+            out.append((cp, ch))
         return tuple(out)
 
+    kept += [links.keep(xs, xs_out), links.keep(u, u_out)]
     carry = ((jnp.ones((1, LANES), F32), jnp.zeros((1, LANES), F32)),) * 4
     for zl in range(2):
-        carry = lax.fori_loop(0, rows // 8, functools.partial(tile, zl=zl), carry)
+        carry = lax.fori_loop(0, rows // CHUNK, functools.partial(tile, zl=zl), carry)
     ends[...] = jnp.zeros_like(ends)
     for seg in range(4):
         ends[seg : seg + 1, :] = carry[seg][1]
     at = to_partner(ends, inc)
-    adjoint.forward_core()
-    w_g.onward(1, (0,))
+    kept += [links.keep(siga, siga_out), links.keep(sigi, sigi_out), links.keep(decay, decay_out)]
     links.arrived(inc, at)
 
     def finish(b):
@@ -1348,16 +1496,16 @@
         chunks(rows, state)
 
     loop(8, finish)
-    w_g.onward(1, (1,))
-    adjoint.end()
-    w_g.end()
+    for copy in kept:
+        copy.wait()
     links.finish()
 
 
 def recur_backward_kernel(
     do_ref, wo_ref, blocks_ref, ch_ref,
-    xs, gy, u, siga, sigi, decay, states, rows_ref, mid_ref, n2_ref, dup_ref,
+    xs_in, gy, u_in, siga_in, sigi_in, decay_in, states, rows_ref, mid_in, n2_ref, dup_ref,
     dboth_out, gb_out, ch_out, block_out, up_out,
+    xs, u, siga, sigi, decay, mid_ref,
     dh, after, dgy, dlog_ref, du, dboth, halo, ends, inc, do, final, sems,
     *scratch,
 ):
@@ -1373,6 +1521,17 @@
         return pltpu.make_async_copy(do_ref.at[b], do.at[b % 2], sems.at[4 + b % 2])
 
     read(0).start()
+    kept = {
+        name: links.keep(src, dst)
+        for name, src, dst in (
+            ("decay", decay_in, decay),
+            ("siga", siga_in, siga),
+            ("sigi", sigi_in, sigi),
+            ("u", u_in, u),
+            ("xs", xs_in, xs),
+            ("mid", mid_in, mid_ref),
+        )
+    }
     up.begin(1)
     scatter.begin()
     ch_out[...] = jnp.zeros_like(ch_out)
@@ -1428,6 +1587,7 @@
         return tuple(out)
 
     carry = ((one, jnp.zeros((1, LANES), F32), one),) * 4
+    kept["decay"].wait()
     for zl in (1, 0):
         carry = lax.fori_loop(0, rows // 8, functools.partial(tile, zl=zl), carry)
     for seg in range(4):
@@ -1435,7 +1595,6 @@
     at = to_partner(ends, inc)
     links.arrived(inc, at)
     up.across(0)
-    scatter.across_z()
 
     def gradients(b):
         seg, zl = b // 2, b % 2
@@ -1471,8 +1630,11 @@
 
     lane = lax.broadcasted_iota(jnp.int32, (1, LANES), 1)
     real = lane < local
+    for name in ("siga", "sigi", "u"):
+        kept[name].wait()
     loop(8, gradients)
     at = to_partner(du.at[:, pl.ds(0, 8)], halo)
+    scatter.across_z()
     up.across(1)
 
     def write(i, at, src, dst, base):
@@ -1514,18 +1676,17 @@
         for i in (2, 3):
             write(i % 2, i * 2 + zl, dboth, dboth_out, 0).wait()
 
+    kept["xs"].wait()
+    kept["mid"].wait()
     loop(4, functools.partial(convolve, zl=0))
     drain(0)
-    up.last(0)
     links.arrived(halo, at)
 
     def tail(seg):
         du[seg, pl.ds(2 * rows, 8), :] = jnp.where(zh == 0, halo[seg], 0.0)
 
     loop(4, tail)
-    loop(4, functools.partial(convolve, zl=1))
-    drain(1)
-    up.last(1)
+    loop(2, functools.partial(convolve, zl=1))
     scatter.arrive()
 
     def add(at):
@@ -1534,39 +1695,42 @@
     chunks(rows, add)
     at = links.pair()
     links.start(final, block_out.at[p.mp], at, p.peer(mp=1))
-    kept = links.keep(final, block_out.at[p.mp])
+    own = links.keep(final, block_out.at[p.mp])
+    loop(2, lambda i: convolve(i + 2, 1))
+    up.last(0)
+    drain(1)
+    up.last(1)
     up.end()
     ff = up.result.shape[2]
     for j in range(4):
         up_out[:, j * ff : (j + 1) * ff] = up.result[j].astype(F32)
-    kept.wait()
+    own.wait()
     links.arrived(block_out.at[1 - p.mp], at)
     links.finish()
 
 
-def recur_forward(tokens, w_ig, blocks, channels, gain, dm, mlp_gate):
+def recur_forward(tokens, w_ig, blocks, channels, gain):
     if not shape_fits():
-        return plain_recur_forward(tokens, w_ig, blocks, channels, gain, dm, mlp_gate)
-    ff, drows = mlp_gate.shape[1] // 4, mlp_gate.shape[0]
+        return plain_recur_forward(tokens, w_ig, blocks, channels, gain)
     rows, width = tokens.shape[1:]
     local = w_ig.shape[1] // 2
-    soft = jax.nn.softplus(-channels[0:1])
-    table = jnp.concatenate([soft, channels[1:]], axis=0)
-    table = pad_lanes(table)
-    wide = jnp.concatenate(
-        [jnp.pad(blocks[:, g * local : (g + 1) * local], ((0, LANES - local),) * 2) for g in (0, 1)],
-        axis=1,
-    )
+    table = jnp.concatenate([jax.nn.softplus(-channels[0:1]), channels[1:]], axis=0)
     f, h = (8, rows, LANES), (4, 2 * rows + 8, LANES)
     n1, *saved = run_kernel(
         recur_forward_kernel,
         "recur_forward",
         [(tokens.shape, BF), (h, F32), (f, F32), (f, BF)]
         + [(f, F32)] * 3
-        + [(h, F32), (f, BF), (tokens.shape, BF), ((width, ff), BF)],
-        [ANY] + [VMEM] * 8 + [ANY] * 2,
-        [ANY] + [VMEM] * 4 + [ANY] * 2,
+        + [(h, F32), (f, BF)],
+        [ANY] * 7 + [VMEM] * 2,
+        [ANY] + [VMEM] * 4,
         [
+            pltpu.VMEM(h, F32),
+            pltpu.VMEM(f, F32),
+            pltpu.VMEM(f, BF),
+            pltpu.VMEM(f, F32),
+            pltpu.VMEM(f, F32),
+            pltpu.VMEM(f, F32),
             pltpu.VMEM(f, F32),
             pltpu.VMEM((8, rows, 2 * LANES), F32),
             pltpu.VMEM((2, rows, width), BF),
@@ -1577,13 +1741,13 @@
             pltpu.VMEM((2, rows, width), BF),
         ]
         + semaphores(6, 2)[:1]
-        + semaphores(24, 8),
+        + semaphores(2, 6),
         5,
-        (tokens, w_ig, wide, table, gain, dm, mlp_gate),
-        56,
-    )
-    *saved, mixed, dm, w_g = saved
-    return n1.reshape(-1, width), mixed.reshape(-1, LANES), (table, wide, *saved), dm, w_g
+        (tokens, w_ig, blocks, table, gain),
+        61,
+    )
+    *saved, mixed = saved
+    return n1.reshape(-1, width), mixed.reshape(-1, LANES), (table, blocks, *saved)
 
 
 def recur_backward(do, saved, w_o, channels, out_part, middle, n2, dup, drows):
@@ -1605,8 +1769,14 @@
             ((drows, 4 * ff), F32),
         ],
         [ANY] + [VMEM] * 2 + [ANY, VMEM],
-        [ANY] + [VMEM] * 10 + [ANY, VMEM, ANY, VMEM],
+        [ANY] + [VMEM] * 3 + [ANY, VMEM] + [ANY] * 4 + [VMEM] + [ANY] * 3 + [VMEM],
         [
+            pltpu.VMEM(h, F32),
+            pltpu.VMEM(f, BF),
+            pltpu.VMEM(f, F32),
+            pltpu.VMEM(f, F32),
+            pltpu.VMEM(f, F32),
+            pltpu.VMEM((rows, width), F32),
             pltpu.VMEM(f, F32),
             pltpu.VMEM(f, F32),
             pltpu.VMEM(f, BF),
@@ -1622,14 +1792,14 @@
         + semaphores(6, 2)[:1]
         + scatter_buffers(rows, width)
         + grad_buffers(2 * drows, ff, 8 * rows)
-        + semaphores(32, 24),
+        + semaphores(32, 32),
         6,
         (do, w_o, wide, table, xs, gy, u, siga, sigi, decay, states)
         + (out_part, middle, n2, dup),
         61,
     )
     sums = jnp.sum(sums, axis=1)[:, :local]
-    dlam = sums[0] * DECAY_SCALE * jax.nn.sigmoid(-channels[0])
+    dlam = sums[0] * DECAY_SCALE * jax.nn.sigmoid(-channels[0, :local])
     g_blocks = jnp.concatenate(
         [g_blocks[:local, g * LANES : g * LANES + local] for g in (0, 1)], axis=1
     )
@@ -1642,7 +1812,7 @@
     )
 
 
-def plain_recur_forward(tokens, w_ig, blocks, channels, gain, dm, mlp_gate):
+def plain_recur_forward(tokens, w_ig, blocks, channels, gain):
     length, local, width = tokens.shape[1], w_ig.shape[1] // 2, tokens.shape[2]
     wide = tokens.reshape(-1, width).astype(F32)
     n1 = (wide * inverse_rms(wide) * gain).astype(BF)
@@ -1667,15 +1837,7 @@
     gelu_y, slope_y = gelu_both(gy)
     mixed = (gelu_y * states).astype(BF).reshape(-1, local)
     saved = (blocks, padded, u, sig_a, sig_i, decay, root, running, incoming, states)
-    exchange = Tokens()
-    dm = exchange.gather(lax.dynamic_index_in_dim(dm, exchange.mp, 0, keepdims=False))
-    return (
-        n1,
-        mixed,
-        saved + (gelu_y, slope_y),
-        dm.reshape(8, length, width),
-        fetch_weight([mlp_gate], 4),
-    )
+    return n1, mixed, saved + (gelu_y, slope_y)
 
 
 def plain_recur_backward(do, saved, w_o, channels, out_part, middle, n2, dup, drows):
@@ -1745,56 +1907,22 @@
     drows = input_weight.shape[0]
     piece = decay_gates.shape[1]
 
-    own = lax.dynamic_index_in_dim(tokens_in[:, 0], mp, 0, keepdims=False)
-    scales = jnp.stack(
-        [
-            jnp.sum(
-                jnp.where(
-                    jnp.arange(source_weight.shape[0], dtype=jnp.int32) == seq_source[m, 0],
-                    source_weight,
-                    0.0,
-                )
-            )
-            for m in range(2)
-        ]
-    )
-    douts = cotangent[:, 0].astype(F32) * scales[:, None, None]
-    dout = lax.dynamic_index_in_dim(douts, mp, 0, keepdims=False)
-
-    small = jnp.concatenate([channel_params.reshape(-1), norm_gains.reshape(-1)])
-    shards = ("dx", "dc", "zh", "zl")
-    small = lax.all_to_all(
-        jnp.broadcast_to(small[None], (group, small.size)), shards, 0, 0, tiled=True
-    )
-    nch = channel_params.size
-    channels = small[:, :nch].reshape(group, 8, -1).transpose(1, 0, 2).reshape(8, -1)
-    channels = lax.dynamic_slice_in_dim(channels, slot * local, local, 1).astype(F32)
-    gains = small[:, nch:].reshape(group, 2, -1).transpose(1, 0, 2).reshape(2, -1).astype(F32)
-
-    ff = mlp_gate.shape[1] // 4
-    tokens, w_ig, w_o = fetch_first(tokens_in[:, 0], input_weight, gelu_weight, output_weight)
-
-    gates = jnp.stack([decay_gates, input_gates]).reshape(2, 4, heads, piece)
-    gates = gates.transpose(1, 0, 2, 3).reshape(2, 1, 2, 1, 2 * heads * piece)
-    gates = jnp.broadcast_to(gates, (2, zhn, 2, dxn, 2 * heads * piece))
-    gates = gates.transpose(3, 0, 1, 2, 4).reshape(group, 2 * heads * piece)
-    gates = lax.all_to_all(gates, shards, 0, 0, tiled=True)
-    gates = gates.reshape(group, 2 * heads, piece).transpose(1, 0, 2)
-    gates = gates.reshape(2, heads, BLOCK, BLOCK)
-
-    zero = jnp.zeros((BLOCK, BLOCK), BF)
-    blocks = jnp.concatenate(
-        [
-            jnp.concatenate(
-                [gates[g, h] if k == h else zero for g in range(2) for k in range(heads)], axis=1
-            )
-            for h in range(heads)
-        ],
-        axis=0,
-    )
-    n1, mixed, saved, dm, w_g = recur_forward(
-        tokens, w_ig, blocks, channels, gains[0:1], douts.astype(BF), mlp_gate
-    )
+    tokens, w_ig, w_o, blocks, channels, gains, dm, dout, own, w_g = fetch_first(
+        tokens_in[:, 0],
+        cotangent[:, 0],
+        seq_source,
+        source_weight,
+        input_weight,
+        gelu_weight,
+        output_weight,
+        decay_gates,
+        input_gates,
+        channel_params,
+        norm_gains,
+        mlp_gate,
+    )
+
+    n1, mixed, saved = recur_forward(tokens, w_ig, blocks, channels, gains[0:1])
     middle, n2, w_u, w_d = reduce_and_fetch(mixed, w_o, own, gains[1:2], mlp_up, mlp_down)
 
     hidden, dgm, dup = feed_forward(n2, dm, w_g, w_u, w_d)

time: 717 us -> 680 us (0.948)
  starting transfers between devices: 17.3 us -> 3.49 us
  local copies, waits for them, and re-layouts: 44.3 us -> 33.4 us
  other arithmetic: 16.8 us -> 7.4 us
    all_to_all x2 -> x0, starting transfers between devices: 13.4 us -> none  [the longest x1 7.32 us: on_device(): lax.all_to_all(jnp.broadcast_to(small[None], (group, small.size)), shards...]
    unnamed x71 -> x61, local copies, waits for them, and re-layouts: 30.1 us -> 24.4 us
  transfers between devices with their start and end apart: 3 -> 1, of which waited for: 2 -> 1; matrix products, arithmetic and copies ran while one was open for 3% -> 0% of each run, Pallas kernels for 10% -> 0%
where the time goes in v4:
time: 680 us; the launch traced here: 673 us
  Pallas kernels  622 us (91%)
  local copies, waits for them, and re-layouts  33.4 us (5%)
  other arithmetic  7.4 us (1%)
    pallas_call x6, Pallas kernels, run_kernel(): pl.pallas_call(body, name=name, out_shape=[jax.ShapeDtypeStruct(*o) for o...  599 us
    unnamed x61, local copies, waits for them, and re-layouts  24.4 us
    pallas_call x1, Pallas kernels, feed_forward(): pl.pallas_call(mlp_kernel, name='feed_forward', grid=(blocks // 2,), in_s...  23.8 us
  transfers between devices with their start and end apart: 1, of which 1 were waited for; matrix products, arithmetic and copies ran while one was open for 0% of the time, Pallas kernels for 0%

profile of v4, /device:TPU:1, one launch (start us, length us, event | category | flops | bytes accessed | tf_op | source)
XLA Modules:
  0.0 673.2 jit_solution(5291075471325363395)
XLA Ops:
  0.7 1.2 copy.42
  1.9 0.2 copy.44
  2.1 1.2 copy.43
  3.3 0.2 copy.45
  3.6 0.1 reshape.137
  3.7 0.1 reshape.138
  3.8 0.6 copy.46.source_ref
  4.5 1.0 maximum_bitcast_fusion.ig_ref
  5.5 0.7 fusion.5
  6.3 0.6 pad.19.small_ref
  6.9 134.4 %fetch_first.1 = (bf16[8,176,2048]{2,1,0:T(8,128)(2,1)}, bf16[2048,640]{1,0:T(8,128)(2,1)}, bf16[320,2048]{1,0:T(8,128)(2,1)}, bf16[384,768]{1,0:T(8,128)(2,1)},...) custom-call(f32[8]{0:T(128)} %weight_ref.1, ...), custom_call_target="tpu_custom_call" | custom-call | tf_op jit(solution)/shard_map/fetch_first/pallas_call | solution.py:974
  141.3 0.7 slice.76
  142.0 0.7 compare_select_fusion
  142.7 1.4 fusion.10
  144.1 0.6 pad_maximum_fusion.3.ch_ref
  144.7 30.7 %recur_forward.1 = (bf16[8,176,2048]{2,1,0:T(8,128)(2,1)}, f32[4,360,384]{2,1,0:T(8,128)}, f32[8,176,384]{2,1,0:T(8,128)}, bf16[8,176,384]{2,1,0:T(8,128)(2,1)},...) custom-call(bf16[8,176,2048]{2,1,0:T(8,128)(2,1)} %get-tuple-element, ...), custom_call_target="tpu_custom_call" | custom-call | tf_op jit(solution)/shard_map/recur_forward/pallas_call | solution.py:974
  175.5 1.2 copy-done.2
  176.7 1.1 copy-done.9
  177.9 114.9 %reduce_and_fetch.1 = (f32[176,2048]{1,0:T(8,128)S(1)}, bf16[8,176,2048]{2,1,0:T(8,128)(2,1)}, bf16[2048,768]{1,0:T(8,128)(2,1)S(1)}, bf16[768,2048]{1,0:T(8,128)(2,1)S(1)}) custom-call(bf16[1408,384]{1,0:T(8,128)(2,1)S(1)} %bitcast.56, bf16[320,2048]{1,0:T(8,128)(2,1)S(1)} %copy-done.1, bf16[176,2048]{1,0:T(8,128)(2,1)S(1)} %copy-done.5, ...), custom_call_target="tpu_custom_call" | custom-call | tf_op jit(solution)/shard_map/reduce_and_fetch/pallas_call | solution.py:974
  292.8 1.1 copy-done
  293.9 1.6 copy-done.3
  295.5 1.7 copy-done.4
  297.2 23.8 %feed_forward.1 = (bf16[1408,768]{1,0:T(8,128)(2,1)S(1)}, bf16[1408,768]{1,0:T(8,128)(2,1)S(1)}, bf16[1408,768]{1,0:T(8,128)(2,1)}) custom-call(bf16[8,176,2048]{2,1,0:T(8,128)(2,1)} %get-tuple-element.69.n2_ref, bf16[8,176,2048]{2,1,0:T(8,128)(2,1)} %get-tuple-element.68.dm_ref, bf16[2048,768]{1,0:T(8,128)(2,1)} %get-tuple-element.55.wg_ref, ...), custom_call_target="tpu_custom_call" | custom-call | flops 13287555072 | bytes 11534336 | tf_op jit(solution)/shard_map/feed_forward/pallas_call | solution.py:950
  321.1 1.3 copy-done.6
  322.4 1.3 copy-done.7
  323.7 134.4 %reduce_and_return.1 = (f32[176,2048]{1,0:T(8,128)}, f32[8,2048]{1,0:T(8,128)}, bf16[8,176,2048]{2,1,0:T(8,128)(2,1)}, f32[128,3072]{1,0:T(8,128)}, f32[3072,128]{1,0:T(8,128)}, /*index=5*/bf16[8,176,2048]{2,1,0:T(8,128)(2,1)}) custom-call(bf16[2048,768]{1,0:T(8,128)(2,1)} %get-tuple-element.55.wg_ref, bf16[2048,768]{1,0:T(8,128)(2,1)} %copy-done.3, ...), custom_call_target="tpu_custom_call" | custom-call | tf_op jit(solution)/shard_map/reduce_and_return/pallas_call | solution.py:974
  458.1 90.8 %recur_backward.1 = (bf16[8,176,640]{2,1,0:T(8,128)(2,1)}, f32[384,768]{1,0:T(8,128)}, f32[8,8,384]{2,1,0:T(8,128)}, bf16[2,176,2048]{2,1,0:T(8,128)(2,1)}, f32[128,3072]{1,0:T(8,128)}) custom-call(bf16[8,176,2048]{2,1,0:T(8,128)(2,1)} %get-tuple-element.73.do_ref, bf16[320,2048]{1,0:T(8,128)(2,1)} %get-tuple-element.62.wo_ref, ...), custom_call_target="tpu_custom_call" | custom-call | tf_op jit(solution)/shard_map/recur_backward/pallas_call | solution.py:974
  549.0 0.9 reduce_sum.38
  549.9 0.7 fusion.8
  550.6 1.3 convert.25
  552.0 0.1 slice_bitcast_fusion.3
  552.2 0.3 reshape.146
  552.5 0.1 copy.47
  552.6 0.2 reshape.147
  552.8 0.8 reshape.148.gg_ref
  553.7 93.4 %return_last.1 = (f32[2,176,2048]{2,1,0:T(8,128)}, f32[8,2048]{1,0:T(8,128)}, f32[128,1280]{1,0:T(8,128)}, f32[128,1280]{1,0:T(8,128)}, f32[1280,128]{1,0:T(8,128)}, /*index=5*/bf16[4,64,128]{2,1,0:T(8,128)(2,1)}) custom-call(bf16[2048,640]{1,0:T(8,128)(2,1)} %get-tuple-element.57.wig_ref, bf16[176,2048]{1,0:T(8,128)(2,1)} %get-tuple-element.63.own_ref, ...), custom_call_target="tpu_custom_call" | custom-call | tf_op jit(solution)/shard_map/return_last/pallas_call | solution.py:974
  647.1 0.9 reduce_sum.36
  648.1 0.1 concatenate.32
  648.1 0.1 concatenate.33
  648.3 0.1 broadcast_in_dim.80
  648.4 0.1 broadcast_in_dim.76
  648.4 0.1 broadcast_in_dim.77
  648.5 0.1 broadcast_select_fusion.1
  648.7 0.1 broadcast_in_dim.74
  648.8 0.1 broadcast_select_fusion
  648.9 0.7 all_to_all.6
  649.7 3.5 all-to-all-start
  653.2 0.9 copy.58
  654.1 0.1 reshape.152
  654.3 0.7 squeeze.20
  654.9 0.7 squeeze.21
  655.6 5.1 all-to-all-done
  660.7 0.1 reduce_sum.39
  660.8 0.6 slice_bitcast_fusion.4
  661.3 0.7 reshape.151
  662.0 2.6 copy.68
  664.6 1.6 copy.69
  666.2 0.8 copy.70
  667.1 0.8 copy.71
  667.9 0.8 copy.72
  668.7 1.1 copy.73
  669.9 1.1 copy.74
  671.0 0.8 copy-done.12
  671.9 1.1 copy.75
  (63 shorter events, 0.5 us)
Async XLA Ops:
  0.6 2.9 copy-start.19
  0.7 3.0 copy-start.20
  0.7 3.2 copy-start.23
  0.7 5.6 copy-start.21
  0.7 5.6 copy-start.22
  144.1 31.4 %copy-start.10 = (f32[1,2048]{1,0:T(1,128)}, f32[1,2048]{1,0:T(1,128)S(1)}, u32[]{:S(2)}) copy-start(f32[1,2048]{1,0:T(1,128)S(1)} %get-tuple-element.140.gain_ref) | copy-start | bytes 24580
  144.7 30.8 %copy-start.1 = (bf16[320,2048]{1,0:T(8,128)(2,1)S(1)}, bf16[320,2048]{1,0:T(8,128)(2,1)}, u32[]{:S(2)}) copy-start(bf16[320,2048]{1,0:T(8,128)(2,1)} %get-tuple-element.62.wo_ref) | copy-start | bytes 3932164
  144.7 30.8 %copy-start.5 = (bf16[176,2048]{1,0:T(8,128)(2,1)S(1)}, bf16[176,2048]{1,0:T(8,128)(2,1)}, u32[]{:S(2)}) copy-start(bf16[176,2048]{1,0:T(8,128)(2,1)} %get-tuple-element.63.own_ref) | copy-start | bytes 2162692
  144.7 30.8 %copy-start.8 = (bf16[128,3072]{1,0:T(8,128)(2,1)S(1)}, bf16[128,3072]{1,0:T(8,128)(2,1)}, u32[]{:S(2)}) copy-start(bf16[128,3072]{1,0:T(8,128)(2,1)} %up_ref.1) | copy-start | bytes 2359300
  175.5 1.2 copy-start.2
  176.7 1.1 copy-start.9
  292.8 1.1 copy-start
  293.9 1.6 copy-start.3
  295.5 1.7 copy-start.4
  321.1 1.3 copy-start.6
  322.4 1.3 copy-start.7
  553.7 94.3 %copy-start.18 = (f32[8,2048]{1,0:T(8,128)S(1)}, f32[8,2048]{1,0:T(8,128)}, u32[]{:S(2)}) copy-start(f32[8,2048]{1,0:T(8,128)} %get-tuple-element.92) | copy-start | bytes 196612
  649.7 15.0 %copy-start.11 = (f32[2,176,2048]{2,1,0:T(8,128)S(1)}, f32[2,176,2048]{2,1,0:T(8,128)}, u32[]{:S(2)}) copy-start(f32[2,176,2048]{2,1,0:T(8,128)} %get-tuple-element.87) | copy-start | bytes 8650756
  649.7 11.0 %all-to-all-start = ((f32[32,1,896]{2,1,0:T(1,128)}), f32[32,1,896]{2,1,0:T(1,128)S(1)}, u32[]{:S(2)}, u32[]{:S(2)}) async-start(f32[32,1,896]{2,1,0:T(1,128)} %all_to_all.6), calls=%async_computation | async-start | bytes 229376 | tf_op jit(solution)/shard_map/all_to_all | solution.py:1982
  664.6 1.6 copy-start.17
  664.6 2.4 copy-start.16
  666.2 1.7 copy-start.15
  666.2 2.5 copy-start.13
  667.9 2.0 copy-start.14
  669.9 2.0 copy-start.12

commit v5 on v4

--- a/solution.py
+++ b/solution.py
@@ -299,22 +299,23 @@
                 dout_ref[rows, :] = value
 
         chunks(cot_ref.shape[1], scale, 1)
+    adjoint.begin()
     w_ig.onward(0)
-    w_s.onward(0)
     w_g.onward(0)
     w_o.onward(0)
+    w_s.onward(0)
+    w_gate.begin((0,))
+    w_o.begin((1,))
     w_g.begin((1,))
-    w_o.begin((1,))
-    w_gate.begin((0,))
+    w_ig.onward(1)
+    w_gate.begin((1,), (0,))
     w_s.onward(1)
     gather.forward()
-    w_ig.onward(1)
-    w_gate.begin((1,))
-    adjoint.begin()
+    w_o.onward(1)
+    w_g.onward(1)
+    w_gate.begin((1,), (1,))
     gather.forward_core()
     w_gate.onward(0)
-    w_g.onward(1)
-    w_o.onward(1)
     adjoint.forward()
     w_gate.onward(1, (0,))
     adjoint.forward_core()
@@ -596,11 +597,12 @@
         down_ref.shape[1],
     )
     gathers = [TokenGather(p, links, normed, all_ref, part) for part in parts]
-    w_u.begin((1,))
+    w_u.begin((1,), (0,))
     scatter.begin((1,))
     w_u.begin((0,))
     scatter.across_y(0)
     scatter.across_y(1)
+    w_u.begin((1,), (1,))
     scatter.begin((0,))
     w_d.begin((0,))
     w_u.onward(0)
@@ -619,15 +621,18 @@
     scatter.across_z(0)
     w_d.onward(0)
     scatter.across_z(1)
+    w_d.begin((1,), (0,))
     middle(0)
-    w_d.begin((1,))
+    w_u.onward(1, (0,))
     middle(1)
+    w_u.onward(1, (1,))
+    w_d.begin((1,), (1,))
     gathers[0].forward()
-    w_u.onward(1)
     gathers[1].forward()
+    w_d.onward(1, (0,))
     gathers[0].forward_core()
     gathers[1].forward_core()
-    w_d.onward(1)
+    w_d.onward(1, (1,))
     for gather in gathers:
         gather.end()
     w_u.end()
@@ -772,14 +777,14 @@
     down = GradScatter(p, links, dm_ref, hidden_ref, scratch[6:13])
     gate = GradScatter(p, links, n2_ref, dgm_ref, scratch[13:20])
     gathers = [TokenGather(p, links, do, all_ref, part) for part in parts]
+    down.begin(1)
     scatter.begin((1,))
-    down.begin(1)
     scatter.across_y(0)
     scatter.across_y(1)
+    down.across(0)
     scatter.begin((0,))
+    down.across(1)
     gate.begin(1)
-    down.across(0)
-    down.across(1)
     gain_out[...] = jnp.zeros_like(gain_out)
     for copy in staged:
         copy.wait()
@@ -854,14 +859,17 @@
     out = GradScatter(p, links, do_ref, mixed_ref, scratch[6:13])
     wide = GradScatter(p, links, n1_ref, dboth_ref, scratch[13:20])
     gates = Ready(p, links, gg_ref, None, scratch[20:26])
+    out.begin(1)
     scatter.begin((1,))
-    out.begin(1)
     scatter.across_y(0)
     scatter.across_y(1)
+    out.across(0)
+    out.across(1)
     wide.begin(1)
     scatter.begin((0,))
     gates.begin(1)
-    for g in (out, wide, gates):
+    out.begin(0)
+    for g in (wide, gates):
         g.across(0)
         g.across(1)
         g.begin(0)
@@ -1532,8 +1540,9 @@
             ("mid", mid_in, mid_ref),
         )
     }
+    scatter.begin()
     up.begin(1)
-    scatter.begin()
+    scatter.across_y()
     ch_out[...] = jnp.zeros_like(ch_out)
     gb_out[...] = jnp.zeros_like(gb_out)
     soft = ch_ref[0:1, :]
@@ -1564,7 +1573,6 @@
         chunks(rows, split)
 
     loop(8, upstream)
-    scatter.across_y()
     up.begin(0)
     row = lax.broadcasted_iota(jnp.int32, (8, LANES), 0)
     one = jnp.ones((1, LANES), F32)
@@ -1594,6 +1602,7 @@
         ends[seg : seg + 1, :] = carry[seg][1] * carry[seg][2]
     at = to_partner(ends, inc)
     links.arrived(inc, at)
+    scatter.across_z()
     up.across(0)
 
     def gradients(b):
@@ -1634,7 +1643,6 @@
         kept[name].wait()
     loop(8, gradients)
     at = to_partner(du.at[:, pl.ds(0, 8)], halo)
-    scatter.across_z()
     up.across(1)
 
     def write(i, at, src, dst, base):
@@ -1686,7 +1694,6 @@
         du[seg, pl.ds(2 * rows, 8), :] = jnp.where(zh == 0, halo[seg], 0.0)
 
     loop(4, tail)
-    loop(2, functools.partial(convolve, zl=1))
     scatter.arrive()
 
     def add(at):
@@ -1696,7 +1703,7 @@
     at = links.pair()
     links.start(final, block_out.at[p.mp], at, p.peer(mp=1))
     own = links.keep(final, block_out.at[p.mp])
-    loop(2, lambda i: convolve(i + 2, 1))
+    loop(4, functools.partial(convolve, zl=1))
     up.last(0)
     drain(1)
     up.last(1)

time: 680 us -> 640 us (0.941)
  Pallas kernels: 622 us -> 581 us
    pallas_call x6, Pallas kernels: 599 us -> 557 us  [run_kernel(): pl.pallas_call(body, name=name, out_shape=[jax.ShapeDtypeStruct(*o) for o...]
where the time goes in v5:
time: 640 us; the launch traced here: 632 us
  Pallas kernels  581 us (91%)
  local copies, waits for them, and re-layouts  33.4 us (5%)
  other arithmetic  7.4 us (1%)
    pallas_call x6, Pallas kernels, run_kernel(): pl.pallas_call(body, name=name, out_shape=[jax.ShapeDtypeStruct(*o) for o...  557 us
    unnamed x61, local copies, waits for them, and re-layouts  24.4 us
    pallas_call x1, Pallas kernels, feed_forward(): pl.pallas_call(mlp_kernel, name='feed_forward', grid=(blocks // 2,), in_s...  23.8 us
  transfers between devices with their start and end apart: 1, of which 1 were waited for; matrix products, arithmetic and copies ran while one was open for 0% of the time, Pallas kernels for 0%

profile of v5, /device:TPU:1, one launch (start us, length us, event | category | flops | bytes accessed | tf_op | source)
XLA Modules:
  0.0 632.2 jit_solution(4299206895125152735)
XLA Ops:
  0.7 1.2 copy.42
  1.9 0.2 copy.44
  2.1 1.2 copy.43
  3.3 0.2 copy.45
  3.6 0.1 reshape.137
  3.7 0.1 reshape.138
  3.8 0.6 copy.46.source_ref
  4.5 1.0 maximum_bitcast_fusion.ig_ref
  5.5 0.7 fusion.5
  6.3 0.6 pad.19.small_ref
  6.9 125.9 %fetch_first.1 = (bf16[8,176,2048]{2,1,0:T(8,128)(2,1)}, bf16[2048,640]{1,0:T(8,128)(2,1)}, bf16[320,2048]{1,0:T(8,128)(2,1)}, bf16[384,768]{1,0:T(8,128)(2,1)},...) custom-call(f32[8]{0:T(128)} %weight_ref.1, ...), custom_call_target="tpu_custom_call" | custom-call | tf_op jit(solution)/shard_map/fetch_first/pallas_call | solution.py:982
  132.8 0.7 slice.76
  133.5 0.7 compare_select_fusion
  134.2 1.4 fusion.10
  135.7 0.6 pad_maximum_fusion.3.ch_ref
  136.3 30.2 %recur_forward.1 = (bf16[8,176,2048]{2,1,0:T(8,128)(2,1)}, f32[4,360,384]{2,1,0:T(8,128)}, f32[8,176,384]{2,1,0:T(8,128)}, bf16[8,176,384]{2,1,0:T(8,128)(2,1)},...) custom-call(bf16[8,176,2048]{2,1,0:T(8,128)(2,1)} %get-tuple-element, ...), custom_call_target="tpu_custom_call" | custom-call | tf_op jit(solution)/shard_map/recur_forward/pallas_call | solution.py:982
  166.5 1.2 copy-done.2
  167.8 1.1 copy-done.9
  168.9 102.4 %reduce_and_fetch.1 = (f32[176,2048]{1,0:T(8,128)S(1)}, bf16[8,176,2048]{2,1,0:T(8,128)(2,1)}, bf16[2048,768]{1,0:T(8,128)(2,1)S(1)}, bf16[768,2048]{1,0:T(8,128)(2,1)S(1)}) custom-call(bf16[1408,384]{1,0:T(8,128)(2,1)S(1)} %bitcast.56, bf16[320,2048]{1,0:T(8,128)(2,1)S(1)} %copy-done.1, bf16[176,2048]{1,0:T(8,128)(2,1)S(1)} %copy-done.5, ...), custom_call_target="tpu_custom_call" | custom-call | tf_op jit(solution)/shard_map/reduce_and_fetch/pallas_call | solution.py:982
  271.3 1.1 copy-done
  272.4 1.6 copy-done.3
  274.0 1.7 copy-done.4
  275.8 23.8 %feed_forward.1 = (bf16[1408,768]{1,0:T(8,128)(2,1)S(1)}, bf16[1408,768]{1,0:T(8,128)(2,1)S(1)}, bf16[1408,768]{1,0:T(8,128)(2,1)}) custom-call(bf16[8,176,2048]{2,1,0:T(8,128)(2,1)} %get-tuple-element.69.n2_ref, bf16[8,176,2048]{2,1,0:T(8,128)(2,1)} %get-tuple-element.68.dm_ref, bf16[2048,768]{1,0:T(8,128)(2,1)} %get-tuple-element.55.wg_ref, ...), custom_call_target="tpu_custom_call" | custom-call | flops 13287555072 | bytes 11534336 | tf_op jit(solution)/shard_map/feed_forward/pallas_call | solution.py:958
  299.6 1.3 copy-done.6
  300.9 1.3 copy-done.7
  302.2 129.0 %reduce_and_return.1 = (f32[176,2048]{1,0:T(8,128)}, f32[8,2048]{1,0:T(8,128)}, bf16[8,176,2048]{2,1,0:T(8,128)(2,1)}, f32[128,3072]{1,0:T(8,128)}, f32[3072,128]{1,0:T(8,128)}, /*index=5*/bf16[8,176,2048]{2,1,0:T(8,128)(2,1)}) custom-call(bf16[2048,768]{1,0:T(8,128)(2,1)} %get-tuple-element.55.wg_ref, bf16[2048,768]{1,0:T(8,128)(2,1)} %copy-done.3, ...), custom_call_target="tpu_custom_call" | custom-call | tf_op jit(solution)/shard_map/reduce_and_return/pallas_call | solution.py:982
  431.2 78.5 %recur_backward.1 = (bf16[8,176,640]{2,1,0:T(8,128)(2,1)}, f32[384,768]{1,0:T(8,128)}, f32[8,8,384]{2,1,0:T(8,128)}, bf16[2,176,2048]{2,1,0:T(8,128)(2,1)}, f32[128,3072]{1,0:T(8,128)}) custom-call(bf16[8,176,2048]{2,1,0:T(8,128)(2,1)} %get-tuple-element.73.do_ref, bf16[320,2048]{1,0:T(8,128)(2,1)} %get-tuple-element.62.wo_ref, ...), custom_call_target="tpu_custom_call" | custom-call | tf_op jit(solution)/shard_map/recur_backward/pallas_call | solution.py:982
  509.8 0.9 reduce_sum.38
  510.7 0.7 fusion.8
  511.5 1.3 convert.25
  512.8 0.1 slice_bitcast_fusion.3
  513.0 0.3 reshape.146
  513.3 0.1 copy.47
  513.4 0.2 reshape.147
  513.6 0.8 reshape.148.gg_ref
  514.5 91.3 %return_last.1 = (f32[2,176,2048]{2,1,0:T(8,128)}, f32[8,2048]{1,0:T(8,128)}, f32[128,1280]{1,0:T(8,128)}, f32[128,1280]{1,0:T(8,128)}, f32[1280,128]{1,0:T(8,128)}, /*index=5*/bf16[4,64,128]{2,1,0:T(8,128)(2,1)}) custom-call(bf16[2048,640]{1,0:T(8,128)(2,1)} %get-tuple-element.57.wig_ref, bf16[176,2048]{1,0:T(8,128)(2,1)} %get-tuple-element.63.own_ref, ...), custom_call_target="tpu_custom_call" | custom-call | tf_op jit(solution)/shard_map/return_last/pallas_call | solution.py:982
  605.8 0.9 reduce_sum.36
  606.7 0.1 concatenate.32
  606.8 0.1 concatenate.33
  606.9 0.1 broadcast_in_dim.80
  607.1 0.1 broadcast_in_dim.76
  607.1 0.1 broadcast_in_dim.77
  607.2 0.1 broadcast_select_fusion.1
  607.4 0.1 broadcast_in_dim.74
  607.5 0.1 broadcast_select_fusion
  607.6 0.7 all_to_all.6
  608.3 3.8 all-to-all-start
  612.1 0.9 copy.58
  613.1 0.1 reshape.152
  613.3 0.7 squeeze.20
  613.9 0.7 squeeze.21
  614.6 5.1 all-to-all-done
  619.7 0.1 reduce_sum.39
  619.8 0.6 slice_bitcast_fusion.4
  620.3 0.7 reshape.151
  621.0 2.6 copy.68
  623.6 1.6 copy.69
  625.2 0.8 copy.70
  626.0 0.8 copy.71
  626.9 0.8 copy.72
  627.7 1.1 copy.73
  628.9 1.1 copy.74
  630.0 0.8 copy-done.12
  630.8 1.1 copy.75
  (63 shorter events, 0.5 us)
Async XLA Ops:
  0.6 2.9 copy-start.19
  0.7 3.0 copy-start.20
  0.7 3.2 copy-start.23
  0.7 5.6 copy-start.21
  0.7 5.6 copy-start.22
  135.7 30.8 %copy-start.10 = (f32[1,2048]{1,0:T(1,128)}, f32[1,2048]{1,0:T(1,128)S(1)}, u32[]{:S(2)}) copy-start(f32[1,2048]{1,0:T(1,128)S(1)} %get-tuple-element.140.gain_ref) | copy-start | bytes 24580
  136.3 30.2 %copy-start.1 = (bf16[320,2048]{1,0:T(8,128)(2,1)S(1)}, bf16[320,2048]{1,0:T(8,128)(2,1)}, u32[]{:S(2)}) copy-start(bf16[320,2048]{1,0:T(8,128)(2,1)} %get-tuple-element.62.wo_ref) | copy-start | bytes 3932164
  136.3 30.3 %copy-start.5 = (bf16[176,2048]{1,0:T(8,128)(2,1)S(1)}, bf16[176,2048]{1,0:T(8,128)(2,1)}, u32[]{:S(2)}) copy-start(bf16[176,2048]{1,0:T(8,128)(2,1)} %get-tuple-element.63.own_ref) | copy-start | bytes 2162692
  136.3 30.3 %copy-start.8 = (bf16[128,3072]{1,0:T(8,128)(2,1)S(1)}, bf16[128,3072]{1,0:T(8,128)(2,1)}, u32[]{:S(2)}) copy-start(bf16[128,3072]{1,0:T(8,128)(2,1)} %up_ref.1) | copy-start | bytes 2359300
  166.5 1.2 copy-start.2
  167.8 1.1 copy-start.9
  271.3 1.1 copy-start
  272.4 1.6 copy-start.3
  274.0 1.7 copy-start.4
  299.6 1.3 copy-start.6
  300.9 1.3 copy-start.7
  514.5 92.2 %copy-start.18 = (f32[8,2048]{1,0:T(8,128)S(1)}, f32[8,2048]{1,0:T(8,128)}, u32[]{:S(2)}) copy-start(f32[8,2048]{1,0:T(8,128)} %get-tuple-element.92) | copy-start | bytes 196612
  608.3 15.3 %copy-start.11 = (f32[2,176,2048]{2,1,0:T(8,128)S(1)}, f32[2,176,2048]{2,1,0:T(8,128)}, u32[]{:S(2)}) copy-start(f32[2,176,2048]{2,1,0:T(8,128)} %get-tuple-element.87) | copy-start | bytes 8650756
  608.3 11.3 %all-to-all-start = ((f32[32,1,896]{2,1,0:T(1,128)}), f32[32,1,896]{2,1,0:T(1,128)S(1)}, u32[]{:S(2)}, u32[]{:S(2)}) async-start(f32[32,1,896]{2,1,0:T(1,128)} %all_to_all.6), calls=%async_computation | async-start | bytes 229376 | tf_op jit(solution)/shard_map/all_to_all | solution.py:1989
  623.6 1.6 copy-start.17
  623.6 2.4 copy-start.16
  625.2 1.7 copy-start.15
  625.2 2.5 copy-start.13
  626.9 2.0 copy-start.14
  628.9 2.0 copy-start.12

commit v6 on v5

--- a/solution.py
+++ b/solution.py
@@ -811,6 +811,10 @@
     middle(1)
     gathers[0].forward()
     gathers[1].forward()
+    down.last(0)
+    down.last(1)
+    gathers[0].forward_core()
+    gate.last(0)
     out = scratch[0]
     writes = []
     for b in range(8):
@@ -819,10 +823,6 @@
         at = pl.ds(b * rows_of, rows_of)
         out[b % 4] = dot(hidden_ref[at, :], wd_ref[...], NN, BF)
         writes.append(links.keep(out.at[b % 4], part_out.at[b]))
-    down.last(0)
-    down.last(1)
-    gathers[0].forward_core()
-    gate.last(0)
     gathers[1].forward_core()
     gate.last(1)
     for gather in gathers:
@@ -830,10 +830,10 @@
     down.end()
     ff = down.result.shape[2]
     for j in range(4):
-        down_out[j * ff : (j + 1) * ff, :] = down.result[j].astype(F32).T
+        down_out[j * ff : (j + 1) * ff, :] = down.result[j].astype(F32).T.astype(BF)
     gate.end()
     for j in range(4):
-        gate_out[:, j * ff : (j + 1) * ff] = gate.result[j].astype(F32)
+        gate_out[:, j * ff : (j + 1) * ff] = gate.result[j]
     for write in writes[4:]:
         write.wait()
     links.finish()
@@ -905,7 +905,7 @@
     out.end()
     for j in range(4):
         out_out[j * out_out.shape[0] // 4 : (j + 1) * out_out.shape[0] // 4, :] = (
-            out.result[j].astype(F32).T[: out_out.shape[0] // 4]
+            out.result[j].astype(F32).T[: out_out.shape[0] // 4].astype(BF)
         )
     gates.end()
     gates_out[...] = gates.result[...]
@@ -915,8 +915,8 @@
     for j in (0, 2):
         a, b = (wide.result[j + i].astype(F32) for i in (0, 1))
         span = slice(j * two // 2, (j + 2) * two // 2)
-        in_out[:, span] = jnp.where(left, a, pltpu.roll(b, two // 2, 1))
-        gelu_out[:, span] = jnp.where(left, pltpu.roll(a, two // 2, 1), b)
+        in_out[:, span] = jnp.where(left, a, pltpu.roll(b, two // 2, 1)).astype(BF)
+        gelu_out[:, span] = jnp.where(left, pltpu.roll(a, two // 2, 1), b).astype(BF)
     for span, at in sent:
         links.arrived(dx_recv.at[span], at)
     dx_ref[1 - p.mp] = dx_recv[...].astype(F32)
@@ -939,7 +939,7 @@
         dgm_ref[at, :] = (d * up * slope).astype(BF)
         dup_ref[at, :] = (d * value).astype(BF)
 
-    chunks(count * rows, body)
+    chunks(count * rows, body, 22)
 
 
 def feed_forward(n2, dm, w_g, w_u, w_d):
@@ -1073,8 +1073,8 @@
             ((rows, width), F32),
             ((8, width), F32),
             ((8, rows, width), BF),
-            ((drows, 4 * ff), F32),
-            ((4 * ff, drows), F32),
+            ((drows, 4 * ff), BF),
+            ((4 * ff, drows), BF),
             ((8, rows, width), BF),
         ],
         [VMEM, VMEM, ANY] + [VMEM] * 2 + [ANY],
@@ -1101,9 +1101,9 @@
         [
             ((2, rows, width), F32),
             ((8, width), F32),
-            ((drows, 4 * local), F32),
-            ((drows, 4 * local), F32),
-            ((4 * local, drows), F32),
+            ((drows, 4 * local), BF),
+            ((drows, 4 * local), BF),
+            ((4 * local, drows), BF),
             ((4, unit, 128), BF),
         ],
         [VMEM] * 6,
@@ -1710,7 +1710,7 @@
     up.end()
     ff = up.result.shape[2]
     for j in range(4):
-        up_out[:, j * ff : (j + 1) * ff] = up.result[j].astype(F32)
+        up_out[:, j * ff : (j + 1) * ff] = up.result[j]
     own.wait()
     links.arrived(block_out.at[1 - p.mp], at)
     links.finish()
@@ -1773,7 +1773,7 @@
             ((LANES, 2 * LANES), F32),
             ((8, 8, LANES), F32),
             ((2, rows, width), BF),
-            ((drows, 4 * ff), F32),
+            ((drows, 4 * ff), BF),
         ],
         [ANY] + [VMEM] * 2 + [ANY, VMEM],
         [ANY] + [VMEM] * 3 + [ANY, VMEM] + [ANY] * 4 + [VMEM] + [ANY] * 3 + [VMEM],
@@ -1992,16 +1992,16 @@
     return (
         block_out[:, None],
         grad_tokens[:, None],
-        g_input,
-        g_gelu,
+        g_input.astype(F32),
+        g_gelu.astype(F32),
         g_gates[0],
         g_gates[1],
         g_channels,
         g_gains,
-        g_output,
-        g_gate,
-        g_up,
-        g_down,
+        g_output.astype(F32),
+        g_gate.astype(F32),
+        g_up.astype(F32),
+        g_down.astype(F32),
     )
 
 

time: 640 us -> 634 us (level)
  local copies, waits for them, and re-layouts: 33.4 us -> 26.7 us
  other arithmetic: 7.4 us -> 13.9 us
    pallas_call x6, Pallas kernels: 557 us -> 550 us  [run_kernel(): pl.pallas_call(body, name=name, out_shape=[jax.ShapeDtypeStruct(*o) for o...]
    unnamed x61 -> x55, local copies, waits for them, and re-layouts: 24.4 us -> 17.7 us
    pallas_call x1, Pallas kernels: 23.8 us -> 30.4 us  [feed_forward(): pl.pallas_call(mlp_kernel, name='feed_forward', grid=(blocks // 2,), in_s...]
    convert_element_type x0 -> x6, other arithmetic: none -> 6.48 us  [the longest x1 1.3 us: on_device(): g_up.astype(F32)]
  transfers between devices with their start and end apart: 1 -> 1, of which waited for: 1 -> 0; matrix products, arithmetic and copies ran while one was open for 0% -> 1% of each run, Pallas kernels for 0% -> 0%
where the time goes in v6:
time: 634 us; the launch traced here: 625 us
  Pallas kernels  581 us (92%)
  local copies, waits for them, and re-layouts  26.7 us (4%)
  other arithmetic  13.9 us (2%)
    pallas_call x6, Pallas kernels, run_kernel(): pl.pallas_call(body, name=name, out_shape=[jax.ShapeDtypeStruct(*o) for o...  550 us
    pallas_call x1, Pallas kernels, feed_forward(): pl.pallas_call(mlp_kernel, name='feed_forward', grid=(blocks // 2,), in_s...  30.4 us
    unnamed x55, local copies, waits for them, and re-layouts  17.7 us
  transfers between devices with their start and end apart: 1, of which 0 were waited for; matrix products, arithmetic and copies ran while one was open for 1% of the time, Pallas kernels for 0%

profile of v6, /device:TPU:1, one launch (start us, length us, event | category | flops | bytes accessed | tf_op | source)
XLA Modules:
  0.0 624.9 jit_solution(3757329027040542926)
XLA Ops:
  0.7 1.2 copy.42
  1.9 0.2 copy.44
  2.1 1.2 copy.43
  3.3 0.2 copy.45
  3.6 0.1 reshape.137
  3.7 0.1 reshape.138
  3.8 0.6 copy.46.source_ref
  4.5 1.0 maximum_bitcast_fusion.ig_ref
  5.5 0.7 fusion.5
  6.3 0.6 pad.19.small_ref
  6.9 125.9 %fetch_first.1 = (bf16[8,176,2048]{2,1,0:T(8,128)(2,1)}, bf16[2048,640]{1,0:T(8,128)(2,1)}, bf16[320,2048]{1,0:T(8,128)(2,1)}, bf16[384,768]{1,0:T(8,128)(2,1)},...) custom-call(f32[8]{0:T(128)} %weight_ref.1, ...), custom_call_target="tpu_custom_call" | custom-call | tf_op jit(solution)/shard_map/fetch_first/pallas_call | solution.py:982
  132.8 0.7 slice.76
  133.5 0.7 compare_select_fusion
  134.2 1.4 fusion.10
  135.7 0.6 pad_maximum_fusion.3.ch_ref
  136.3 30.3 %recur_forward.1 = (bf16[8,176,2048]{2,1,0:T(8,128)(2,1)}, f32[4,360,384]{2,1,0:T(8,128)}, f32[8,176,384]{2,1,0:T(8,128)}, bf16[8,176,384]{2,1,0:T(8,128)(2,1)},...) custom-call(bf16[8,176,2048]{2,1,0:T(8,128)(2,1)} %get-tuple-element, ...), custom_call_target="tpu_custom_call" | custom-call | tf_op jit(solution)/shard_map/recur_forward/pallas_call | solution.py:982
  166.6 1.2 copy-done.2
  167.8 1.1 copy-done.9
  169.0 102.4 %reduce_and_fetch.1 = (f32[176,2048]{1,0:T(8,128)S(1)}, bf16[8,176,2048]{2,1,0:T(8,128)(2,1)}, bf16[2048,768]{1,0:T(8,128)(2,1)S(1)}, bf16[768,2048]{1,0:T(8,128)(2,1)S(1)}) custom-call(bf16[1408,384]{1,0:T(8,128)(2,1)S(1)} %bitcast.56, bf16[320,2048]{1,0:T(8,128)(2,1)S(1)} %copy-done.1, bf16[176,2048]{1,0:T(8,128)(2,1)S(1)} %copy-done.5, ...), custom_call_target="tpu_custom_call" | custom-call | tf_op jit(solution)/shard_map/reduce_and_fetch/pallas_call | solution.py:982
  271.4 1.1 copy-done
  272.5 1.6 copy-done.3
  274.1 1.7 copy-done.4
  275.8 30.4 %feed_forward.1 = (bf16[1408,768]{1,0:T(8,128)(2,1)S(1)}, bf16[1408,768]{1,0:T(8,128)(2,1)S(1)}, bf16[1408,768]{1,0:T(8,128)(2,1)}) custom-call(bf16[8,176,2048]{2,1,0:T(8,128)(2,1)} %get-tuple-element.69.n2_ref, bf16[8,176,2048]{2,1,0:T(8,128)(2,1)} %get-tuple-element.68.dm_ref, bf16[2048,768]{1,0:T(8,128)(2,1)} %get-tuple-element.55.wg_ref, ...), custom_call_target="tpu_custom_call" | custom-call | flops 13287555072 | bytes 11534336 | tf_op jit(solution)/shard_map/feed_forward/pallas_call | solution.py:958
  306.3 1.3 copy-done.6
  307.6 1.3 copy-done.7
  308.9 119.9 %reduce_and_return.1 = (f32[176,2048]{1,0:T(8,128)}, f32[8,2048]{1,0:T(8,128)}, bf16[8,176,2048]{2,1,0:T(8,128)(2,1)}, bf16[128,3072]{1,0:T(8,128)(2,1)}, bf16[3...) custom-call(bf16[2048,768]{1,0:T(8,128)(2,1)} %get-tuple-element.55.wg_ref, bf16[2048,768]{1,0:T(8,128)(2,1)} %copy-done.3, ...), custom_call_target="tpu_custom_call" | custom-call | tf_op jit(solution)/shard_map/reduce_and_return/pallas_call | solution.py:982
  428.8 78.4 %recur_backward.1 = (bf16[8,176,640]{2,1,0:T(8,128)(2,1)}, f32[384,768]{1,0:T(8,128)}, f32[8,8,384]{2,1,0:T(8,128)}, bf16[2,176,2048]{2,1,0:T(8,128)(2,1)}, bf16[128,3072]{1,0:T(8,128)(2,1)}) custom-call(bf16[8,176,2048]{2,1,0:T(8,128)(2,1)} %get-tuple-element.73.do_ref, bf16[320,2048]{1,0:T(8,128)(2,1)} %get-tuple-element.62.wo_ref, ...), custom_call_target="tpu_custom_call" | custom-call | tf_op jit(solution)/shard_map/recur_backward/pallas_call | solution.py:982
  507.2 0.9 reduce_sum.38
  508.1 0.7 fusion.8
  508.9 1.3 convert.25
  510.2 0.1 slice_bitcast_fusion.3
  510.3 0.1 maximum_bitcast_fusion.1
  510.4 0.1 pad_maximum_fusion
  510.5 0.3 reshape.146
  510.8 0.1 copy.47
  510.8 0.2 reshape.147
  511.1 0.8 reshape.148.gg_ref
  511.9 93.2 %return_last.1 = (f32[2,176,2048]{2,1,0:T(8,128)}, f32[8,2048]{1,0:T(8,128)}, bf16[128,1280]{1,0:T(8,128)(2,1)}, bf16[128,1280]{1,0:T(8,128)(2,1)}, bf16[1280,12...) custom-call(bf16[2048,640]{1,0:T(8,128)(2,1)} %get-tuple-element.57.wig_ref, bf16[176,2048]{1,0:T(8,128)(2,1)} %get-tuple-element.63.own_ref, ...), custom_call_target="tpu_custom_call" | custom-call | tf_op jit(solution)/shard_map/return_last/pallas_call | solution.py:982
  605.1 0.9 reduce_sum.36
  606.2 0.1 concatenate.32
  606.3 0.1 concatenate.33
  606.4 0.1 broadcast_in_dim.80
  606.5 0.1 broadcast_in_dim.76
  606.6 0.1 broadcast_in_dim.77
  606.7 0.1 broadcast_select_fusion.1
  606.9 0.1 broadcast_in_dim.74
  607.0 0.1 broadcast_select_fusion
  607.1 0.7 all_to_all.6
  607.8 2.4 all-to-all-start
  610.3 0.9 copy.58
  611.2 0.1 reshape.152
  611.4 0.9 convert_element_type.28
  612.3 0.9 convert_element_type.29
  613.1 0.9 convert_element_type.30
  614.0 0.7 squeeze.20
  614.7 0.7 squeeze.21
  615.3 1.3 convert_element_type.32
  616.6 1.3 convert_element_type.31
  617.9 1.2 convert_element_type.33
  619.2 0.1 reduce_sum.39
  619.3 0.6 slice_bitcast_fusion.4
  619.9 0.7 reshape.151
  620.5 2.6 copy.62
  623.2 1.6 copy.63
  (63 shorter events, 0.4 us)
Async XLA Ops:
  0.6 2.9 copy-start.19
  0.7 3.0 copy-start.20
  0.7 3.2 copy-start.23
  0.7 5.6 copy-start.21
  0.7 5.6 copy-start.22
  135.7 30.9 %copy-start.10 = (f32[1,2048]{1,0:T(1,128)}, f32[1,2048]{1,0:T(1,128)S(1)}, u32[]{:S(2)}) copy-start(f32[1,2048]{1,0:T(1,128)S(1)} %get-tuple-element.140.gain_ref) | copy-start | bytes 24580
  136.3 30.3 %copy-start.1 = (bf16[320,2048]{1,0:T(8,128)(2,1)S(1)}, bf16[320,2048]{1,0:T(8,128)(2,1)}, u32[]{:S(2)}) copy-start(bf16[320,2048]{1,0:T(8,128)(2,1)} %get-tuple-element.62.wo_ref) | copy-start | bytes 3932164
  136.3 30.3 %copy-start.5 = (bf16[176,2048]{1,0:T(8,128)(2,1)S(1)}, bf16[176,2048]{1,0:T(8,128)(2,1)}, u32[]{:S(2)}) copy-start(bf16[176,2048]{1,0:T(8,128)(2,1)} %get-tuple-element.63.own_ref) | copy-start | bytes 2162692
  136.3 30.3 %copy-start.8 = (bf16[128,3072]{1,0:T(8,128)(2,1)S(1)}, bf16[128,3072]{1,0:T(8,128)(2,1)}, u32[]{:S(2)}) copy-start(bf16[128,3072]{1,0:T(8,128)(2,1)} %up_ref.1) | copy-start | bytes 2359300
  166.6 1.2 copy-start.2
  167.8 1.1 copy-start.9
  271.4 1.1 copy-start
  272.5 1.6 copy-start.3
  274.1 1.7 copy-start.4
  306.3 1.3 copy-start.6
  307.6 1.3 copy-start.7
  511.9 94.2 %copy-start.18 = (f32[8,2048]{1,0:T(8,128)S(1)}, f32[8,2048]{1,0:T(8,128)}, u32[]{:S(2)}) copy-start(f32[8,2048]{1,0:T(8,128)} %get-tuple-element.92) | copy-start | bytes 196612
  605.1 6.2 copy-start.17
  605.1 7.1 %copy-start.16 = (bf16[128,1280]{1,0:T(8,128)(2,1)S(1)}, bf16[128,1280]{1,0:T(8,128)(2,1)}, u32[]{:S(2)}) copy-start(bf16[128,1280]{1,0:T(8,128)(2,1)} %get-tuple-element.89) | copy-start | bytes 983044
  606.4 6.8 %copy-start.15 = (bf16[1280,128]{1,0:T(8,128)(2,1)S(1)}, bf16[1280,128]{1,0:T(8,128)(2,1)}, u32[]{:S(2)}) copy-start(bf16[1280,128]{1,0:T(8,128)(2,1)} %get-tuple-element.94) | copy-start | bytes 983044
  607.8 7.5 %copy-start.14 = (bf16[128,3072]{1,0:T(8,128)(2,1)S(1)}, bf16[128,3072]{1,0:T(8,128)(2,1)}, u32[]{:S(2)}) copy-start(bf16[128,3072]{1,0:T(8,128)(2,1)} %get-tuple-element.96) | copy-start | bytes 2359300
  607.8 11.4 %all-to-all-start = ((f32[32,1,896]{2,1,0:T(1,128)}), f32[32,1,896]{2,1,0:T(1,128)S(1)}, u32[]{:S(2)}, u32[]{:S(2)}) async-start(f32[32,1,896]{2,1,0:T(1,128)} %all_to_all.6), calls=%async_computation | async-start | bytes 229376 | tf_op jit(solution)/shard_map/all_to_all | solution.py:1989
  612.3 4.4 copy-start.13
  615.3 2.6 copy-start.12
  617.9 5.2 copy-start.11

commit v7 on v6

--- a/solution.py
+++ b/solution.py
@@ -939,7 +939,7 @@
         dgm_ref[at, :] = (d * up * slope).astype(BF)
         dup_ref[at, :] = (d * value).astype(BF)
 
-    chunks(count * rows, body, 22)
+    chunks(count * rows, body)
 
 
 def feed_forward(n2, dm, w_g, w_u, w_d):

time: 634 us -> 638 us (level)
  no operation moved by 1% of the time
where the time goes in v7:
time: 638 us; the launch traced here: 629 us
  Pallas kernels  584 us (92%)
  local copies, waits for them, and re-layouts  26.7 us (4%)
  other arithmetic  13.9 us (2%)
    pallas_call x6, Pallas kernels, run_kernel(): pl.pallas_call(body, name=name, out_shape=[jax.ShapeDtypeStruct(*o) for o...  550 us
    pallas_call x1, Pallas kernels, feed_forward(): pl.pallas_call(mlp_kernel, name='feed_forward', grid=(blocks // 2,), in_s...  34 us
    unnamed x55, local copies, waits for them, and re-layouts  17.7 us
  transfers between devices with their start and end apart: 1, of which 0 were waited for; matrix products, arithmetic and copies ran while one was open for 1% of the time, Pallas kernels for 0%

profile of v7, /device:TPU:1, one launch (start us, length us, event | category | flops | bytes accessed | tf_op | source)
XLA Modules:
  0.0 628.8 jit_solution(1466665982989730096)
XLA Ops:
  0.7 1.2 copy.42
  1.9 0.2 copy.44
  2.1 1.2 copy.43
  3.3 0.2 copy.45
  3.6 0.1 reshape.137
  3.7 0.1 reshape.138
  3.8 0.6 copy.46.source_ref
  4.5 1.0 maximum_bitcast_fusion.ig_ref
  5.5 0.7 fusion.5
  6.3 0.6 pad.19.small_ref
  6.9 125.9 %fetch_first.1 = (bf16[8,176,2048]{2,1,0:T(8,128)(2,1)}, bf16[2048,640]{1,0:T(8,128)(2,1)}, bf16[320,2048]{1,0:T(8,128)(2,1)}, bf16[384,768]{1,0:T(8,128)(2,1)},...) custom-call(f32[8]{0:T(128)} %weight_ref.1, ...), custom_call_target="tpu_custom_call" | custom-call | tf_op jit(solution)/shard_map/fetch_first/pallas_call | solution.py:982
  132.8 0.7 slice.76
  133.5 0.7 compare_select_fusion
  134.2 1.4 fusion.10
  135.7 0.6 pad_maximum_fusion.3.ch_ref
  136.3 30.3 %recur_forward.1 = (bf16[8,176,2048]{2,1,0:T(8,128)(2,1)}, f32[4,360,384]{2,1,0:T(8,128)}, f32[8,176,384]{2,1,0:T(8,128)}, bf16[8,176,384]{2,1,0:T(8,128)(2,1)},...) custom-call(bf16[8,176,2048]{2,1,0:T(8,128)(2,1)} %get-tuple-element, ...), custom_call_target="tpu_custom_call" | custom-call | tf_op jit(solution)/shard_map/recur_forward/pallas_call | solution.py:982
  166.6 1.2 copy-done.2
  167.8 1.1 copy-done.9
  169.0 102.4 %reduce_and_fetch.1 = (f32[176,2048]{1,0:T(8,128)S(1)}, bf16[8,176,2048]{2,1,0:T(8,128)(2,1)}, bf16[2048,768]{1,0:T(8,128)(2,1)S(1)}, bf16[768,2048]{1,0:T(8,128)(2,1)S(1)}) custom-call(bf16[1408,384]{1,0:T(8,128)(2,1)S(1)} %bitcast.56, bf16[320,2048]{1,0:T(8,128)(2,1)S(1)} %copy-done.1, bf16[176,2048]{1,0:T(8,128)(2,1)S(1)} %copy-done.5, ...), custom_call_target="tpu_custom_call" | custom-call | tf_op jit(solution)/shard_map/reduce_and_fetch/pallas_call | solution.py:982
  271.4 1.1 copy-done
  272.5 1.6 copy-done.3
  274.1 1.7 copy-done.4
  275.8 34.0 %feed_forward.1 = (bf16[1408,768]{1,0:T(8,128)(2,1)S(1)}, bf16[1408,768]{1,0:T(8,128)(2,1)S(1)}, bf16[1408,768]{1,0:T(8,128)(2,1)}) custom-call(bf16[8,176,2048]{2,1,0:T(8,128)(2,1)} %get-tuple-element.69.n2_ref, bf16[8,176,2048]{2,1,0:T(8,128)(2,1)} %get-tuple-element.68.dm_ref, bf16[2048,768]{1,0:T(8,128)(2,1)} %get-tuple-element.55.wg_ref, ...), custom_call_target="tpu_custom_call" | custom-call | flops 13287555072 | bytes 11534336 | tf_op jit(solution)/shard_map/feed_forward/pallas_call | solution.py:958
  309.9 1.3 copy-done.6
  311.2 1.3 copy-done.7
  312.5 119.8 %reduce_and_return.1 = (f32[176,2048]{1,0:T(8,128)}, f32[8,2048]{1,0:T(8,128)}, bf16[8,176,2048]{2,1,0:T(8,128)(2,1)}, bf16[128,3072]{1,0:T(8,128)(2,1)}, bf16[3...) custom-call(bf16[2048,768]{1,0:T(8,128)(2,1)} %get-tuple-element.55.wg_ref, bf16[2048,768]{1,0:T(8,128)(2,1)} %copy-done.3, ...), custom_call_target="tpu_custom_call" | custom-call | tf_op jit(solution)/shard_map/reduce_and_return/pallas_call | solution.py:982
  432.4 78.4 %recur_backward.1 = (bf16[8,176,640]{2,1,0:T(8,128)(2,1)}, f32[384,768]{1,0:T(8,128)}, f32[8,8,384]{2,1,0:T(8,128)}, bf16[2,176,2048]{2,1,0:T(8,128)(2,1)}, bf16[128,3072]{1,0:T(8,128)(2,1)}) custom-call(bf16[8,176,2048]{2,1,0:T(8,128)(2,1)} %get-tuple-element.73.do_ref, bf16[320,2048]{1,0:T(8,128)(2,1)} %get-tuple-element.62.wo_ref, ...), custom_call_target="tpu_custom_call" | custom-call | tf_op jit(solution)/shard_map/recur_backward/pallas_call | solution.py:982
  510.8 0.9 reduce_sum.38
  511.7 0.7 fusion.8
  512.4 1.3 convert.25
  513.8 0.1 slice_bitcast_fusion.3
  513.9 0.1 maximum_bitcast_fusion.1
  514.0 0.1 pad_maximum_fusion
  514.0 0.3 reshape.146
  514.3 0.1 copy.47
  514.4 0.2 reshape.147
  514.6 0.8 reshape.148.gg_ref
  515.5 93.5 %return_last.1 = (f32[2,176,2048]{2,1,0:T(8,128)}, f32[8,2048]{1,0:T(8,128)}, bf16[128,1280]{1,0:T(8,128)(2,1)}, bf16[128,1280]{1,0:T(8,128)(2,1)}, bf16[1280,12...) custom-call(bf16[2048,640]{1,0:T(8,128)(2,1)} %get-tuple-element.57.wig_ref, bf16[176,2048]{1,0:T(8,128)(2,1)} %get-tuple-element.63.own_ref, ...), custom_call_target="tpu_custom_call" | custom-call | tf_op jit(solution)/shard_map/return_last/pallas_call | solution.py:982
  609.0 0.9 reduce_sum.36
  610.1 0.1 concatenate.32
  610.2 0.1 concatenate.33
  610.3 0.1 broadcast_in_dim.80
  610.4 0.1 broadcast_in_dim.76
  610.5 0.1 broadcast_in_dim.77
  610.6 0.1 broadcast_select_fusion.1
  610.8 0.1 broadcast_in_dim.74
  610.9 0.1 broadcast_select_fusion
  611.0 0.7 all_to_all.6
  611.7 2.4 all-to-all-start
  614.1 0.9 copy.58
  615.1 0.1 reshape.152
  615.3 0.9 convert_element_type.28
  616.1 0.9 convert_element_type.29
  617.0 0.9 convert_element_type.30
  617.9 0.7 squeeze.20
  618.6 0.7 squeeze.21
  619.2 1.3 convert_element_type.32
  620.5 1.3 convert_element_type.31
  621.8 1.2 convert_element_type.33
  623.1 0.1 reduce_sum.39
  623.2 0.6 slice_bitcast_fusion.4
  623.7 0.7 reshape.151
  624.4 2.6 copy.62
  627.0 1.6 copy.63
  (63 shorter events, 0.4 us)
Async XLA Ops:
  0.6 2.9 copy-start.19
  0.7 3.0 copy-start.20
  0.7 3.2 copy-start.23
  0.7 5.6 copy-start.21
  0.7 5.6 copy-start.22
  135.7 30.9 %copy-start.10 = (f32[1,2048]{1,0:T(1,128)}, f32[1,2048]{1,0:T(1,128)S(1)}, u32[]{:S(2)}) copy-start(f32[1,2048]{1,0:T(1,128)S(1)} %get-tuple-element.140.gain_ref) | copy-start | bytes 24580
  136.3 30.3 %copy-start.1 = (bf16[320,2048]{1,0:T(8,128)(2,1)S(1)}, bf16[320,2048]{1,0:T(8,128)(2,1)}, u32[]{:S(2)}) copy-start(bf16[320,2048]{1,0:T(8,128)(2,1)} %get-tuple-element.62.wo_ref) | copy-start | bytes 3932164
  136.3 30.3 %copy-start.5 = (bf16[176,2048]{1,0:T(8,128)(2,1)S(1)}, bf16[176,2048]{1,0:T(8,128)(2,1)}, u32[]{:S(2)}) copy-start(bf16[176,2048]{1,0:T(8,128)(2,1)} %get-tuple-element.63.own_ref) | copy-start | bytes 2162692
  136.3 30.3 %copy-start.8 = (bf16[128,3072]{1,0:T(8,128)(2,1)S(1)}, bf16[128,3072]{1,0:T(8,128)(2,1)}, u32[]{:S(2)}) copy-start(bf16[128,3072]{1,0:T(8,128)(2,1)} %up_ref.1) | copy-start | bytes 2359300
  166.6 1.2 copy-start.2
  167.8 1.1 copy-start.9
  271.4 1.1 copy-start
  272.5 1.6 copy-start.3
  274.1 1.7 copy-start.4
  309.9 1.3 copy-start.6
  311.2 1.3 copy-start.7
  515.5 94.5 %copy-start.18 = (f32[8,2048]{1,0:T(8,128)S(1)}, f32[8,2048]{1,0:T(8,128)}, u32[]{:S(2)}) copy-start(f32[8,2048]{1,0:T(8,128)} %get-tuple-element.92) | copy-start | bytes 196612
  609.0 6.2 copy-start.17
  609.0 7.1 %copy-start.16 = (bf16[128,1280]{1,0:T(8,128)(2,1)S(1)}, bf16[128,1280]{1,0:T(8,128)(2,1)}, u32[]{:S(2)}) copy-start(bf16[128,1280]{1,0:T(8,128)(2,1)} %get-tuple-element.89) | copy-start | bytes 983044
  610.3 6.8 %copy-start.15 = (bf16[1280,128]{1,0:T(8,128)(2,1)S(1)}, bf16[1280,128]{1,0:T(8,128)(2,1)}, u32[]{:S(2)}) copy-start(bf16[1280,128]{1,0:T(8,128)(2,1)} %get-tuple-element.94) | copy-start | bytes 983044
  611.7 7.5 %copy-start.14 = (bf16[128,3072]{1,0:T(8,128)(2,1)S(1)}, bf16[128,3072]{1,0:T(8,128)(2,1)}, u32[]{:S(2)}) copy-start(bf16[128,3072]{1,0:T(8,128)(2,1)} %get-tuple-element.96) | copy-start | bytes 2359300
  611.7 11.4 %all-to-all-start = ((f32[32,1,896]{2,1,0:T(1,128)}), f32[32,1,896]{2,1,0:T(1,128)S(1)}, u32[]{:S(2)}, u32[]{:S(2)}) async-start(f32[32,1,896]{2,1,0:T(1,128)} %all_to_all.6), calls=%async_computation | async-start | bytes 229376 | tf_op jit(solution)/shard_map/all_to_all | solution.py:1989
  616.1 4.4 copy-start.13
  619.2 2.6 copy-start.12
  621.8 5.2 copy-start.11

commit v8 on v5

--- a/solution.py
+++ b/solution.py
@@ -811,6 +811,10 @@
     middle(1)
     gathers[0].forward()
     gathers[1].forward()
+    down.last(0)
+    down.last(1)
+    gathers[0].forward_core()
+    gate.last(0)
     out = scratch[0]
     writes = []
     for b in range(8):
@@ -819,10 +823,6 @@
         at = pl.ds(b * rows_of, rows_of)
         out[b % 4] = dot(hidden_ref[at, :], wd_ref[...], NN, BF)
         writes.append(links.keep(out.at[b % 4], part_out.at[b]))
-    down.last(0)
-    down.last(1)
-    gathers[0].forward_core()
-    gate.last(0)
     gathers[1].forward_core()
     gate.last(1)
     for gather in gathers:

time: 640 us -> 644 us (level)
    pallas_call x1, Pallas kernels: 23.8 us -> 34 us  [feed_forward(): pl.pallas_call(mlp_kernel, name='feed_forward', grid=(blocks // 2,), in_s...]
where the time goes in v8:
time: 644 us; the launch traced here: 634 us
  Pallas kernels  585 us (91%)
  local copies, waits for them, and re-layouts  33.4 us (5%)
  other arithmetic  7.4 us (1%)
    pallas_call x6, Pallas kernels, run_kernel(): pl.pallas_call(body, name=name, out_shape=[jax.ShapeDtypeStruct(*o) for o...  551 us
    pallas_call x1, Pallas kernels, feed_forward(): pl.pallas_call(mlp_kernel, name='feed_forward', grid=(blocks // 2,), in_s...  34 us
    unnamed x61, local copies, waits for them, and re-layouts  24.4 us
  transfers between devices with their start and end apart: 1, of which 1 were waited for; matrix products, arithmetic and copies ran while one was open for 0% of the time, Pallas kernels for 0%

profile of v8, /device:TPU:1, one launch (start us, length us, event | category | flops | bytes accessed | tf_op | source)
XLA Modules:
  0.0 634.1 jit_solution(14297107435540834398)
XLA Ops:
  0.7 1.2 copy.42
  1.9 0.2 copy.44
  2.1 1.2 copy.43
  3.3 0.2 copy.45
  3.6 0.1 reshape.137
  3.7 0.1 reshape.138
  3.8 0.6 copy.46.source_ref
  4.5 1.0 maximum_bitcast_fusion.ig_ref
  5.5 0.7 fusion.5
  6.3 0.6 pad.19.small_ref
  6.9 125.9 %fetch_first.1 = (bf16[8,176,2048]{2,1,0:T(8,128)(2,1)}, bf16[2048,640]{1,0:T(8,128)(2,1)}, bf16[320,2048]{1,0:T(8,128)(2,1)}, bf16[384,768]{1,0:T(8,128)(2,1)},...) custom-call(f32[8]{0:T(128)} %weight_ref.1, ...), custom_call_target="tpu_custom_call" | custom-call | tf_op jit(solution)/shard_map/fetch_first/pallas_call | solution.py:982
  132.8 0.7 slice.76
  133.5 0.7 compare_select_fusion
  134.2 1.4 fusion.10
  135.7 0.6 pad_maximum_fusion.3.ch_ref
  136.3 30.2 %recur_forward.1 = (bf16[8,176,2048]{2,1,0:T(8,128)(2,1)}, f32[4,360,384]{2,1,0:T(8,128)}, f32[8,176,384]{2,1,0:T(8,128)}, bf16[8,176,384]{2,1,0:T(8,128)(2,1)},...) custom-call(bf16[8,176,2048]{2,1,0:T(8,128)(2,1)} %get-tuple-element, ...), custom_call_target="tpu_custom_call" | custom-call | tf_op jit(solution)/shard_map/recur_forward/pallas_call | solution.py:982
  166.5 1.2 copy-done.2
  167.8 1.1 copy-done.9
  168.9 102.4 %reduce_and_fetch.1 = (f32[176,2048]{1,0:T(8,128)S(1)}, bf16[8,176,2048]{2,1,0:T(8,128)(2,1)}, bf16[2048,768]{1,0:T(8,128)(2,1)S(1)}, bf16[768,2048]{1,0:T(8,128)(2,1)S(1)}) custom-call(bf16[1408,384]{1,0:T(8,128)(2,1)S(1)} %bitcast.56, bf16[320,2048]{1,0:T(8,128)(2,1)S(1)} %copy-done.1, bf16[176,2048]{1,0:T(8,128)(2,1)S(1)} %copy-done.5, ...), custom_call_target="tpu_custom_call" | custom-call | tf_op jit(solution)/shard_map/reduce_and_fetch/pallas_call | solution.py:982
  271.3 1.1 copy-done
  272.4 1.6 copy-done.3
  274.0 1.7 copy-done.4
  275.8 34.0 %feed_forward.1 = (bf16[1408,768]{1,0:T(8,128)(2,1)S(1)}, bf16[1408,768]{1,0:T(8,128)(2,1)S(1)}, bf16[1408,768]{1,0:T(8,128)(2,1)}) custom-call(bf16[8,176,2048]{2,1,0:T(8,128)(2,1)} %get-tuple-element.69.n2_ref, bf16[8,176,2048]{2,1,0:T(8,128)(2,1)} %get-tuple-element.68.dm_ref, bf16[2048,768]{1,0:T(8,128)(2,1)} %get-tuple-element.55.wg_ref, ...), custom_call_target="tpu_custom_call" | custom-call | flops 13287555072 | bytes 11534336 | tf_op jit(solution)/shard_map/feed_forward/pallas_call | solution.py:958
  309.8 1.3 copy-done.6
  311.1 1.3 copy-done.7
  312.4 120.3 %reduce_and_return.1 = (f32[176,2048]{1,0:T(8,128)}, f32[8,2048]{1,0:T(8,128)}, bf16[8,176,2048]{2,1,0:T(8,128)(2,1)}, f32[128,3072]{1,0:T(8,128)}, f32[3072,128]{1,0:T(8,128)}, /*index=5*/bf16[8,176,2048]{2,1,0:T(8,128)(2,1)}) custom-call(bf16[2048,768]{1,0:T(8,128)(2,1)} %get-tuple-element.55.wg_ref, bf16[2048,768]{1,0:T(8,128)(2,1)} %copy-done.3, ...), custom_call_target="tpu_custom_call" | custom-call | tf_op jit(solution)/shard_map/reduce_and_return/pallas_call | solution.py:982
  432.7 78.7 %recur_backward.1 = (bf16[8,176,640]{2,1,0:T(8,128)(2,1)}, f32[384,768]{1,0:T(8,128)}, f32[8,8,384]{2,1,0:T(8,128)}, bf16[2,176,2048]{2,1,0:T(8,128)(2,1)}, f32[128,3072]{1,0:T(8,128)}) custom-call(bf16[8,176,2048]{2,1,0:T(8,128)(2,1)} %get-tuple-element.73.do_ref, bf16[320,2048]{1,0:T(8,128)(2,1)} %get-tuple-element.62.wo_ref, ...), custom_call_target="tpu_custom_call" | custom-call | tf_op jit(solution)/shard_map/recur_backward/pallas_call | solution.py:982
  511.4 0.9 reduce_sum.38
  512.3 0.7 fusion.8
  513.1 1.3 convert.25
  514.4 0.1 slice_bitcast_fusion.3
  514.7 0.3 reshape.146
  515.0 0.1 copy.47
  515.1 0.2 reshape.147
  515.3 0.8 reshape.148.gg_ref
  516.1 93.9 %return_last.1 = (f32[2,176,2048]{2,1,0:T(8,128)}, f32[8,2048]{1,0:T(8,128)}, f32[128,1280]{1,0:T(8,128)}, f32[128,1280]{1,0:T(8,128)}, f32[1280,128]{1,0:T(8,128)}, /*index=5*/bf16[4,64,128]{2,1,0:T(8,128)(2,1)}) custom-call(bf16[2048,640]{1,0:T(8,128)(2,1)} %get-tuple-element.57.wig_ref, bf16[176,2048]{1,0:T(8,128)(2,1)} %get-tuple-element.63.own_ref, ...), custom_call_target="tpu_custom_call" | custom-call | tf_op jit(solution)/shard_map/return_last/pallas_call | solution.py:982
  610.0 0.9 reduce_sum.36
  611.0 0.1 concatenate.32
  611.1 0.1 concatenate.33
  611.2 0.1 broadcast_in_dim.80
  611.3 0.1 broadcast_in_dim.76
  611.4 0.1 broadcast_in_dim.77
  611.5 0.1 broadcast_select_fusion.1
  611.7 0.1 broadcast_in_dim.74
  611.8 0.1 broadcast_select_fusion
  611.9 0.7 all_to_all.6
  612.6 2.5 all-to-all-start
  615.2 0.9 copy.58
  616.1 0.1 reshape.152
  616.3 0.7 squeeze.20
  616.9 0.7 squeeze.21
  617.6 4.0 all-to-all-done
  621.6 0.1 reduce_sum.39
  621.7 0.6 slice_bitcast_fusion.4
  622.3 0.7 reshape.151
  622.9 2.6 copy.68
  625.6 1.6 copy.69
  627.2 0.8 copy.70
  628.0 0.8 copy.71
  628.8 0.8 copy.72
  629.7 1.1 copy.73
  630.8 1.1 copy.74
  632.0 0.8 copy-done.12
  632.8 1.1 copy.75
  (63 shorter events, 0.5 us)
Async XLA Ops:
  0.6 2.9 copy-start.19
  0.7 3.0 copy-start.20
  0.7 3.2 copy-start.23
  0.7 5.6 copy-start.21
  0.7 5.6 copy-start.22
  135.7 30.8 %copy-start.10 = (f32[1,2048]{1,0:T(1,128)}, f32[1,2048]{1,0:T(1,128)S(1)}, u32[]{:S(2)}) copy-start(f32[1,2048]{1,0:T(1,128)S(1)} %get-tuple-element.140.gain_ref) | copy-start | bytes 24580
  136.3 30.2 %copy-start.1 = (bf16[320,2048]{1,0:T(8,128)(2,1)S(1)}, bf16[320,2048]{1,0:T(8,128)(2,1)}, u32[]{:S(2)}) copy-start(bf16[320,2048]{1,0:T(8,128)(2,1)} %get-tuple-element.62.wo_ref) | copy-start | bytes 3932164
  136.3 30.3 %copy-start.5 = (bf16[176,2048]{1,0:T(8,128)(2,1)S(1)}, bf16[176,2048]{1,0:T(8,128)(2,1)}, u32[]{:S(2)}) copy-start(bf16[176,2048]{1,0:T(8,128)(2,1)} %get-tuple-element.63.own_ref) | copy-start | bytes 2162692
  136.3 30.3 %copy-start.8 = (bf16[128,3072]{1,0:T(8,128)(2,1)S(1)}, bf16[128,3072]{1,0:T(8,128)(2,1)}, u32[]{:S(2)}) copy-start(bf16[128,3072]{1,0:T(8,128)(2,1)} %up_ref.1) | copy-start | bytes 2359300
  166.5 1.2 copy-start.2
  167.8 1.1 copy-start.9
  271.3 1.1 copy-start
  272.4 1.6 copy-start.3
  274.0 1.7 copy-start.4
  309.8 1.3 copy-start.6
  311.1 1.3 copy-start.7
  516.1 94.8 %copy-start.18 = (f32[8,2048]{1,0:T(8,128)S(1)}, f32[8,2048]{1,0:T(8,128)}, u32[]{:S(2)}) copy-start(f32[8,2048]{1,0:T(8,128)} %get-tuple-element.92) | copy-start | bytes 196612
  612.6 13.0 %copy-start.11 = (f32[2,176,2048]{2,1,0:T(8,128)S(1)}, f32[2,176,2048]{2,1,0:T(8,128)}, u32[]{:S(2)}) copy-start(f32[2,176,2048]{2,1,0:T(8,128)} %get-tuple-element.87) | copy-start | bytes 8650756
  612.6 9.0 %all-to-all-start = ((f32[32,1,896]{2,1,0:T(1,128)}), f32[32,1,896]{2,1,0:T(1,128)S(1)}, u32[]{:S(2)}, u32[]{:S(2)}) async-start(f32[32,1,896]{2,1,0:T(1,128)} %all_to_all.6), calls=%async_computation | async-start | bytes 229376 | tf_op jit(solution)/shard_map/all_to_all | solution.py:1989
  625.6 1.6 copy-start.17
  625.6 2.4 copy-start.16
  627.2 1.7 copy-start.15
  627.2 2.5 copy-start.13
  628.8 2.0 copy-start.14
  630.8 2.0 copy-start.12
